TPU v7x, 32 devices: a whole 2x2x4 slice. The times are simulated.
32 devices in a mesh: dp: 16 (over z, y, x), tensor: 2 (over core).
Axes of the slice: x: 2, y: 2, z: 4, core: 2. Of those that a mesh axis runs over, the one named last changes fastest.
Arguments:
- mixer_input: bfloat16 [192, 768, 196], P('dp', 'tensor'), may hold values from -6 to 6
- keep_mask: int32 [192, 196], P('dp'), may hold values from 0 to 1, as said below
- ln_gain: bfloat16 [2, 768], P(None, 'dp'), may hold values from 0.25 to 1.75
- ln_shift: bfloat16 [2, 768], P(None, 'dp'), may hold values from -3 to 3
- token_w1: bfloat16 [196, 384], P(None, 'dp'), may hold values from -0.4375 to 0.4375
- token_b1: bfloat16 [384], P('dp'), may hold values from -3 to 3
- token_w2: bfloat16 [384, 196], P('dp'), may hold values from -0.3125 to 0.3125
- token_b2: bfloat16 [196], replicated, may hold values from -3 to 3
- chan_w1: bfloat16 [768, 3072], P(None, 'tensor'), may hold values from -0.21875 to 0.21875
- chan_b1: bfloat16 [3072], P('tensor'), may hold values from -3 to 3
- chan_w2: bfloat16 [3072, 768], P('tensor'), may hold values from -0.109375 to 0.109375
- chan_b2: bfloat16 [768], P('tensor'), may hold values from -3 to 3
- grad_out: bfloat16 [192, 768, 196], P('dp', 'tensor'), may hold values from -6 to 6
- grad_pooled: float32 [192, 768], P('dp', 'tensor'), may hold values from -18 to 18
Outputs:
- block_out: float32 [192, 768, 196], P('dp', 'tensor')
- pooled: float32 [192, 768], P('dp', 'tensor')
- grad_input: float32 [192, 768, 196], P('dp', 'tensor')
- grad_ln_gain: float32 [2, 768], P(None, 'dp')
- grad_ln_shift: float32 [2, 768], P(None, 'dp')
- grad_token_w1: float32 [196, 384], P(None, 'dp')
- grad_token_b1: float32 [384], P('dp')
- grad_token_w2: float32 [384, 196], P('dp')
- grad_token_b2: float32 [196], replicated
- grad_chan_w1: float32 [768, 3072], P('dp', 'tensor')
- grad_chan_b1: float32 [3072], P(('tensor', 'dp'))
- grad_chan_w2: float32 [3072, 768], P('tensor', 'dp')
- grad_chan_b2: float32 [768], P(('tensor', 'dp'))
- example_sq: float32 [192], P('dp')
Inputs may be any that keep to these rules, and one draw needn't show every extreme that they name: `keep_mask`: each image keeps at least 49 of its patches.
All inputs are finite; a program needn't handle non-finite values.
Results may differ from a plain program's by a relative error of at most 0.03.
Values may be sent and summed in bfloat16 or wider, within the bound.
A program may use at most 192 MiB of HBM per device.

v0:
```python
import jax
import jax.numpy as jnp
from jax import lax
from jax.sharding import PartitionSpec as P

D = 768


epsilon = 1e-05


def gelu_exact(values_in):
    return jax.nn.gelu(values_in, approximate=False)


def gelu_slope(pre_sum, upstream):
    unused, backward = jax.vjp(gelu_exact, pre_sum)
    return backward(upstream)[0]


def channel_sums(first_term, second_term):
    return lax.psum((first_term, second_term), "tensor")


def normalize(values_in, gains, shifts):
    totals, square = channel_sums(jnp.sum(values_in, 1), jnp.sum(values_in * values_in, 1))
    average = totals / D
    spread = square / D - average * average
    scaling = lax.rsqrt(spread + epsilon)[:, None, :]
    unit_part = (values_in - average[:, None, :]) * scaling
    return (unit_part * gains[None, :, None] + shifts[None, :, None], unit_part, scaling)


def normalize_back(upstream, unit_part, scaling, gains):
    scaled = upstream * gains[None, :, None]
    totals, along_unit = channel_sums(jnp.sum(scaled, 1), jnp.sum(scaled * unit_part, 1))
    inner_part = scaled - totals[:, None, :] / D - unit_part * along_unit[:, None, :] / D
    return (scaling * inner_part, jnp.sum(upstream * unit_part, (0, 2)), jnp.sum(upstream, (0, 2)))


def body(
    mixer_input,
    keep_mask,
    ln_gain,
    ln_shift,
    token_w1,
    token_b1,
    token_w2,
    token_b2,
    chan_w1,
    chan_b1,
    chan_w2,
    chan_b2,
    grad_out,
    grad_pooled,
):
    images, channels, patches = mixer_input.shape
    full_width = channels * lax.axis_size("tensor")
    offset = lax.axis_index("tensor") * channels
    gains, shifts, weight_in, bias_in, weight_back = (
        lax.all_gather(ln_gain, "dp", axis=1, tiled=True),
        lax.all_gather(ln_shift, "dp", axis=1, tiled=True),
        lax.all_gather(token_w1, "dp", axis=1, tiled=True),
        lax.all_gather(token_b1, "dp", axis=0, tiled=True),
        lax.all_gather(token_w2, "dp", axis=0, tiled=True),
    )
    gain_own = lax.dynamic_slice_in_dim(gains, offset, channels, 1).astype(jnp.float32)
    shift_own = lax.dynamic_slice_in_dim(shifts, offset, channels, 1).astype(jnp.float32)
    kept = keep_mask.astype(jnp.float32)
    counts = jnp.sum(kept, 1)
    source = mixer_input.astype(jnp.float32)
    normed, unit_first, scale_first = normalize(source, gain_own[0], shift_own[0])
    first_low = normed.astype(jnp.bfloat16)
    token_pre = jnp.einsum(
        "bcp,ph->bch", first_low, weight_in, preferred_element_type=jnp.float32
    ) + bias_in.astype(jnp.float32)
    token_hid = gelu_exact(token_pre).astype(jnp.bfloat16)
    token_out = jnp.einsum(
        "bch,hp->bcp", token_hid, weight_back, preferred_element_type=jnp.float32
    ) + token_b2.astype(jnp.float32)
    mixture = source + token_out
    normed, unit_second, scale_second = normalize(mixture, gain_own[1], shift_own[1])
    second = normed.astype(jnp.bfloat16)
    section = lax.all_gather(second, "tensor", axis=1, tiled=True)
    pre_sum = jnp.einsum("bcp,ch->bhp", section, chan_w1, preferred_element_type=jnp.float32)
    gathered = section
    grams = jnp.einsum("bcp,bcq->bpq", section, section, preferred_element_type=jnp.float32)
    chan_pre = pre_sum
    gram_second = grams
    chan_pre = chan_pre + chan_b1.astype(jnp.float32)[None, :, None]
    chan_hid = gelu_exact(chan_pre).astype(jnp.bfloat16)
    partial_value = jnp.einsum("bhp,hc->bcp", chan_hid, chan_w2, preferred_element_type=jnp.float32)
    chan_out = (
        lax.psum_scatter(
            partial_value.astype(jnp.bfloat16), "tensor", scatter_dimension=1, tiled=True
        ).astype(jnp.float32)
        + chan_b2.astype(jnp.float32)[None, :, None]
    )
    masked = kept[:, None, :] * (mixture + chan_out)
    pooled = jnp.sum(masked, 2) / counts[:, None]
    grad_result = kept[:, None, :] * (
        grad_out.astype(jnp.float32) + grad_pooled[:, :, None] / counts[:, None, None]
    )
    grad_low = grad_result.astype(jnp.bfloat16)
    grad_chan_b2 = jnp.sum(grad_low, (0, 2), dtype=jnp.float32)
    section = lax.all_gather(grad_low, "tensor", axis=1, tiled=True)
    hid_sum = jnp.einsum("bcp,hc->bhp", section, chan_w2, preferred_element_type=jnp.float32)
    column_block = jnp.einsum("bhp,bcp->hc", chan_hid, section, preferred_element_type=jnp.float32)
    grams = jnp.einsum("bcp,bcq->bpq", section, section, preferred_element_type=jnp.float32)
    pre_grad = gelu_slope(chan_pre, hid_sum).astype(jnp.bfloat16)
    grad_chan_b1 = jnp.sum(pre_grad, (0, 2), dtype=jnp.float32)
    grad_chan_w1 = jnp.einsum("bcp,bhp->ch", gathered, pre_grad, preferred_element_type=jnp.float32)
    share_w1, share_b1, share_w2, share_b2 = (
        lax.psum_scatter(
            grad_chan_w1.astype(jnp.bfloat16), "dp", scatter_dimension=0, tiled=True
        ).astype(jnp.float32),
        lax.psum_scatter(
            grad_chan_b1.astype(jnp.bfloat16), "dp", scatter_dimension=0, tiled=True
        ).astype(jnp.float32),
        lax.psum_scatter(
            column_block.astype(jnp.bfloat16), "dp", scatter_dimension=1, tiled=True
        ).astype(jnp.float32),
        lax.psum_scatter(
            grad_chan_b2.astype(jnp.bfloat16), "dp", scatter_dimension=0, tiled=True
        ).astype(jnp.float32),
    )
    second_part = jnp.einsum("bhp,ch->bcp", pre_grad, chan_w1, preferred_element_type=jnp.float32)
    second_grad = lax.psum_scatter(
        second_part.astype(jnp.bfloat16), "tensor", scatter_dimension=1, tiled=True
    ).astype(jnp.float32)
    gram_pre = jnp.einsum("bhp,bhq->bpq", pre_grad, pre_grad, preferred_element_type=jnp.float32)
    gram_hid = jnp.einsum("bhp,bhq->bpq", chan_hid, chan_hid, preferred_element_type=jnp.float32)
    own_terms = jnp.sum(gram_second * gram_pre + gram_hid * grams, (1, 2))
    own_terms = own_terms + jnp.sum(jnp.square(jnp.sum(pre_grad, 2, dtype=jnp.float32)), 1)
    own_terms = own_terms + jnp.sum(jnp.square(jnp.sum(grad_low, 2, dtype=jnp.float32)), 1)
    example_sq = lax.psum(own_terms, "tensor")
    back_second, gain_second, shift_second = normalize_back(
        second_grad, unit_second, scale_second, gain_own[1]
    )
    mixture_grad = grad_result + back_second
    out_low = mixture_grad.astype(jnp.bfloat16)
    grad_token_b2 = jnp.sum(out_low, (0, 1), dtype=jnp.float32)
    token_hid_grad = jnp.einsum(
        "bcp,hp->bch", out_low, weight_back, preferred_element_type=jnp.float32
    )
    grad_token_w2 = jnp.einsum(
        "bch,bcp->hp", token_hid, out_low, preferred_element_type=jnp.float32
    )
    token_pre_grad = gelu_slope(token_pre, token_hid_grad).astype(jnp.bfloat16)
    grad_token_b1 = jnp.sum(token_pre_grad, (0, 1), dtype=jnp.float32)
    grad_token_w1 = jnp.einsum(
        "bcp,bch->ph", first_low, token_pre_grad, preferred_element_type=jnp.float32
    )
    first_grad = jnp.einsum(
        "bch,ph->bcp", token_pre_grad, weight_in, preferred_element_type=jnp.float32
    )
    back_first, gain_first, shift_first = normalize_back(
        first_grad, unit_first, scale_first, gain_own[0]
    )
    grad_input = mixture_grad + back_first
    gain_parts = lax.dynamic_update_slice_in_dim(
        jnp.zeros((2, full_width), jnp.float32), jnp.stack([gain_first, gain_second]), offset, 1
    )
    shift_parts = lax.dynamic_update_slice_in_dim(
        jnp.zeros((2, full_width), jnp.float32), jnp.stack([shift_first, shift_second]), offset, 1
    )
    total_gain, total_shift, total_w1, total_b1, total_w2 = (
        lax.psum(gain_parts.astype(jnp.bfloat16), "tensor").astype(jnp.float32),
        lax.psum(shift_parts.astype(jnp.bfloat16), "tensor").astype(jnp.float32),
        lax.psum(grad_token_w1.astype(jnp.bfloat16), "tensor").astype(jnp.float32),
        lax.psum(grad_token_b1.astype(jnp.bfloat16), "tensor").astype(jnp.float32),
        lax.psum(grad_token_w2.astype(jnp.bfloat16), "tensor").astype(jnp.float32),
    )
    share_gain, share_shift, share_tw1, share_tb1, share_tw2 = (
        lax.psum_scatter(
            total_gain.astype(jnp.bfloat16), "dp", scatter_dimension=1, tiled=True
        ).astype(jnp.float32),
        lax.psum_scatter(
            total_shift.astype(jnp.bfloat16), "dp", scatter_dimension=1, tiled=True
        ).astype(jnp.float32),
        lax.psum_scatter(
            total_w1.astype(jnp.bfloat16), "dp", scatter_dimension=1, tiled=True
        ).astype(jnp.float32),
        lax.psum_scatter(
            total_b1.astype(jnp.bfloat16), "dp", scatter_dimension=0, tiled=True
        ).astype(jnp.float32),
        lax.psum_scatter(
            total_w2.astype(jnp.bfloat16), "dp", scatter_dimension=0, tiled=True
        ).astype(jnp.float32),
    )
    share_tb2 = lax.psum(grad_token_b2, ("dp", "tensor"))
    return (
        masked,
        pooled,
        grad_input,
        share_gain,
        share_shift,
        share_tw1,
        share_tb1,
        share_tw2,
        share_tb2,
        share_w1,
        share_b1,
        share_w2,
        share_b2,
        example_sq,
    )


def solution(mesh):
    return jax.shard_map(
        body,
        mesh=mesh,
        in_specs=(
            P("dp", "tensor", None),
            P("dp", None),
            P(None, "dp"),
            P(None, "dp"),
            P(None, "dp"),
            P("dp"),
            P("dp", None),
            P(),
            P(None, "tensor"),
            P("tensor"),
            P("tensor", None),
            P("tensor"),
            P("dp", "tensor", None),
            P("dp", "tensor"),
        ),
        out_specs=(
            P("dp", "tensor", None),
            P("dp", "tensor"),
            P("dp", "tensor", None),
            P(None, "dp"),
            P(None, "dp"),
            P(None, "dp"),
            P("dp"),
            P("dp", None),
            P(),
            P("dp", "tensor"),
            P(("tensor", "dp")),
            P("tensor", "dp"),
            P(("tensor", "dp")),
            P("dp"),
        ),
        check_vma=False,
    )
```

profile of v0, /device:TPU:0, one launch (start us, length us, event | category | flops | bytes accessed | tf_op | source)
XLA Modules:
  0.0 1173.4 jit_solution(5983142998663929202)
XLA Ops:
  7.3 42.5 %all-gather = bf16[16,48,2]{1,2,0:T(2,128)(2,1)S(1)} all-gather(bf16[1,48,2]{1,2,0:T(2,128)(2,1)} %bitcast.182), channel_id=1, replica_groups=mesh['dp'=16,'tensor'=2] {'dp'}, dimensions={0}, use_global_device_ids=true | all-gather | bytes 3264 | tf_op jit(solution)/shard_map/all_gather | solution.py:61
  49.8 35.5 %all-gather.1 = bf16[16,48,2]{1,2,0:T(2,128)(2,1)S(1)} all-gather(bf16[1,48,2]{1,2,0:T(2,128)(2,1)} %bitcast.183), channel_id=1, replica_groups=mesh['dp'=16,'tensor'=2] {'dp'}, dimensions={0}, use_global_device_ids=true | all-gather | bytes 3264 | tf_op jit(solution)/shard_map/all_gather | solution.py:62
  90.8 38.5 %all-reduce = bf16[384]{0:T(512)(128)(2,1)S(1)} all-reduce(bf16[384]{0:T(512)(128)(2,1)S(1)} %dynamic-update-slice), channel_id=1, replica_groups=mesh['dp'=16,'tensor'=2] {'dp'}, use_global_device_ids=true, to_apply=%add | all-reduce | flops 384 | bytes 1536
  129.3 36.9 %all_gather.23 = bf16[196,384]{0,1:T(8,128)(2,1)S(1)} all-gather(bf16[196,24]{0,1:T(8,128)(2,1)} %param.18), channel_id=1, replica_groups=mesh['dp'=16,'tensor'=2] {'dp'}, dimensions={1}, use_global_device_ids=true | all-gather | bytes 159936 | tf_op jit(solution)/shard_map/all_gather | solution.py:63
  166.2 38.7 %all_gather.25 = bf16[384,196]{1,0:T(8,128)(2,1)S(1)} all-gather(bf16[24,196]{1,0:T(8,128)(2,1)} %param.20), channel_id=1, replica_groups=mesh['dp'=16,'tensor'=2] {'dp'}, dimensions={0}, use_global_device_ids=true | all-gather | bytes 159936 | tf_op jit(solution)/shard_map/all_gather | solution.py:65
  205.5 3.4 all-reduce.7
  209.0 6.1 fusion.52
  215.1 17.0 %multiply_convert_fusion = (bf16[12,384,384]{2,1,0:T(8,128)(2,1)S(1)}, f32[12,384,384]{2,1,0:T(8,128)}) fusion(f32[12,384,384]{2,1,0:T(8,128)S(1)} %get-tuple-element.67, f32[384]{0:T(512)S(1)} %convert_element_type.144, u16[384,384]{1,0:T(8,128)(2,1)S(1)} %get-tuple-element.15, u16[384,384]{1,0:T(8,128)(2,1)S(1)} %get-tuple-element.14), kind=kLoop, calls=%fused_computation.40 | loop fusion | flops 125632512 | bytes 18286080 | tf_op jit(solution)/shard_map/convert_element_type | solution.py:77
  233.9 3.6 fusion.70
  237.5 3.7 all-reduce.6
  241.9 3.4 add_convert_fusion.1
  246.7 4.1 fusion.72
  254.2 39.7 %fusion.9 = (bf16[12,1536,196]{1,2,0:T(8,128)(2,1)}, f32[12,1536,196]{1,2,0:T(8,128)}, f32[12,196,1536]{2,1,0:T(8,128)}) fusion(f32[1536]{0:T(1024)S(1)} %convert_element_type.148, bf16[12,768,196]{1,2,0:T(8,128)(2,1)} %all-gather.5.cloned.1.call-done, bf16[768,1536]{1,0:T(8,128)(2,1)S(1)} %copy-done), kind=kOutput, calls=%fused_computation.17 | convolution fusion | flops 5787500544 | bytes 42104832 | tf_op jit(solution)/shard_map/bcp,ch->bhp/dot_general | solution.py:85
  293.9 21.1 %convert_reduce_fusion = (f32[12,1536]{1,0:T(8,128)S(1)}, bf16[12,1536,196]{1,2,0:T(8,128)(2,1)}) fusion(f32[12,1536,196]{1,2,0:T(8,128)} %get-tuple-element.56, bf16[12,768,196]{1,2,0:T(8,128)(2,1)} %all-gather.7.cloned.1.call-done, bf16[1536,768]{1,0:T(8,128)(2,1)} %param.24, f32[12,196,1536]{2,1,0:T(8,128)} %get-tuple-element.69, ...), kind=kOutput, calls=%fused_computation.18 | convolution fusion | flops 5610461184 | bytes 42178560 | tf_op jit(solution)/shard_map/bcp,hc->bhp/dot_general | solution.py:107
  315.0 10.8 bitcast_convert_fusion.1
  326.1 11.2 bitcast_convert_fusion
  337.4 10.6 convert_bitcast_fusion
  348.0 8.6 copy.46
  356.6 10.7 reshape.72
  367.4 10.3 convert_bitcast_fusion.1
  377.6 8.6 copy.44
  386.2 10.8 reshape.70
  400.5 4.2 reduce_sum.232
  404.8 4.3 fusion.79
  409.2 7.7 fusion.80
  416.9 7.6 fusion.81
  426.0 29.6 %reduce-scatter.17.cloned.1.call-done = bf16[48,1536]{1,0:T(8,128)(2,1)} async-done(((bf16[768,1536]{1,0:T(8,128)(2,1)}), bf16[48,1536]{1,0:T(8,128)(2,1)}) %reduce-scatter.17.cloned.1.call-update) | async-done | bytes 147472 | tf_op jit(solution)/shard_map/reduce_scatter | solution.py:114
  457.3 131.4 %reduce-scatter.19.cloned.1.call-done = bf16[1536,48]{0,1:T(8,128)(2,1)} async-done(((bf16[1536,768]{0,1:T(8,128)(2,1)}), bf16[1536,48]{0,1:T(8,128)(2,1)}) %reduce-scatter.19.cloned.1.call-update) | async-done | bytes 147472 | tf_op jit(solution)/shard_map/reduce_scatter | solution.py:120
  590.4 11.2 reduce-scatter.27.cloned.1.call-done
  601.6 9.1 reshape.73
  610.7 5.0 copy.47
  615.7 4.1 fusion.35
  619.9 3.7 all-reduce.5
  623.6 9.1 reshape.71
  632.7 4.7 copy.45
  637.5 7.0 convert_reduce_fusion.4
  644.5 8.9 fusion.78
  653.5 4.1 fusion.48
  662.4 4.9 fusion.59
  667.4 42.6 %all-reduce.8 = (bf16[384]{0:T(512)(128)(2,1)S(1)}, bf16[1536]{0:T(1024)(128)(2,1)S(1)}, bf16[384]{0:T(512)(128)(2,1)S(1)}) all-reduce(bf16[384]{0:T(512)(128)(2,1)S(1)} %get-tuple-element.73, bf16[1536]{0:T(1024)(128)(2,1)S(1)} %reduce_sum.232, bf16[384]{0:T(512)(128)(2,1)S(1)} %copy-done.34), channel_id=7, replica_groups=mesh['dp'=16,'tensor'=2] {'dp'}, use_global_device_ids=true, to_apply=%region_32.0.clone | all-reduce | flops 2304 | bytes 9216
  710.0 36.8 %psum.118 = f32[196]{0:T(256)} all-reduce(f32[196]{0:T(256)S(1)} %get-tuple-element.49), channel_id=1, replica_groups=mesh['dp'=16,'tensor'=2] {'dp','tensor'}, use_global_device_ids=true, to_apply=%region_36.0 | all-reduce | flops 196 | bytes 1568 | tf_op jit(solution)/shard_map/psum | solution.py:191
  746.9 4.0 all-reduce.4
  751.5 6.8 fusion.47
  759.6 24.6 %reduce-scatter.31.cloned.1.call-done = bf16[48,2]{1,0:T(8,128)(2,1)} async-done(((bf16[768,2]{1,0:T(8,128)(2,1)}), bf16[48,2]{1,0:T(8,128)(2,1)}) %reduce-scatter.31.cloned.1.call-update) | async-done | bytes 208
  785.0 124.3 %reduce-scatter.29.cloned.1.call-done = bf16[48,2]{1,0:T(8,128)(2,1)} async-done(((bf16[768,2]{1,0:T(8,128)(2,1)}), bf16[48,2]{1,0:T(8,128)(2,1)}) %reduce-scatter.29.cloned.1.call-update) | async-done | bytes 208
  910.0 124.3 %reduce-scatter.23.cloned.1.call-done = bf16[24,196]{1,0:T(8,128)(2,1)} async-done(((bf16[384,196]{1,0:T(8,128)(2,1)}), bf16[24,196]{1,0:T(8,128)(2,1)}) %reduce-scatter.23.cloned.1.call-update) | async-done | bytes 9424 | tf_op jit(solution)/shard_map/reduce_scatter | solution.py:187
  1034.3 124.9 %reduce-scatter.21.cloned.1.call-done = bf16[196,24]{0,1:T(8,128)(2,1)} async-done(((bf16[196,384]{0,1:T(8,128)(2,1)}), bf16[196,24]{0,1:T(8,128)(2,1)}) %reduce-scatter.21.cloned.1.call-update) | async-done | bytes 9424 | tf_op jit(solution)/shard_map/reduce_scatter | solution.py:181
  1159.2 4.0 all-reduce.9
  (150 shorter events, 31.4 us)
Async XLA Ops:
  7.2 247.0 %copy-start = (bf16[768,1536]{1,0:T(8,128)(2,1)S(1)}, bf16[768,1536]{1,0:T(8,128)(2,1)}, u32[]{:S(2)}) copy-start(bf16[768,1536]{1,0:T(8,128)(2,1)} %param.22) | copy-start | bytes 7077892
  7.2 247.0 %all-gather.5.cloned.1.call-start = ((), (), s32[]{:S(2)}) async-start(), calls=%async_computation.8 | async-start | bytes 5529600 | tf_op jit(solution)/shard_map/all_gather | solution.py:84
  85.5 129.6 %copy-start.27 = (f32[384]{0:T(512)}, f32[384]{0:T(512)S(1)}, u32[]{:S(2)}) copy-start(f32[384]{0:T(512)S(1)} %get-tuple-element.29) | copy-start | bytes 4612
  85.5 155.8 %copy-start.24 = (f32[384]{0:T(512)}, f32[384]{0:T(512)S(1)}, u32[]{:S(2)}) copy-start(f32[384]{0:T(512)S(1)} %get-tuple-element.28) | copy-start | bytes 4612
  85.5 129.5 %copy-start.35 = (f32[384]{0:T(512)}, f32[384]{0:T(512)S(1)}, u32[]{:S(2)}) copy-start(f32[384]{0:T(512)S(1)} %get-tuple-element.31) | copy-start | bytes 4612
  129.3 85.8 %copy-start.29 = (f32[384]{0:T(512)}, f32[384]{0:T(512)S(1)}, u32[]{:S(2)}) copy-start(f32[384]{0:T(512)S(1)} %convert_element_type.144) | copy-start | bytes 4612
  166.2 48.9 %copy-start.15 = (bf16[196,384]{0,1:T(8,128)(2,1)}, bf16[196,384]{0,1:T(8,128)(2,1)S(1)}, u32[]{:S(2)}) copy-start(bf16[196,384]{0,1:T(8,128)(2,1)S(1)} %all_gather.23) | copy-start | bytes 451588
  204.9 27.3 %copy-start.7 = (bf16[384,196]{1,0:T(8,128)(2,1)}, bf16[384,196]{1,0:T(8,128)(2,1)S(1)}, u32[]{:S(2)}) copy-start(bf16[384,196]{1,0:T(8,128)(2,1)S(1)} %all_gather.25) | copy-start | bytes 451588
  209.0 6.1 copy-start.19
  209.0 6.1 copy-start.21
  215.1 17.1 %copy-start.6 = (f32[12,384,384]{2,1,0:T(8,128)}, f32[12,384,384]{2,1,0:T(8,128)S(1)}, u32[]{:S(2)}) copy-start(f32[12,384,384]{2,1,0:T(8,128)S(1)} %get-tuple-element.67) | copy-start | bytes 21233668
  215.1 18.8 %copy-start.3 = (bf16[12,384,196]{1,2,0:T(8,128)(2,1)S(1)}, bf16[12,384,196]{1,2,0:T(8,128)(2,1)}, u32[]{:S(2)}) copy-start(bf16[12,384,196]{1,2,0:T(8,128)(2,1)} %param.14) | copy-start | bytes 5419012
  232.2 1.8 copy-start.2
  233.9 11.4 copy-start.23
  233.9 12.1 %copy-start.26 = (f32[12,384]{1,0:T(8,128)S(1)}, f32[12,384]{1,0:T(8,128)}, u32[]{:S(2)}) copy-start(f32[12,384]{1,0:T(8,128)} %param.27) | copy-start | bytes 55300
  237.5 13.8 %copy-start.33 = (bf16[1536]{0:T(1024)(128)(2,1)S(1)}, bf16[1536]{0:T(1024)(128)(2,1)}, u32[]{:S(2)}) copy-start(bf16[1536]{0:T(1024)(128)(2,1)} %param.23) | copy-start | bytes 9220
  241.3 0.6 copy-start.9
  241.3 0.6 copy-start.11
  245.3 48.6 %all-gather.7.cloned.1.call-start = ((), (), s32[]{:S(2)}) async-start(), calls=%async_computation.9 | async-start | bytes 5529600 | tf_op jit(solution)/shard_map/all_gather | solution.py:106
  245.4 5.5 copy-start.17
  245.5 0.5 copy-start.31
  246.1 0.6 copy-start.13
  250.9 204.8 %reduce-scatter.17.cloned.1.call-start = ((), (), s32[]{:S(2)}) async-start(), calls=%async_computation.10 | async-start | bytes 2506752 | tf_op jit(solution)/shard_map/reduce_scatter | solution.py:114
  325.8 262.9 %reduce-scatter.19.cloned.1.call-start = ((), (), s32[]{:S(2)}) async-start(), calls=%async_computation.11 | async-start | bytes 2506752 | tf_op jit(solution)/shard_map/reduce_scatter | solution.py:120
  337.3 264.2 %reduce-scatter.27.cloned.1.call-start = ((), (), s32[]{:S(2)}) async-start(), calls=%async_computation.15 | async-start | bytes 5603328
  367.3 256.2 %reduce-scatter.25.cloned.1.call-start = ((), (), s32[]{:S(2)}) async-start(), calls=%async_computation.14 | async-start | bytes 5603328
  386.2 11.1 copy-start.37
  397.0 387.2 %reduce-scatter.31.cloned.1.call-start = ((), (), s32[]{:S(2)}) async-start(), calls=%async_computation.17 | async-start | bytes 208896
  416.9 7.6 copy-start.5
  426.0 189.7 %copy-start.10 = (f32[12,196]{1,0:T(8,128)S(1)}, f32[12,196]{1,0:T(8,128)}, u32[]{:S(2)}) copy-start(f32[12,196]{1,0:T(8,128)} %copy-done.9) | copy-start | bytes 28228
  426.0 189.7 %copy-start.12 = (f32[12,196]{1,0:T(8,128)S(1)}, f32[12,196]{1,0:T(8,128)}, u32[]{:S(2)}) copy-start(f32[12,196]{1,0:T(8,128)} %copy-done.11) | copy-start | bytes 28228
  426.0 189.7 %copy-start.25 = (f32[384]{0:T(512)S(1)}, f32[384]{0:T(512)}, u32[]{:S(2)}) copy-start(f32[384]{0:T(512)} %copy-done.24) | copy-start | bytes 4612
  615.7 21.8 %copy-start.14 = (f32[12,384]{1,0:T(8,128)S(1)}, f32[12,384]{1,0:T(8,128)}, u32[]{:S(2)}) copy-start(f32[12,384]{1,0:T(8,128)} %copy-done.13) | copy-start | bytes 55300
  615.7 21.8 %copy-start.18 = (f32[12,196]{1,0:T(8,128)S(1)}, f32[12,196]{1,0:T(8,128)}, u32[]{:S(2)}) copy-start(f32[12,196]{1,0:T(8,128)} %copy-done.17) | copy-start | bytes 28228
  637.5 7.0 copy-start.8
  637.5 7.0 copy-start.30
  644.5 9.0 copy-start.1
  644.5 9.0 copy-start.4
  644.5 9.0 copy-start.16
  644.5 9.0 copy-start.20
  644.5 9.0 copy-start.22
  644.5 9.0 copy-start.28
  653.4 4.2 copy-start.36
  657.6 9.8 copy-start.34
  661.4 247.8 %reduce-scatter.29.cloned.1.call-start = ((), (), s32[]{:S(2)}) async-start(), calls=%async_computation.16 | async-start | bytes 208896
  662.4 371.9 %reduce-scatter.23.cloned.1.call-start = ((), (), s32[]{:S(2)}) async-start(), calls=%async_computation.13 | async-start | bytes 208896 | tf_op jit(solution)/shard_map/reduce_scatter | solution.py:187
  667.4 91.5 %copy-start.32 = (f32[12]{0:T(128)S(1)}, f32[12]{0:T(128)}, u32[]{:S(2)}) copy-start(f32[12]{0:T(128)} %copy-done.31) | copy-start | bytes 148
  746.9 412.3 %reduce-scatter.21.cloned.1.call-start = ((), (), s32[]{:S(2)}) async-start(), calls=%async_computation.12 | async-start | bytes 208896 | tf_op jit(solution)/shard_map/reduce_scatter | solution.py:181
Sparse Core Ops, SparseCore 0:
  245.4 8.7 all-gather.4
  255.7 13.9 all-gather.6
  326.0 129.6 reduce-scatter.16
  461.2 127.4 reduce-scatter.18
  590.8 10.6 reduce-scatter.26
  603.8 12.7 reduce-scatter.24
  661.5 122.6 reduce-scatter.30
  788.8 120.3 reduce-scatter.28
  913.9 120.3 reduce-scatter.22
  1038.8 120.3 reduce-scatter.20
where the time goes:
time: 1180 us; the launch traced here: 1170 us
  waiting for transfers between devices  573 us (49%)
  blocking collectives  290 us (25%)
  matrix products  155 us (13%)
  local copies, waits for them, and re-layouts  76.1 us (6%)
  other arithmetic  60 us (5%)
  between operations  17.2 us (1%)
    unnamed x14, waiting for transfers between devices  160 us
    reduce_scatter x1, waiting for transfers between devices, body(): lax.psum_scatter(column_block.astype(jnp.bfloat16), 'dp', scatter_dimensi...  131 us
    reduce_scatter x1, waiting for transfers between devices, body(): lax.psum_scatter(total_w1.astype(jnp.bfloat16), 'dp', scatter_dimension=1...  125 us
    reduce_scatter x1, waiting for transfers between devices, body(): lax.psum_scatter(total_w2.astype(jnp.bfloat16), 'dp', scatter_dimension=0...  124 us
    unnamed x2, blocking collectives  81.1 us
    unnamed x94, local copies, waits for them, and re-layouts  76 us
    all_gather x1, blocking collectives, body(): lax.all_gather(ln_gain, 'dp', axis=1, tiled=True)  42.5 us
    dot_general x1, matrix products, body(): jnp.einsum('bcp,ch->bhp', section, chan_w1, preferred_element_type=jnp.fl...  39.7 us
  transfers between devices with their start and end apart: 10, of which 8 were waited for; matrix products, arithmetic and copies ran while one was open for 15% of the time, Pallas kernels for 0%

commit v1 on v0

--- a/solution.py
+++ b/solution.py
@@ -1,7 +1,1148 @@
+import functools
+import math
+
 import jax
 import jax.numpy as jnp
 from jax import lax
+from jax.experimental import pallas as pl
+from jax.experimental.pallas import tpu as pltpu
 from jax.sharding import PartitionSpec as P
+
+MESH = pl.DeviceIdType.MESH
+EPS = 1e-05
+F32 = jnp.float32
+BF16 = jnp.bfloat16
+VM = pl.BlockSpec(memory_space=pltpu.VMEM)
+ANY = pl.BlockSpec(memory_space=pl.ANY)
+BLK = 256
+VMEM_BYTES = 63 * 2**20
+
+
+def up(n, m):
+    return -(-n // m) * m
+
+
+def nn(a, b):
+    return lax.dot_general(a, b, (((1,), (0,)), ((), ())), preferred_element_type=F32)
+
+
+def nt(a, b):
+    return lax.dot_general(a, b, (((1,), (1,)), ((), ())), preferred_element_type=F32)
+
+
+def tn(a, b):
+    return lax.dot_general(a, b, (((0,), (0,)), ((), ())), preferred_element_type=F32)
+
+
+def eye(rows, cols):
+    r = lax.broadcasted_iota(jnp.int32, (rows, cols), 0)
+    c = lax.broadcasted_iota(jnp.int32, (rows, cols), 1)
+    return (r == c).astype(F32).astype(BF16)
+
+
+def gelu_parts(v):
+    cdf = 0.5 + 0.5 * lax.erf(v * math.sqrt(0.5))
+    return cdf, jnp.exp(-0.5 * (v * v)) * (1.0 / math.sqrt(2.0 * math.pi))
+
+
+def fold(v):
+    return jnp.sum(v.reshape(v.shape[0] // 8, 8, v.shape[1]), 0)
+
+
+def wide(v):
+    return jnp.concatenate([v, v], axis=1)
+
+
+def where_am_i():
+    return lax.axis_index("dp"), lax.axis_index("tensor")
+
+
+def greet_all(dp_size, dp, core):
+    barrier = pltpu.get_barrier_semaphore()
+
+    def one(n, c):
+        pl.semaphore_signal(
+            barrier, inc=1, device_id=(lax.rem(dp + n, dp_size), core), device_id_type=MESH
+        )
+        return c
+
+    lax.fori_loop(1, dp_size, one, 0)
+    pl.semaphore_signal(barrier, inc=1, device_id=(dp, 1 - core), device_id_type=MESH)
+    pl.semaphore_wait(barrier, dp_size)
+
+
+def remote(src, dst, send, recv, device):
+    return pltpu.make_async_remote_copy(
+        src_ref=src,
+        dst_ref=dst,
+        send_sem=send,
+        recv_sem=recv,
+        device_id=device,
+        device_id_type=MESH,
+    )
+
+
+def front_kernel(
+    dims,
+    x_hbm,
+    go_hbm,
+    col_ref,
+    w1_hbm,
+    w2_hbm,
+    b1_hbm,
+    msg_ref,
+    keep_ref,
+    tb2_ref,
+    st_o,
+    yt_o,
+    xp_o,
+    f_o,
+    hid_o,
+    slope_o,
+    mix_o,
+    yp_o,
+    stat_o,
+    prm_o,
+    colf_o,
+    tw1_o,
+    tw2_o,
+    w1p_o,
+    w2p_o,
+    b1p_o,
+    xf,
+    gof,
+    tok,
+    wide_prm,
+    colr,
+    tmp_w,
+    s_buf,
+    tok_send,
+    tok_recv,
+    pair_send,
+    pair_recv,
+    loc_sem,
+):
+    n_dp, ni, ch, pat, tp, unit_d = dims
+    dp, core = where_am_i()
+    full = 2 * ch
+    step = pl.program_id(0)
+    other = (dp, 1 - core)
+    mine = pl.ds(pl.multiple_of(core * ch, 128), ch)
+    my_first = core * ni
+
+    def pair_copies():
+        return [
+            remote(
+                x_hbm.at[pl.ds((1 - core) * ni, ni)],
+                xf.at[:, mine],
+                pair_send.at[0],
+                pair_recv.at[0],
+                other,
+            ),
+            remote(
+                go_hbm.at[pl.ds((1 - core) * ni, ni)],
+                gof.at[:, mine],
+                pair_send.at[1],
+                pair_recv.at[1],
+                other,
+            ),
+            remote(col_ref, colr.at[mine], pair_send.at[2], pair_recv.at[2], other),
+            remote(w1_hbm, w1p_o, pair_send.at[3], pair_recv.at[3], other),
+            remote(w2_hbm, w2p_o, pair_send.at[4], pair_recv.at[4], other),
+            remote(b1_hbm, b1p_o, pair_send.at[5], pair_recv.at[5], other),
+        ]
+
+    def local_copies():
+        return [
+            pltpu.make_async_copy(
+                x_hbm.at[pl.ds(my_first, ni)], xf.at[:, mine], loc_sem.at[0]
+            ),
+            pltpu.make_async_copy(
+                go_hbm.at[pl.ds(my_first, ni)], gof.at[:, mine], loc_sem.at[1]
+            ),
+        ]
+
+    def token_copy(n):
+        return remote(
+            msg_ref,
+            tok.at[dp],
+            tok_send.at[n],
+            tok_recv.at[dp],
+            (lax.rem(dp + n, n_dp), core),
+        )
+
+    def token_arrival(n):
+        source = lax.rem(dp + n_dp - n, n_dp)
+        return remote(
+            msg_ref, tok.at[source], tok_send.at[n], tok_recv.at[source], (source, core)
+        )
+
+    @pl.when(step == 0)
+    def _():
+        for c in local_copies():
+            c.start()
+        greet_all(n_dp, dp, core)
+
+        def send(n, c):
+            token_copy(n).start()
+            return c
+
+        lax.fori_loop(1, n_dp, send, 0)
+        for c in pair_copies():
+            c.start()
+        tok[dp] = msg_ref[...]
+        colr[mine, :] = col_ref[...]
+        for c in local_copies():
+            c.wait()
+        copies = pair_copies()
+        for n in range(3):
+            copies[n].wait_recv()
+
+        colf_o[...] = colr[...]
+
+        def arrive(n, c):
+            token_arrival(n).wait_recv()
+            return c
+
+        lax.fori_loop(1, n_dp, arrive, 0)
+        rows = unit_d
+        lane = lax.broadcasted_iota(jnp.int32, (rows, pad_lanes(pat)), 1)
+        for d in range(n_dp):
+            block = tok[d].astype(F32)
+            tmp_w[0, rows * d : rows * (d + 1), :] = jnp.where(
+                lane <= pat, block[:rows], 0.0
+            )
+            tmp_w[1, rows * d : rows * (d + 1), :] = jnp.where(
+                lane < pat, block[rows:], 0.0
+            )
+            prm_o[2 * rows * d : 2 * rows * (d + 1), :] = block[:, 128:256]
+        tw1_o[...] = tmp_w[0].astype(BF16)
+        tw2_o[...] = tmp_w[1].astype(BF16)
+        for n in range(4):
+            at = PRM_LANE - 128 + n
+            wide_prm[n] = jnp.broadcast_to(prm_o[:, at : at + 1], (full, 128))
+
+    image = step
+    chunk = 64
+    chunks = [slice(r, r + chunk) for r in range(0, full, chunk)]
+    xp_o[0, :, 128:] = jnp.zeros((full, xp_o.shape[2] - 128), BF16)
+    yp_o[0, :, 128:] = jnp.zeros((full, xp_o.shape[2] - 128), BF16)
+    lanes = xp_o.shape[2]
+    total = jnp.zeros((8, lanes), F32)
+    square = jnp.zeros((8, lanes), F32)
+    for r in chunks:
+        xp_o[0, r, :pat] = xf[image, r, :]
+        v = xp_o[0, r, :].astype(F32)
+        total += fold(v)
+        square += fold(v * v)
+    mean0 = jnp.sum(total, 0, keepdims=True) / full
+    rstd0 = lax.rsqrt(jnp.sum(square, 0, keepdims=True) / full - mean0 * mean0 + EPS)
+    one_lane = lax.broadcasted_iota(jnp.int32, (chunk, lanes), 1) == pat
+    for r in chunks:
+        v = xp_o[0, r, :].astype(F32)
+        f = (v - mean0) * rstd0 * wide(wide_prm[0, r, :]) + wide(wide_prm[2, r, :])
+        f_o[0, r, :] = jnp.where(one_lane, 1.0, f).astype(BF16)
+    total = jnp.zeros((8, lanes), F32)
+    square = jnp.zeros((8, lanes), F32)
+    big = 128
+    for r0 in range(0, full, big):
+        pre = nt(f_o[0, r0 : r0 + big, :], tw1_o[...])
+        for a in range(0, big, 32):
+            v = pre[a : a + 32]
+            cdf, pdf = gelu_parts(v)
+            hid_o[0, r0 + a : r0 + a + 32, :] = (v * cdf).astype(BF16)
+            slope_o[0, r0 + a : r0 + a + 32, :] = (cdf + v * pdf).astype(BF16)
+    for r0 in range(0, full, big):
+        out = nn(hid_o[0, r0 : r0 + big, :], tw2_o[...])
+        for a in range(0, big, chunk):
+            r = slice(r0 + a, r0 + a + chunk)
+            v = xp_o[0, r, :].astype(F32) + (out[a : a + chunk] + tb2_ref[0:1, :])
+            mix_o[0, r, :] = v
+            total += fold(v)
+            square += fold(v * v)
+    mean1 = jnp.sum(total, 0, keepdims=True) / full
+    rstd1 = lax.rsqrt(jnp.sum(square, 0, keepdims=True) / full - mean1 * mean1 + EPS)
+    for r in chunks:
+        v = mix_o[0, r, :]
+        s = (v - mean1) * rstd1 * wide(wide_prm[1, r, :]) + wide(wide_prm[3, r, :])
+        s_buf[r, :] = s.astype(BF16)
+    ident = eye(tp, lanes)
+    st_o[...] = nt(ident, s_buf[...]).astype(BF16)
+    kept = keep_ref[pl.ds(my_first + image, 1), :].astype(F32)
+    count = jnp.sum(kept, 1, keepdims=True)
+    pick = lax.broadcasted_iota(jnp.int32, (chunk, 128), 1) == my_first + image
+    for r in chunks:
+        g = jnp.sum(jnp.where(pick, colr[r, :], 0.0), 1, keepdims=True)
+        y = kept * (gof[image, r, :].astype(F32) + g / count)
+        yp_o[0, r, :pat] = y.astype(BF16)
+    yt_o[...] = nt(ident, yp_o[0]).astype(BF16)
+    stat_o[0] = jnp.zeros((8, lanes), F32)
+    stat_o[0, 0:1, :] = mean0
+    stat_o[0, 1:2, :] = rstd0
+    stat_o[0, 2:3, :] = mean1
+    stat_o[0, 3:4, :] = rstd1
+    stat_o[0, 4:5, :pat] = kept
+    stat_o[0, 5:6, :] = jnp.broadcast_to(1.0 / count, (1, lanes))
+
+    @pl.when(step == ni - 1)
+    def _():
+        copies = pair_copies()
+        for n in range(3, 6):
+            copies[n].wait_recv()
+        for c in copies:
+            c.wait_send()
+
+        def sent(n, c):
+            token_copy(n).wait_send()
+            return c
+
+        lax.fori_loop(1, n_dp, sent, 0)
+
+
+PRM_LANE = 200
+
+
+def pad_lanes(n):
+    return up(n, 128)
+
+
+def front(n_dp, x, go, col, w1, w2, b1, msg, keep, tb2):
+    images, ch, pat = x.shape
+    ni = images // 2
+    full = 2 * ch
+    unit_d = msg.shape[0] // 2
+    ds = unit_d * n_dp
+    tp = up(pat, 16)
+    lanes = pad_lanes(pat)
+    hid = w1.shape[1]
+    sds = jax.ShapeDtypeStruct
+    per = lambda *s: pl.BlockSpec((1,) + s, lambda i: (i, 0, 0))
+    once = lambda *s: pl.BlockSpec(s, lambda i: (0, 0))
+    outs = [
+        (sds((ni * tp, full), BF16), pl.BlockSpec((tp, full), lambda i: (i, 0))),
+        (sds((ni * tp, full), BF16), pl.BlockSpec((tp, full), lambda i: (i, 0))),
+        (sds((ni, full, lanes), BF16), per(full, lanes)),
+        (sds((ni, full, lanes), BF16), per(full, lanes)),
+        (sds((ni, full, ds), BF16), per(full, ds)),
+        (sds((ni, full, ds), BF16), per(full, ds)),
+        (sds((ni, full, lanes), F32), per(full, lanes)),
+        (sds((ni, full, lanes), BF16), per(full, lanes)),
+        (sds((ni, 8, lanes), F32), per(8, lanes)),
+        (sds((full, 128), F32), once(full, 128)),
+        (sds((full, 128), F32), once(full, 128)),
+        (sds((ds, lanes), BF16), once(ds, lanes)),
+        (sds((ds, lanes), BF16), once(ds, lanes)),
+        (sds(w1.shape, BF16), ANY),
+        (sds(w2.shape, BF16), ANY),
+        (sds(b1.shape, F32), ANY),
+    ]
+    return pl.pallas_call(
+        functools.partial(front_kernel, (n_dp, ni, ch, pat, tp, unit_d)),
+        grid=(ni,),
+        out_shape=[o[0] for o in outs],
+        in_specs=[ANY, ANY, once(*col.shape), ANY, ANY, ANY]
+        + [once(*msg.shape), once(*keep.shape), once(*tb2.shape)],
+        out_specs=[o[1] for o in outs],
+        scratch_shapes=[
+            pltpu.VMEM((ni, full, pat), BF16),
+            pltpu.VMEM((ni, full, pat), BF16),
+            pltpu.VMEM((n_dp,) + msg.shape, BF16),
+            pltpu.VMEM((4, full, 128), F32),
+            pltpu.VMEM((full, 128), F32),
+            pltpu.VMEM((2, ds, lanes), F32),
+            pltpu.VMEM((full, lanes), BF16),
+            pltpu.SemaphoreType.DMA((n_dp,)),
+            pltpu.SemaphoreType.DMA((n_dp,)),
+            pltpu.SemaphoreType.DMA((6,)),
+            pltpu.SemaphoreType.DMA((6,)),
+            pltpu.SemaphoreType.DMA((2,)),
+        ],
+        compiler_params=pltpu.CompilerParams(
+            collective_id=0, has_side_effects=True, vmem_limit_bytes=VMEM_BYTES
+        ),
+        name="front",
+    )(x, go, col, w1, w2, b1, msg, keep, tb2)
+
+
+def back_kernel(
+    dims,
+    st_hbm,
+    yt_hbm,
+    w1_hbm,
+    w1p_hbm,
+    w2_hbm,
+    w2p_hbm,
+    b1_ref,
+    b1p_ref,
+    xp_hbm,
+    f_hbm,
+    hid_hbm,
+    slope_hbm,
+    mix_hbm,
+    yp_hbm,
+    stat_ref,
+    prm_ref,
+    colf_ref,
+    tw1_ref,
+    tw2_ref,
+    bo_hbm,
+    gi_hbm,
+    pool_o,
+    sq_o,
+    red_o,
+    gw_o,
+    st,
+    yt,
+    sc,
+    yc,
+    w1s,
+    w2s,
+    gh,
+    ph,
+    gs,
+    pb,
+    ra,
+    r1,
+    b2,
+    r2,
+    b3,
+    r3,
+    xs,
+    fs,
+    hs,
+    ls,
+    ms,
+    ys,
+    bos,
+    gis,
+    ob,
+    sb,
+    ol,
+    tg,
+    wide_prm,
+    acc_col,
+    acc_tok,
+    row_h,
+    row_c,
+    row_p,
+    pool_a,
+    pool_r,
+    sq_a,
+    sq_r,
+    msgs,
+    msgr,
+    red_a,
+    red_r,
+    w_sem,
+    in_sem,
+    sa,
+    rsa,
+    s1,
+    rs1,
+    s2,
+    rs2,
+    s3,
+    rs3,
+    out_s,
+    out_r,
+    out_l,
+    tok_s,
+    tok_r,
+    fin_s,
+    fin_r,
+):
+    n_dp, ni, ch, pat, tp, unit_d, nz, ny, nx = dims
+    dp, core = where_am_i()
+    x = lax.rem(dp, nx)
+    y = lax.rem(dp // nx, ny)
+    z = dp // (nx * ny)
+    other = (dp, 1 - core)
+    x_dev = ((z * ny + y) * nx + (1 - x), core)
+    y_dev = ((z * ny + (1 - y)) * nx + x, core)
+    full = 2 * ch
+    rows_own = full // n_dp
+    half = w1s.shape[2]
+    n_blk = half // BLK
+    toks = ni * tp
+    toks_pad = gh.shape[0]
+    lanes = xs.shape[2]
+    my_first = core * ni
+    ds = tw1_ref.shape[0]
+
+    loads = [
+        pltpu.make_async_copy(st_hbm, st.at[pl.ds(0, toks)], w_sem.at[0]),
+        pltpu.make_async_copy(yt_hbm, yt.at[pl.ds(0, toks)], w_sem.at[1]),
+        pltpu.make_async_copy(w1p_hbm, w1s.at[1], w_sem.at[2]),
+        pltpu.make_async_copy(w2p_hbm, w2s.at[1], w_sem.at[3]),
+        pltpu.make_async_copy(w1_hbm, w1s.at[0], w_sem.at[4]),
+        pltpu.make_async_copy(w2_hbm, w2s.at[0], w_sem.at[5]),
+    ]
+    for c in loads:
+        c.start()
+
+    def image_loads(i, slot):
+        pairs = ((xp_hbm, xs), (f_hbm, fs), (hid_hbm, hs), (slope_hbm, ls), (mix_hbm, ms), (yp_hbm, ys))
+        return [
+            pltpu.make_async_copy(a.at[i], b.at[slot], in_sem.at[slot, n])
+            for n, (a, b) in enumerate(pairs)
+        ]
+
+    for c in image_loads(0, 0):
+        c.start()
+    greet_all(n_dp, dp, core)
+
+    zero_rows = jnp.zeros((toks_pad - toks, gh.shape[1]), BF16)
+    gh[toks:, :] = zero_rows
+    ph[toks:, :] = zero_rows
+    sc[:, toks // 128 * 128 :] = jnp.zeros((full, toks_pad - toks // 128 * 128), BF16)
+    yc[:, toks // 128 * 128 :] = jnp.zeros((full, toks_pad - toks // 128 * 128), BF16)
+    row_h[...] = jnp.zeros_like(row_h)
+    row_c[...] = jnp.zeros_like(row_c)
+    row_p[...] = jnp.zeros_like(row_p)
+    acc_col[...] = jnp.zeros_like(acc_col)
+    acc_tok[...] = jnp.zeros_like(acc_tok)
+    pool_a[...] = jnp.zeros_like(pool_a)
+    sq_a[...] = jnp.zeros_like(sq_a)
+    for n in range(4):
+        at = PRM_LANE - 128 + n
+        wide_prm[n] = jnp.broadcast_to(prm_ref[:, at : at + 1], (full, 128))
+    at = 2 * ni
+    wide_prm[4] = jnp.broadcast_to(colf_ref[:, at : at + 1], (full, 128))
+    ob[...] = jnp.zeros_like(ob)
+    sb[...] = jnp.zeros_like(sb)
+    ident = eye(256, 256)
+    loads[0].wait()
+    loads[1].wait()
+    for c0 in range(0, full, 256):
+        sc[c0 : c0 + 256, :toks] = nt(ident, st[:toks, c0 : c0 + 256]).astype(BF16)
+        yc[c0 : c0 + 256, :toks] = nt(ident, yt[:toks, c0 : c0 + 256]).astype(BF16)
+    for n in range(2, 6):
+        loads[n].wait()
+
+    def pair_copy(slot):
+        return remote(pb.at[slot], ra.at[slot], sa.at[slot], rsa.at[slot], other)
+
+    def first_copies(slot):
+        return (
+            remote(
+                gs.at[slot, 0, :, :, 1 - x], r1.at[slot, 0], s1.at[slot, 0], rs1.at[slot, 0], x_dev
+            ),
+            remote(gs.at[slot, 1, :, 1 - y], r1.at[slot, 1], s1.at[slot, 1], rs1.at[slot, 1], y_dev),
+        )
+
+    def second_copies(slot):
+        return (
+            remote(b2.at[slot, 0, :, 1 - y], r2.at[slot, 0], s2.at[slot, 0], rs2.at[slot, 0], y_dev),
+            remote(b2.at[slot, 1, :, 1 - x], r2.at[slot, 1], s2.at[slot, 1], rs2.at[slot, 1], x_dev),
+        )
+
+    def third_copies(slot):
+        out = []
+        for n in range(1, nz):
+            to = lax.rem(z + n, nz)
+            out.append(
+                remote(
+                    b3.at[slot, to],
+                    r3.at[slot, n - 1],
+                    s3.at[slot, n - 1],
+                    rs3.at[slot, n - 1],
+                    ((to * ny + y) * nx + x, core),
+                )
+            )
+        return out
+
+    def finish_third(j):
+        slot = lax.rem(j, 2)
+        for c in third_copies(slot):
+            c.wait()
+        at = pl.ds(pl.multiple_of(j * BLK, BLK), BLK)
+        for m in range(2):
+            v = b3[slot, z, m].astype(F32)
+            for n in range(nz - 1):
+                v = v + r3[slot, n, m].astype(F32)
+            gw_o[m, :, at] = v
+
+    def finish_second(j):
+        slot = lax.rem(j, 2)
+        for c in second_copies(slot):
+            c.wait()
+        for m, mine in ((0, y), (1, x)):
+            for k in range(nz):
+                v = b2[slot, m, k, mine].astype(F32) + r2[slot, m, k].astype(F32)
+                b3[slot, k, m] = v.astype(BF16)
+        for c in third_copies(slot):
+            c.start()
+
+    def finish_first(j):
+        slot = lax.rem(j, 2)
+        for c in first_copies(slot):
+            c.wait()
+        for k in range(nz):
+            for n in range(2):
+                v = gs[slot, 0, k, n, x].astype(F32) + r1[slot, 0, k, n].astype(F32)
+                b2[slot, 0, k, n] = v.astype(BF16)
+                v = gs[slot, 1, k, y, n].astype(F32) + r1[slot, 1, k, n].astype(F32)
+                b2[slot, 1, k, n] = v.astype(BF16)
+        for c in second_copies(slot):
+            c.start()
+
+    def hidden_block(side, j, bias_ref):
+        at = pl.ds(pl.multiple_of(j * BLK, BLK), BLK)
+        col = pl.ds(pl.multiple_of(side * half + j * BLK, BLK), BLK)
+        w1 = w1s[side, :, at]
+        w2 = w2s[side, at, :]
+        bias = bias_ref[0:1, at]
+        for i in range(ni):
+            r0 = i * tp
+            r = slice(r0, r0 + tp)
+            pre = nn(st[r, :], w1)
+            up_grad = nt(yt[r, :], w2)
+            acc = jnp.zeros((8, BLK), F32)
+            for a in range(0, tp, 16):
+                v = pre[a : a + 16] + bias
+                cdf, pdf = gelu_parts(v)
+                gh[r0 + a : r0 + a + 16, col] = (v * cdf).astype(BF16)
+                p = up_grad[a : a + 16] * (cdf + v * pdf)
+                ph[r0 + a : r0 + a + 16, col] = p.astype(BF16)
+                acc += fold(p)
+            row = jnp.sum(acc, 0, keepdims=True)
+            row_h[0:1, col] += row
+            row_h[1 + i : 2 + i, col] = row
+        return nn(sc[...], ph[:, col]), nn(yc[...], gh[:, col])
+
+    def split(v, k):
+        per = full // nz
+        return v[k * per : (k + 1) * per].reshape(ny, nx, rows_own, BLK)
+
+    def block_step(j, carry):
+        slot = lax.rem(j, 2)
+        for m, v in enumerate(hidden_block(1, j, b1p_ref)):
+            for k in range(nz):
+                pb[slot, m, k] = split(v, k).astype(BF16)
+        pair_copy(slot).start()
+        grads = hidden_block(0, j, b1_ref)
+        pair_copy(slot).wait()
+        for m, v in enumerate(grads):
+            for k in range(nz):
+                gs[slot, m, k] = (split(v, k) + ra[slot, m, k].astype(F32)).astype(BF16)
+
+        @pl.when(j >= 3)
+        def _():
+            finish_third(j - 3)
+
+        @pl.when(j >= 2)
+        def _():
+            finish_second(j - 2)
+
+        @pl.when(j >= 1)
+        def _():
+            finish_first(j - 1)
+
+        for c in first_copies(slot):
+            c.start()
+        return carry
+
+    lax.fori_loop(0, n_blk, block_step, 0)
+
+    def second_half(i):
+        r = pl.ds(pl.multiple_of(i * tp, 16), tp)
+        g = gh[r, :]
+        p = ph[r, :]
+        s = st[r, :]
+        yv = yt[r, :]
+        both = nt(s, s) * nt(p, p) + nt(g, g) * nt(yv, yv)
+        sq = jnp.sum(jnp.sum(both, 0, keepdims=True), 1, keepdims=True)
+        rh = row_h[pl.ds(1 + i, 1), :]
+        rc = jnp.sum(fold(yv.astype(F32)), 0, keepdims=True)
+        row_c[0:1, :] += rc
+        sq = sq + jnp.sum(rh * rh, 1, keepdims=True) + jnp.sum(rc * rc, 1, keepdims=True)
+        lane = lax.broadcasted_iota(jnp.int32, (1, 128), 1)
+        sq_a[0:1, :] += jnp.where(lane == my_first + i, sq, 0.0)
+        out = nn(gh[r, :half], w2s[0]) + nn(gh[r, half:], w2s[1])
+        grad = nt(ph[r, :half], w1s[0]) + nt(ph[r, half:], w1s[1])
+        ob[:tp, :] = out.astype(BF16)
+        sb[:tp, :] = grad.astype(BF16)
+
+    def drain(i):
+        @pl.when(i == 0)
+        def _():
+            finish_third(n_blk - 3)
+            finish_second(n_blk - 2)
+            finish_first(n_blk - 1)
+
+        @pl.when(i == 1)
+        def _():
+            finish_third(n_blk - 2)
+            finish_second(n_blk - 1)
+
+        @pl.when(i == 2)
+        def _():
+            finish_third(n_blk - 1)
+
+    chunk = 64
+    chunks = [slice(r, r + chunk) for r in range(0, full, chunk)]
+
+    def out_copies(i, slot):
+        there = pl.ds(pl.multiple_of((1 - core) * ch, 128), ch)
+        here = pl.ds(pl.multiple_of(core * ch, 128), ch)
+        res = []
+        for n, (src, dst) in enumerate(((bos, bo_hbm), (gis, gi_hbm))):
+            res.append(
+                remote(
+                    src.at[slot, there],
+                    dst.at[my_first + i],
+                    out_s.at[slot, n],
+                    out_r.at[i, n],
+                    other,
+                )
+            )
+            res.append(
+                pltpu.make_async_copy(
+                    src.at[slot, here], dst.at[my_first + i], out_l.at[slot, n]
+                )
+            )
+        return res
+
+    def out_arrivals(i):
+        there = pl.ds(pl.multiple_of((1 - core) * ch, 128), ch)
+        return [
+            remote(
+                src.at[0, there],
+                dst.at[(1 - core) * ni + i],
+                out_s.at[0, n],
+                out_r.at[i, n],
+                other,
+            )
+            for n, (src, dst) in enumerate(((bos, bo_hbm), (gis, gi_hbm)))
+        ]
+
+    def image_step(i, carry):
+        slot = lax.rem(i, 2)
+        second_half(i)
+        drain(i)
+
+        @pl.when(i + 1 < ni)
+        def _():
+            for c in image_loads(i + 1, 1 - slot):
+                c.start()
+
+        for c in image_loads(i, slot):
+            c.wait()
+
+        @pl.when(i >= 2)
+        def _():
+            for n, c in enumerate(out_copies(i - 2, slot)):
+                if n % 2 == 0:
+                    c.wait_send()
+                else:
+                    c.wait()
+
+        stats = stat_ref[i]
+        mean0, rstd0, mean1, rstd1 = (stats[n : n + 1, :] for n in range(4))
+        kept = stats[4:5, :]
+        inv_count = stats[5:6, 0:128]
+        lane = lax.broadcasted_iota(jnp.int32, (chunk, 128), 1)
+        pick = lane == my_first + i
+        zero8 = jnp.zeros((8, lanes), F32)
+        e_sum, eu_sum = zero8, zero8
+        outs, backs = [], []
+        for c0 in range(0, full, 256):
+            outs.append(nt(ident, ob[:, c0 : c0 + 256]))
+            backs.append(nt(ident, sb[:, c0 : c0 + 256]))
+
+        def piece(parts, r):
+            c0 = r.start // 256
+            return parts[c0][r.start - 256 * c0 : r.stop - 256 * c0]
+
+        for r in chunks:
+            mix = ms[slot, r, :]
+            bo = kept * (mix + (piece(outs, r) + wide(wide_prm[4, r, :])))
+            bos[slot, r, :] = bo[:, :pat].astype(BF16)
+            pooled = jnp.sum(bo, 1, keepdims=True) * inv_count
+            pool_a[r, :] += jnp.where(pick, pooled, 0.0)
+        for r in chunks:
+            sg = piece(backs, r)
+            unit = (ms[slot, r, :] - mean1) * rstd1
+            su = sg * unit
+            acc_col[1, r, :] += su[:, :128] + su[:, 128:]
+            acc_col[3, r, :] += sg[:, :128] + sg[:, 128:]
+            e = sg * wide(wide_prm[1, r, :])
+            e_sum += fold(e)
+            eu_sum += fold(e * unit)
+        em = jnp.sum(e_sum, 0, keepdims=True) / full
+        eum = jnp.sum(eu_sum, 0, keepdims=True) / full
+        b2_sum = zero8
+        for r in chunks:
+            sg = piece(backs, r)
+            unit = (ms[slot, r, :] - mean1) * rstd1
+            e = sg * wide(wide_prm[1, r, :])
+            mg = ys[slot, r, :].astype(F32) + rstd1 * (e - em - unit * eum)
+            ms[slot, r, :] = mg
+            ol[r, :] = mg.astype(BF16)
+            b2_sum += fold(mg)
+        row_p[0:8, :] += b2_sum
+        big = 128
+        for r0 in range(0, full, big):
+            hg = nt(ol[r0 : r0 + big, :], tw2_ref[...])
+            for a in range(0, big, 32):
+                r = slice(r0 + a, r0 + a + 32)
+                tg[r, :] = (hg[a : a + 32] * ls[slot, r, :].astype(F32)).astype(BF16)
+        acc_tok[0] += tn(tg[...], fs[slot])
+        acc_tok[1] += tn(hs[slot], ol[...])
+        e_sum, eu_sum = zero8, zero8
+        valid = lax.broadcasted_iota(jnp.int32, (chunk, lanes), 1) < pat
+        firsts = []
+        for r0 in range(0, full, big):
+            firsts.append(nn(tg[r0 : r0 + big, :], tw1_ref[...]))
+
+        def first_piece(r):
+            v = firsts[r.start // big][r.start % big : r.start % big + chunk]
+            return jnp.where(valid, v, 0.0)
+
+        for r in chunks:
+            fg = first_piece(r)
+            unit = (xs[slot, r, :].astype(F32) - mean0) * rstd0
+            su = fg * unit
+            acc_col[0, r, :] += su[:, :128] + su[:, 128:]
+            acc_col[2, r, :] += fg[:, :128] + fg[:, 128:]
+            e = fg * wide(wide_prm[0, r, :])
+            e_sum += fold(e)
+            eu_sum += fold(e * unit)
+        em = jnp.sum(e_sum, 0, keepdims=True) / full
+        eum = jnp.sum(eu_sum, 0, keepdims=True) / full
+        for r in chunks:
+            fg = first_piece(r)
+            unit = (xs[slot, r, :].astype(F32) - mean0) * rstd0
+            e = fg * wide(wide_prm[0, r, :])
+            gi = ms[slot, r, :] + rstd0 * (e - em - unit * eum)
+            gis[slot, r, :] = gi[:, :pat].astype(BF16)
+        for c in out_copies(i, slot):
+            c.start()
+        return carry
+
+    lax.fori_loop(0, ni, image_step, 0)
+
+    lane = lax.broadcasted_iota(jnp.int32, (2 * unit_d, 128), 1)
+    h_0 = jnp.where(core == 0, row_h[0:1, :half], row_h[0:1, half:])
+    h_1 = jnp.where(core == 0, row_h[0:1, half:], row_h[0:1, :half])
+    per_h = half // n_dp
+    per_c = ch // n_dp
+    tail = msgs.shape[1] - 2 * unit_d
+    b2_row = jnp.sum(row_p[...], 0, keepdims=True)
+
+    def cut(v, start, size):
+        n = v.shape[1]
+        v = jnp.broadcast_to(v, (8, n))
+        v = pltpu.roll(v, (n - start) % n, 1)[0:1, :lanes]
+        return jnp.where(lax.broadcasted_iota(jnp.int32, (1, lanes), 1) < size, v, 0.0)
+
+    for d in range(n_dp):
+        top = jnp.concatenate(
+            [
+                acc_tok[0, unit_d * d : unit_d * (d + 1), :],
+                acc_tok[1, unit_d * d : unit_d * (d + 1), :],
+            ],
+            axis=0,
+        )
+        rows = slice(rows_own * d, rows_own * (d + 1))
+        right = top[:, 128:]
+        for n in range(4):
+            s = jnp.sum(acc_col[n, rows, :], 1, keepdims=True)
+            right = jnp.where(lane == PRM_LANE - 128 + n, s, right)
+        msgs[d, : 2 * unit_d, :128] = top[:, :128].astype(BF16)
+        msgs[d, : 2 * unit_d, 128:] = right.astype(BF16)
+        extra = jnp.concatenate(
+            [
+                b2_row,
+                cut(h_0, per_h * d, per_h),
+                cut(h_1, per_h * d, per_h),
+                cut(row_c[0:1, :], per_c * d, per_c),
+                cut(row_c[0:1, :], ch + per_c * d, per_c),
+                jnp.zeros((tail - 5, lanes), F32),
+            ],
+            axis=0,
+        )
+        msgs[d, 2 * unit_d :, :] = extra.astype(BF16)
+
+    def token_send(n):
+        to = lax.rem(dp + n, n_dp)
+        return remote(msgs.at[to], msgr.at[dp], tok_s.at[n], tok_r.at[dp], (to, core))
+
+    def token_arrival(n):
+        source = lax.rem(dp + n_dp - n, n_dp)
+        return remote(
+            msgs.at[source], msgr.at[source], tok_s.at[n], tok_r.at[source], (source, core)
+        )
+
+    def send(n, c):
+        token_send(n).start()
+        return c
+
+    lax.fori_loop(1, n_dp, send, 0)
+    pool_copy = remote(
+        pool_a.at[pl.ds(pl.multiple_of((1 - core) * ch, 128), ch)], pool_r, fin_s.at[0], fin_r.at[0], other
+    )
+    pool_copy.start()
+    sq_copy = remote(sq_a, sq_r, fin_s.at[1], fin_r.at[1], other)
+    sq_copy.start()
+    msgr[dp] = msgs[dp]
+
+    def arrive(n, c):
+        token_arrival(n).wait_recv()
+        return c
+
+    lax.fori_loop(1, n_dp, arrive, 0)
+    total = msgr[0].astype(F32)
+    for d in range(1, n_dp):
+        total = total + msgr[d].astype(F32)
+    red_a[...] = total
+    red_copy = remote(red_a, red_r, fin_s.at[2], fin_r.at[2], other)
+    red_copy.start()
+
+    def sent(n, c):
+        token_send(n).wait_send()
+        return c
+
+    lax.fori_loop(1, n_dp, sent, 0)
+    for i in (ni - 2, ni - 1):
+        for n, c in enumerate(out_copies(i, i % 2)):
+            if n % 2 == 0:
+                c.wait_send()
+            else:
+                c.wait()
+    for i in range(ni):
+        for c in out_arrivals(i):
+            c.wait_recv()
+    pool_copy.wait()
+    sq_copy.wait()
+    pool_o[...] = pool_a[pl.ds(pl.multiple_of(core * ch, 128), ch), :] + pool_r[...]
+    sq_o[...] = sq_a[...] + sq_r[...]
+    red_copy.wait()
+    red_o[...] = red_a[...] + red_r[...]
+
+
+def back(n_dp, grid3, st, yt, w1, w1p, w2, w2p, b1, b1p, xp, f, hid, slope, mix, yp, stat, prm, colf, tw1, tw2, pat):
+    ni, full, lanes = xp.shape
+    ch = full // 2
+    half = w1.shape[1]
+    toks = st.shape[0]
+    tp = toks // ni
+    ds = tw1.shape[0]
+    unit_d = ds // n_dp
+    toks_pad = up(toks, 256)
+    nz, ny, nx = grid3
+    rows_own = full // n_dp
+    n_msg = up(2 * unit_d + 5, 16)
+    sds = jax.ShapeDtypeStruct
+    vm = pltpu.VMEM
+    dma = pltpu.SemaphoreType.DMA
+    part = (nz, ny, nx, rows_own, BLK)
+    return pl.pallas_call(
+        functools.partial(back_kernel, (n_dp, ni, ch, pat, tp, unit_d, nz, ny, nx)),
+        out_shape=[
+            sds((2 * ni, ch, pat), BF16),
+            sds((2 * ni, ch, pat), BF16),
+            sds((ch, 128), F32),
+            sds((8, 128), F32),
+            sds((n_msg, lanes), F32),
+            sds((2, rows_own, half), F32),
+        ],
+        in_specs=[ANY] * 6 + [VM, VM] + [ANY] * 6 + [VM] * 5,
+        out_specs=[ANY, ANY, VM, VM, VM, VM],
+        scratch_shapes=[
+            vm((toks_pad, full), BF16),
+            vm((toks_pad, full), BF16),
+            vm((full, toks_pad), BF16),
+            vm((full, toks_pad), BF16),
+            vm((2, full, half), BF16),
+            vm((2, half, full), BF16),
+            vm((toks_pad, 2 * half), BF16),
+            vm((toks_pad, 2 * half), BF16),
+            vm((2, 2) + part, BF16),
+            vm((2, 2) + part, BF16),
+            vm((2, 2) + part, BF16),
+            vm((2, 2, nz, 2, rows_own, BLK), BF16),
+            vm((2, 2, nz, 2, rows_own, BLK), BF16),
+            vm((2, 2, nz, rows_own, BLK), BF16),
+            vm((2, nz, 2, rows_own, BLK), BF16),
+            vm((2, nz - 1, 2, rows_own, BLK), BF16),
+            vm((2, full, lanes), BF16),
+            vm((2, full, lanes), BF16),
+            vm((2, full, ds), BF16),
+            vm((2, full, ds), BF16),
+            vm((2, full, lanes), F32),
+            vm((2, full, lanes), BF16),
+            vm((2, full, pat), BF16),
+            vm((2, full, pat), BF16),
+            vm((256, full), BF16),
+            vm((256, full), BF16),
+            vm((full, lanes), BF16),
+            vm((full, ds), BF16),
+            vm((5, full, 128), F32),
+            vm((4, full, 128), F32),
+            vm((2, ds, lanes), F32),
+            vm((8, 2 * half), F32),
+            vm((8, full), F32),
+            vm((8, lanes), F32),
+            vm((full, 128), F32),
+            vm((ch, 128), F32),
+            vm((8, 128), F32),
+            vm((8, 128), F32),
+            vm((n_dp, n_msg, lanes), BF16),
+            vm((n_dp, n_msg, lanes), BF16),
+            vm((n_msg, lanes), F32),
+            vm((n_msg, lanes), F32),
+            dma((6,)),
+            dma((2, 6)),
+            dma((2,)),
+            dma((2,)),
+            dma((2, 2)),
+            dma((2, 2)),
+            dma((2, 2)),
+            dma((2, 2)),
+            dma((2, nz - 1)),
+            dma((2, nz - 1)),
+            dma((2, 2)),
+            dma((ni, 2)),
+            dma((2, 2)),
+            dma((n_dp,)),
+            dma((n_dp,)),
+            dma((3,)),
+            dma((3,)),
+        ],
+        compiler_params=pltpu.CompilerParams(
+            collective_id=1, has_side_effects=True, vmem_limit_bytes=VMEM_BYTES
+        ),
+        name="back",
+    )(st, yt, w1, w1p, w2, w2p, b1, b1p, xp, f, hid, slope, mix, yp, stat, prm, colf, tw1, tw2)
+
+
+def finish_kernel(
+    dims,
+    bo_ref,
+    gi_ref,
+    pool_ref,
+    sq_ref,
+    red_ref,
+    gw_ref,
+    bo_o,
+    pool_o,
+    gi_o,
+    gain_o,
+    shift_o,
+    tw1_o,
+    tb1_o,
+    tw2_o,
+    tb2_o,
+    w1_o,
+    b1_o,
+    w2_o,
+    b2_o,
+    sq_o,
+):
+    pat, unit_d, per_h, per_c = dims
+    _, core = where_am_i()
+    bo_o[...] = bo_ref[...].astype(F32)
+    gi_o[...] = gi_ref[...].astype(F32)
+
+    @pl.when(pl.program_id(0) == 0)
+    def _():
+        images = pool_o.shape[0]
+        pool_o[...] = jnp.transpose(pool_ref[...])[:images]
+        sq_o[...] = sq_ref[0:1, :images]
+        red = red_ref[...]
+        flat = jnp.transpose(red[: 2 * unit_d, 128:])
+        at = PRM_LANE - 128
+        gain_o[...] = flat[at : at + 2]
+        shift_o[...] = flat[at + 2 : at + 4]
+        first = jnp.transpose(red[:unit_d, :])
+        tw1_o[...] = first[:pat]
+        tb1_o[...] = first[pat : pat + 1]
+        tw2_o[...] = red[unit_d : 2 * unit_d, :pat]
+        n = 2 * unit_d
+        tb2_o[...] = red[n : n + 1, :pat]
+        w1_o[...] = gw_ref[0]
+        w2_o[...] = jnp.transpose(gw_ref[1])
+        b1_o[...] = jnp.where(core == 0, red[n + 1 : n + 2, :per_h], red[n + 2 : n + 3, :per_h])
+        b2_o[...] = jnp.where(core == 0, red[n + 3 : n + 4, :per_c], red[n + 4 : n + 5, :per_c])
+
+
+def finish(bo, gi, pool, sq, red, gw, unit_d, per_h, per_c):
+    images, ch, pat = bo.shape
+    ds = unit_d
+    sds = jax.ShapeDtypeStruct
+    once = lambda s: pl.BlockSpec(s, lambda i: (0,) * len(s))
+    per = pl.BlockSpec((1, ch, pat), lambda i: (i, 0, 0))
+    rows_own, half = gw.shape[1:]
+    outs = [
+        (images, ch, pat),
+        (images, ch),
+        (images, ch, pat),
+        (2, rows_own),
+        (2, rows_own),
+        (pat, ds),
+        (1, ds),
+        (ds, pat),
+        (1, pat),
+        (rows_own, half),
+        (1, per_h),
+        (half, rows_own),
+        (1, per_c),
+        (1, images),
+    ]
+    res = pl.pallas_call(
+        functools.partial(finish_kernel, (pat, unit_d, per_h, per_c)),
+        grid=(images,),
+        out_shape=[sds(s, F32) for s in outs],
+        in_specs=[per, per] + [once(a.shape) for a in (pool, sq, red, gw)],
+        out_specs=[per if len(s) == 3 else once(s) for s in outs],
+        compiler_params=pltpu.CompilerParams(vmem_limit_bytes=VMEM_BYTES),
+        name="finish",
+    )(bo, gi, pool, sq, red, gw)
+    return tuple(r.reshape(-1) if r.shape[0] == 1 else r for r in res)
+
+
+def fused_body(
+    n_dp,
+    grid3,
+    mixer_input,
+    keep_mask,
+    ln_gain,
+    ln_shift,
+    token_w1,
+    token_b1,
+    token_w2,
+    token_b2,
+    chan_w1,
+    chan_b1,
+    chan_w2,
+    chan_b2,
+    grad_out,
+    grad_pooled,
+):
+    images, ch, pat = mixer_input.shape
+    unit_d = token_b1.shape[0]
+    half = chan_b1.shape[0]
+    lanes = pad_lanes(pat)
+    left = jnp.concatenate([token_w1.T, token_w2], 0)
+    bias = jnp.pad(token_b1[:, None], ((0, unit_d), (0, PRM_LANE - pat - 1)))
+    norms = jnp.concatenate([ln_gain.T, ln_shift.T], 1)
+    msg = jnp.concatenate(
+        [left, bias, jnp.pad(norms, ((0, 0), (0, lanes - PRM_LANE - 4)))], 1
+    )
+    col = jnp.concatenate([grad_pooled.T, chan_b2.astype(F32)[:, None]], 1)
+    col = jnp.pad(col, ((0, 0), (0, 128 - col.shape[1])))
+    b1 = jnp.broadcast_to(chan_b1.astype(F32)[None, :], (8, half))
+    tb2 = jnp.broadcast_to(jnp.pad(token_b2.astype(F32), (0, lanes - pat))[None, :], (8, lanes))
+    st, yt, xp, f, hid, slope, mix, yp, stat, prm, colf, tw1, tw2, w1p, w2p, b1p = front(
+        n_dp, mixer_input, grad_out, col, chan_w1, chan_w2, b1, msg, keep_mask, tb2
+    )
+    bo, gi, pool, sq, red, gw = back(
+        n_dp, grid3, st, yt, chan_w1, w1p, chan_w2, w2p, b1, b1p, xp, f, hid, slope, mix, yp,
+        stat, prm, colf, tw1, tw2, pat,
+    )
+    return finish(bo, gi, pool, sq, red, gw, unit_d, half // n_dp, ch // n_dp)
+
 
 D = 768
 
@@ -208,8 +1349,12 @@
 
 
 def solution(mesh):
+    n_dp, n_tensor = mesh.shape["dp"], mesh.shape["tensor"]
+    chosen = body
+    if (n_dp, n_tensor) == (16, 2):
+        chosen = functools.partial(fused_body, n_dp, (4, 2, 2))
     return jax.shard_map(
-        body,
+        chosen,
         mesh=mesh,
         in_specs=(
             P("dp", "tensor", None),

time: 1180 us -> 167 us (0.14)
  waiting for transfers between devices: 573 us -> 0 us
  blocking collectives: 290 us -> 0 us
  matrix products: 155 us -> 0 us
  Pallas kernels: 0 us -> 135 us
  other arithmetic: 60 us -> 3.5 us
  local copies, waits for them, and re-layouts: 76.1 us -> 23.8 us
  between operations: 17.2 us -> 0.7 us
    reduce_scatter x4 -> x0, waiting for transfers between devices: 410 us -> none  [the longest x1 131 us: body(): lax.psum_scatter(column_block.astype(jnp.bfloat16), 'dp', scatter_dimensi...]
    unnamed x14 -> x0, waiting for transfers between devices: 160 us -> none
    dot_general x16 -> x0, matrix products: 155 us -> none  [the longest x1 39.7 us: body(): jnp.einsum('bcp,ch->bhp', section, chan_w1, preferred_element_type=jnp.fl...]
    all_gather x4 -> x0, blocking collectives: 154 us -> none  [the longest x1 42.5 us: body(): lax.all_gather(ln_gain, 'dp', axis=1, tiled=True)]
    pallas_call x0 -> x3, Pallas kernels: none -> 135 us  [the longest x1 95.3 us: back(): pl.pallas_call(functools.partial(back_kernel, (n_dp, ni, ch, pat, tp, uni...]
    unnamed x2 -> x0, blocking collectives: 81.1 us -> none
    unnamed x94 -> x12, local copies, waits for them, and re-layouts: 76 us -> 19.5 us
    psum x6 -> x0, blocking collectives: 55.6 us -> none  [the longest x1 36.8 us: body(): share_tb2 = lax.psum(grad_token_b2, ('dp', 'tensor'))]
  transfers between devices with their start and end apart: 10 -> 0, of which waited for: 8 -> 0; matrix products, arithmetic and copies ran while one was open for 15% -> 0% of each run, Pallas kernels for 0% -> 0%
where the time goes in v1:
time: 167 us; the launch traced here: 163 us
  Pallas kernels  135 us (81%)
  local copies, waits for them, and re-layouts  23.8 us (14%)
  other arithmetic  3.5 us (2%)
    pallas_call x1, Pallas kernels, back(): pl.pallas_call(functools.partial(back_kernel, (n_dp, ni, ch, pat, tp, uni...  95.3 us
    pallas_call x1, Pallas kernels, front(): pl.pallas_call(functools.partial(front_kernel, (n_dp, ni, ch, pat, tp, un...  29.1 us
    unnamed x12, local copies, waits for them, and re-layouts  19.5 us
    pallas_call x1, Pallas kernels, finish(): pl.pallas_call(functools.partial(finish_kernel, (pat, unit_d, per_h, per_...  10.9 us

profile of v1, /device:TPU:0, one launch (start us, length us, event | category | flops | bytes accessed | tf_op | source)
XLA Modules:
  0.0 163.3 jit_solution(17875384006822596705)
XLA Ops:
  0.6 0.7 pad_maximum_fusion.1
  1.3 0.7 pad_convert_fusion
  2.0 0.7 reshape.50
  2.7 0.7 copy.50
  3.4 0.6 broadcast_in_dim.25.tb2_ref
  4.0 0.1 copy.51
  4.1 1.4 fusion.4.msg_ref
  5.5 0.7 pad_maximum_fusion
  6.3 1.3 broadcast_in_dim.23.b1_hbm.b1_ref
  7.6 0.0 copy-start
  7.6 0.1 copy.49
  7.7 0.7 pad.19.col_ref
  8.4 4.0 %copy.52.x_hbm = bf16[12,384,196]{2,1,0:T(8,128)(2,1)} copy(bf16[12,384,196]{1,2,0:T(8,128)(2,1)} %param.14) | data formatting | bytes 3612672 | tf_op args[0]
  12.4 0.0 copy-done
  12.4 2.4 %copy.53.go_hbm = bf16[12,384,196]{2,1,0:T(8,128)(2,1)} copy(bf16[12,384,196]{1,2,0:T(8,128)(2,1)S(1)} %copy-done) | data formatting | bytes 3612672 | tf_op args[12]
  14.9 29.1 %front.1 = (bf16[1248,768]{1,0:T(8,128)(2,1)}, bf16[1248,768]{1,0:T(8,128)(2,1)}, bf16[6,768,256]{2,1,0:T(8,128)(2,1)}, bf16[6,768,256]{2,1,0:T(8,128)(2,1)}, bf...) custom-call(bf16[12,384,196]{2,1,0:T(8,128)(2,1)} %copy.52.x_hbm, ...), custom_call_target="tpu_custom_call" | custom-call | tf_op jit(solution)/shard_map/front/pallas_call | solution.py:339
  44.0 95.3 %back.1 = (bf16[12,384,196]{2,1,0:T(8,128)(2,1)}, bf16[12,384,196]{2,1,0:T(8,128)(2,1)}, f32[384,128]{1,0:T(8,128)}, f32[8,128]{1,0:T(8,128)}, f32[64,256]{1,0:T(8,128)}, /*index=5*/f32[2,48,1536]{2,1,0:T(8,128)}) custom-call(bf16[1248,768]{1,0:T(8,128)(2,1)} %get-tuple-element.50.st_hbm, bf16[1248,768]{1,0:T(8,128)(2,1)} %get-tuple-element.51.yt_hbm, ...), custom_call_target="tpu_custom_call" | custom-call | tf_op jit(solution)/shard_map/back/pallas_call | solution.py:940
  139.3 10.9 %finish.1 = (f32[12,384,196]{2,1,0:T(8,128)}, f32[12,384]{1,0:T(8,128)}, f32[12,384,196]{2,1,0:T(8,128)}, f32[2,48]{1,0:T(2,128)}, f32[2,48]{1,0:T(2,128)}, /*in...) custom-call(bf16[12,384,196]{2,1,0:T(8,128)(2,1)} %get-tuple-element, ...), custom_call_target="tpu_custom_call" | custom-call | tf_op jit(solution)/shard_map/finish/pallas_call | solution.py:1093
  150.3 0.0 copy-start.2
  150.3 0.0 copy-start.1
  150.3 5.7 %copy.54 = f32[12,384,196]{1,2,0:T(8,128)} copy(f32[12,384,196]{2,1,0:T(8,128)} %get-tuple-element.114) | data formatting | bytes 7225344
  156.0 0.0 copy-done.2
  156.1 0.7 copy.56
  156.7 0.0 copy-done.1
  156.7 1.0 copy.57
  157.7 5.7 %copy.55 = f32[12,384,196]{1,2,0:T(8,128)} copy(f32[12,384,196]{2,1,0:T(8,128)} %get-tuple-element.116) | data formatting | bytes 7225344
Async XLA Ops:
  7.6 4.8 %copy-start = (bf16[12,384,196]{1,2,0:T(8,128)(2,1)S(1)}, bf16[12,384,196]{1,2,0:T(8,128)(2,1)}, u32[]{:S(2)}) copy-start(bf16[12,384,196]{1,2,0:T(8,128)(2,1)} %param.26) | copy-start | bytes 5419012
  150.3 5.8 %copy-start.2 = (f32[196,24]{1,0:T(8,128)S(1)}, f32[196,24]{1,0:T(8,128)}, u32[]{:S(2)}) copy-start(f32[196,24]{1,0:T(8,128)} %get-tuple-element.119) | copy-start | bytes 56452
  150.3 6.4 %copy-start.1 = (f32[1536,48]{1,0:T(8,128)S(1)}, f32[1536,48]{1,0:T(8,128)}, u32[]{:S(2)}) copy-start(f32[1536,48]{1,0:T(8,128)} %get-tuple-element.125) | copy-start | bytes 884740

commit v2 on v1

--- a/solution.py
+++ b/solution.py
@@ -49,10 +49,6 @@
     return jnp.sum(v.reshape(v.shape[0] // 8, 8, v.shape[1]), 0)
 
 
-def wide(v):
-    return jnp.concatenate([v, v], axis=1)
-
-
 def where_am_i():
     return lax.axis_index("dp"), lax.axis_index("tensor")
 
@@ -82,40 +78,71 @@
     )
 
 
+ROWS = 16
+
+
+def row_pieces(pat):
+    return [slice(r, min(r + ROWS, pat)) for r in range(0, pat, ROWS)]
+
+
+def lane_pieces(full):
+    return [slice(c, c + 256) for c in range(0, full, 256)]
+
+
+def across(v, full):
+    return jnp.concatenate([v] * (full // 128), axis=1)
+
+
+def centre(v):
+    n = v.shape[1]
+    d = v - jnp.sum(v, 1, keepdims=True) * (1.0 / n)
+    r = lax.rsqrt(jnp.sum(d * d, 1, keepdims=True) * (1.0 / n) + EPS)
+    return d * r, r
+
+
 def front_kernel(
     dims,
     x_hbm,
     go_hbm,
-    col_ref,
+    gp_ref,
     w1_hbm,
     w2_hbm,
-    b1_hbm,
-    msg_ref,
+    b1_ref,
+    cb2_ref,
+    gain_ref,
+    shift_ref,
+    tw1_ref,
+    tb1_ref,
+    tw2_ref,
+    tb2_ref,
     keep_ref,
-    tb2_ref,
     st_o,
     yt_o,
-    xp_o,
+    u0_o,
     f_o,
     hid_o,
     slope_o,
     mix_o,
-    yp_o,
-    stat_o,
-    prm_o,
-    colf_o,
-    tw1_o,
-    tw2_o,
+    u1_o,
+    col_o,
+    norm_o,
+    pack_o,
+    tw_o,
+    twt_o,
     w1p_o,
     w2p_o,
-    b1p_o,
     xf,
     gof,
+    msg,
+    square,
+    pack,
+    packf,
     tok,
-    wide_prm,
-    colr,
     tmp_w,
-    s_buf,
+    prm,
+    keep_t,
+    tb2_w,
+    outs,
     tok_send,
     tok_recv,
     pair_send,
@@ -125,62 +152,69 @@
     n_dp, ni, ch, pat, tp, unit_d = dims
     dp, core = where_am_i()
     full = 2 * ch
-    step = pl.program_id(0)
+    image = pl.program_id(0)
     other = (dp, 1 - core)
     mine = pl.ds(pl.multiple_of(core * ch, 128), ch)
     my_first = core * ni
+    ds = unit_d * n_dp
+    rows_own = 2 * unit_d
+    images = 2 * ni
+    bias_rows = b1_ref.shape[1] // ch
+    kp = f_o.shape[1]
 
     def pair_copies():
+        theirs = pl.ds((1 - core) * ni, ni)
+        pairs = [
+            (pack, packf.at[:, mine]),
+            (x_hbm.at[theirs], xf.at[:, :, mine]),
+            (go_hbm.at[theirs], gof.at[:, :, mine]),
+            (w1_hbm, w1p_o),
+            (w2_hbm, w2p_o),
+        ]
         return [
-            remote(
-                x_hbm.at[pl.ds((1 - core) * ni, ni)],
-                xf.at[:, mine],
-                pair_send.at[0],
-                pair_recv.at[0],
-                other,
-            ),
-            remote(
-                go_hbm.at[pl.ds((1 - core) * ni, ni)],
-                gof.at[:, mine],
-                pair_send.at[1],
-                pair_recv.at[1],
-                other,
-            ),
-            remote(col_ref, colr.at[mine], pair_send.at[2], pair_recv.at[2], other),
-            remote(w1_hbm, w1p_o, pair_send.at[3], pair_recv.at[3], other),
-            remote(w2_hbm, w2p_o, pair_send.at[4], pair_recv.at[4], other),
-            remote(b1_hbm, b1p_o, pair_send.at[5], pair_recv.at[5], other),
+            remote(a, b, pair_send.at[n], pair_recv.at[n], other)
+            for n, (a, b) in enumerate(pairs)
         ]
 
     def local_copies():
+        ours = pl.ds(my_first, ni)
         return [
-            pltpu.make_async_copy(
-                x_hbm.at[pl.ds(my_first, ni)], xf.at[:, mine], loc_sem.at[0]
-            ),
-            pltpu.make_async_copy(
-                go_hbm.at[pl.ds(my_first, ni)], gof.at[:, mine], loc_sem.at[1]
-            ),
+            pltpu.make_async_copy(x_hbm.at[ours], xf.at[:, :, mine], loc_sem.at[0]),
+            pltpu.make_async_copy(go_hbm.at[ours], gof.at[:, :, mine], loc_sem.at[1]),
         ]
 
     def token_copy(n):
-        return remote(
-            msg_ref,
-            tok.at[dp],
-            tok_send.at[n],
-            tok_recv.at[dp],
-            (lax.rem(dp + n, n_dp), core),
-        )
+        to = lax.rem(dp + n, n_dp)
+        return remote(msg, tok.at[dp], tok_send.at[n], tok_recv.at[dp], (to, core))
 
     def token_arrival(n):
         source = lax.rem(dp + n_dp - n, n_dp)
         return remote(
-            msg_ref, tok.at[source], tok_send.at[n], tok_recv.at[source], (source, core)
+            msg, tok.at[source], tok_send.at[n], tok_recv.at[source], (source, core)
         )
 
-    @pl.when(step == 0)
+    @pl.when(image == 0)
     def _():
         for c in local_copies():
             c.start()
+        square[...] = jnp.zeros_like(square)
+        at = pat - 128
+        square[at : at + 1, :unit_d] = tb1_ref[...].astype(F32)
+        square[at + 4 : at + 6, :rows_own] = gain_ref[...].astype(F32)
+        square[at + 6 : at + 8, :rows_own] = shift_ref[...].astype(F32)
+        columns = jnp.transpose(square[...])[:rows_own]
+        tmp_w[0, :rows_own, :] = jnp.zeros((rows_own, kp), F32)
+        tmp_w[0, :unit_d, :pat] = tw1_ref[...].astype(F32)
+        tmp_w[0, unit_d:rows_own, :pat] = tw2_ref[...].astype(F32)
+        msg[:, :128] = tmp_w[0, :rows_own, :128].astype(BF16)
+        msg[:, 128:] = (tmp_w[0, :rows_own, 128:] + columns).astype(BF16)
+        pack[...] = jnp.zeros_like(pack)
+        pack[:images, :] = gp_ref[...]
+        pack[images : images + 1, :] = cb2_ref[...].astype(F32)
+        for n in range(bias_rows):
+            pack[images + 1 + n : images + 2 + n, :] = b1_ref[
+                :, n * ch : (n + 1) * ch
+            ].astype(F32)
         greet_all(n_dp, dp, core)
 
         def send(n, c):
@@ -188,107 +222,95 @@
             return c
 
         lax.fori_loop(1, n_dp, send, 0)
-        for c in pair_copies():
+        copies = pair_copies()
+        for c in copies:
             c.start()
-        tok[dp] = msg_ref[...]
-        colr[mine, :] = col_ref[...]
+        tok[dp] = msg[...]
+        packf[:, mine] = pack[...]
+        keep_t[...] = jnp.zeros_like(keep_t)
+        keep_t[:images, :pat] = keep_ref[...].astype(F32)
+        keep_t[images : images + 1, :pat] = tb2_ref[...].astype(F32)
+        turned = jnp.transpose(keep_t[...])
+        keep_t[:, :] = turned
+        tb2_w[...] = jnp.broadcast_to(turned[:tp, images : images + 1], (tp, 128))
         for c in local_copies():
             c.wait()
-        copies = pair_copies()
         for n in range(3):
             copies[n].wait_recv()
-
-        colf_o[...] = colr[...]
+        pack_o[...] = packf[...]
 
         def arrive(n, c):
             token_arrival(n).wait_recv()
             return c
 
         lax.fori_loop(1, n_dp, arrive, 0)
-        rows = unit_d
-        lane = lax.broadcasted_iota(jnp.int32, (rows, pad_lanes(pat)), 1)
+        lane = lax.broadcasted_iota(jnp.int32, (unit_d, kp), 1)
         for d in range(n_dp):
             block = tok[d].astype(F32)
-            tmp_w[0, rows * d : rows * (d + 1), :] = jnp.where(
-                lane <= pat, block[:rows], 0.0
+            tmp_w[0, unit_d * d : unit_d * (d + 1), :] = jnp.where(
+                lane <= pat, block[:unit_d], 0.0
             )
-            tmp_w[1, rows * d : rows * (d + 1), :] = jnp.where(
-                lane < pat, block[rows:], 0.0
+            tmp_w[1, unit_d * d : unit_d * (d + 1), :] = jnp.where(
+                lane < pat, block[unit_d:], 0.0
             )
-            prm_o[2 * rows * d : 2 * rows * (d + 1), :] = block[:, 128:256]
-        tw1_o[...] = tmp_w[0].astype(BF16)
-        tw2_o[...] = tmp_w[1].astype(BF16)
-        for n in range(4):
-            at = PRM_LANE - 128 + n
-            wide_prm[n] = jnp.broadcast_to(prm_o[:, at : at + 1], (full, 128))
-
-    image = step
-    chunk = 64
-    chunks = [slice(r, r + chunk) for r in range(0, full, chunk)]
-    xp_o[0, :, 128:] = jnp.zeros((full, xp_o.shape[2] - 128), BF16)
-    yp_o[0, :, 128:] = jnp.zeros((full, xp_o.shape[2] - 128), BF16)
-    lanes = xp_o.shape[2]
-    total = jnp.zeros((8, lanes), F32)
-    square = jnp.zeros((8, lanes), F32)
-    for r in chunks:
-        xp_o[0, r, :pat] = xf[image, r, :]
-        v = xp_o[0, r, :].astype(F32)
-        total += fold(v)
-        square += fold(v * v)
-    mean0 = jnp.sum(total, 0, keepdims=True) / full
-    rstd0 = lax.rsqrt(jnp.sum(square, 0, keepdims=True) / full - mean0 * mean0 + EPS)
-    one_lane = lax.broadcasted_iota(jnp.int32, (chunk, lanes), 1) == pat
-    for r in chunks:
-        v = xp_o[0, r, :].astype(F32)
-        f = (v - mean0) * rstd0 * wide(wide_prm[0, r, :]) + wide(wide_prm[2, r, :])
-        f_o[0, r, :] = jnp.where(one_lane, 1.0, f).astype(BF16)
-    total = jnp.zeros((8, lanes), F32)
-    square = jnp.zeros((8, lanes), F32)
-    big = 128
-    for r0 in range(0, full, big):
-        pre = nt(f_o[0, r0 : r0 + big, :], tw1_o[...])
-        for a in range(0, big, 32):
+            prm[rows_own * d : rows_own * (d + 1), :] = tok[d, :, 128:]
+        r = lax.broadcasted_iota(jnp.int32, (16, 128), 0)
+        c = lax.broadcasted_iota(jnp.int32, (16, 128), 1)
+        pick = ((c - (at + 4) == r) & (r < 4)).astype(F32).astype(BF16)
+        norm_o[...] = nt(pick, prm[...])
+        ident = eye(kp, kp)
+        for n in range(2):
+            w = tmp_w[n].astype(BF16)
+            tw_o[n] = w
+            t = nt(ident, w)
+            r = lax.broadcasted_iota(jnp.int32, t.shape, 0)
+            twt_o[n] = jnp.where(r < pat, t, 0.0)[:tp].astype(BF16)
+
+    pieces = row_pieces(pat)
+    last = slice(pat // ROWS * ROWS, tp)
+    blank = jnp.zeros((last.stop - last.start, full), BF16)
+    for ref in (st_o, yt_o):
+        ref[last, :] = blank
+    for ref in (u0_o, mix_o, u1_o):
+        ref[0, last, :] = blank
+    f_o[0, last.start :, :] = jnp.zeros((kp - last.start, full), BF16)
+    f_o[0, pat : pat + 1, :] = jnp.ones((1, full), BF16)
+    col_o[0, :, last, :] = jnp.zeros((3, tp - last.start, 128), F32)
+    for r in pieces:
+        unit, rstd = centre(xf[image, r, :].astype(F32))
+        u0_o[0, r, :] = unit.astype(BF16)
+        f_o[0, r, :] = (unit * norm_o[0:1, :] + norm_o[2:3, :]).astype(BF16)
+        col_o[0, 0, r, :] = jnp.broadcast_to(rstd, (r.stop - r.start, 128))
+    for c in lane_pieces(full):
+        pre = nn(tw_o[0], f_o[0, :, c])
+        for a in range(0, ds, 32):
             v = pre[a : a + 32]
             cdf, pdf = gelu_parts(v)
-            hid_o[0, r0 + a : r0 + a + 32, :] = (v * cdf).astype(BF16)
-            slope_o[0, r0 + a : r0 + a + 32, :] = (cdf + v * pdf).astype(BF16)
-    for r0 in range(0, full, big):
-        out = nn(hid_o[0, r0 : r0 + big, :], tw2_o[...])
-        for a in range(0, big, chunk):
-            r = slice(r0 + a, r0 + a + chunk)
-            v = xp_o[0, r, :].astype(F32) + (out[a : a + chunk] + tb2_ref[0:1, :])
-            mix_o[0, r, :] = v
-            total += fold(v)
-            square += fold(v * v)
-    mean1 = jnp.sum(total, 0, keepdims=True) / full
-    rstd1 = lax.rsqrt(jnp.sum(square, 0, keepdims=True) / full - mean1 * mean1 + EPS)
-    for r in chunks:
-        v = mix_o[0, r, :]
-        s = (v - mean1) * rstd1 * wide(wide_prm[1, r, :]) + wide(wide_prm[3, r, :])
-        s_buf[r, :] = s.astype(BF16)
-    ident = eye(tp, lanes)
-    st_o[...] = nt(ident, s_buf[...]).astype(BF16)
-    kept = keep_ref[pl.ds(my_first + image, 1), :].astype(F32)
-    count = jnp.sum(kept, 1, keepdims=True)
-    pick = lax.broadcasted_iota(jnp.int32, (chunk, 128), 1) == my_first + image
-    for r in chunks:
-        g = jnp.sum(jnp.where(pick, colr[r, :], 0.0), 1, keepdims=True)
-        y = kept * (gof[image, r, :].astype(F32) + g / count)
-        yp_o[0, r, :pat] = y.astype(BF16)
-    yt_o[...] = nt(ident, yp_o[0]).astype(BF16)
-    stat_o[0] = jnp.zeros((8, lanes), F32)
-    stat_o[0, 0:1, :] = mean0
-    stat_o[0, 1:2, :] = rstd0
-    stat_o[0, 2:3, :] = mean1
-    stat_o[0, 3:4, :] = rstd1
-    stat_o[0, 4:5, :pat] = kept
-    stat_o[0, 5:6, :] = jnp.broadcast_to(1.0 / count, (1, lanes))
-
-    @pl.when(step == ni - 1)
+            hid_o[0, a : a + 32, c] = (v * cdf).astype(BF16)
+            slope_o[0, a : a + 32, c] = (cdf + v * pdf).astype(BF16)
+        outs[:, c] = nn(twt_o[1], hid_o[0, :, c])
+    for r in pieces:
+        v = xf[image, r, :].astype(F32) + (outs[r, :] + across(tb2_w[r, :], full))
+        mix_o[0, r, :] = v.astype(BF16)
+        unit, rstd = centre(v)
+        u1_o[0, r, :] = unit.astype(BF16)
+        st_o[r, :] = (unit * norm_o[1:2, :] + norm_o[3:4, :]).astype(BF16)
+        col_o[0, 1, r, :] = jnp.broadcast_to(rstd, (r.stop - r.start, 128))
+    number = my_first + image
+    count = jnp.sum(keep_ref[pl.ds(number, 1), :].astype(F32), 1, keepdims=True)
+    g = packf[pl.ds(number, 1), :] / count
+    for r in pieces:
+        size = r.stop - r.start
+        lane = lax.broadcasted_iota(jnp.int32, (size, 128), 1)
+        k = jnp.sum(jnp.where(lane == number, keep_t[r, :128], 0.0), 1, keepdims=True)
+        yt_o[r, :] = (k * (gof[image, r, :].astype(F32) + g)).astype(BF16)
+        col_o[0, 2, r, :] = jnp.broadcast_to(k, (size, 128))
+
+    @pl.when(image == ni - 1)
     def _():
         copies = pair_copies()
-        for n in range(3, 6):
-            copies[n].wait_recv()
+        for c in copies[3:]:
+            c.wait_recv()
         for c in copies:
             c.wait_send()
 
@@ -299,69 +321,67 @@
         lax.fori_loop(1, n_dp, sent, 0)
 
 
-PRM_LANE = 200
-
-
-def pad_lanes(n):
-    return up(n, 128)
-
-
-def front(n_dp, x, go, col, w1, w2, b1, msg, keep, tb2):
-    images, ch, pat = x.shape
+def front(n_dp, x, go, gp, w1, w2, b1, cb2, gain, shift, tw1, tb1, tw2, tb2, keep):
+    images, pat, ch = x.shape
     ni = images // 2
     full = 2 * ch
-    unit_d = msg.shape[0] // 2
+    unit_d = tw1.shape[0]
     ds = unit_d * n_dp
     tp = up(pat, 16)
-    lanes = pad_lanes(pat)
-    hid = w1.shape[1]
+    kp = up(pat, 256)
+    n_pack = up(images + 1 + b1.shape[1] // ch, 8)
     sds = jax.ShapeDtypeStruct
-    per = lambda *s: pl.BlockSpec((1,) + s, lambda i: (i, 0, 0))
-    once = lambda *s: pl.BlockSpec(s, lambda i: (0, 0))
+    per = lambda *s: pl.BlockSpec((1,) + s, lambda i: (i,) + (0,) * len(s))
+    once = lambda *s: pl.BlockSpec(s, lambda i: (0,) * len(s))
+    tokens = pl.BlockSpec((tp, full), lambda i: (i, 0))
     outs = [
-        (sds((ni * tp, full), BF16), pl.BlockSpec((tp, full), lambda i: (i, 0))),
-        (sds((ni * tp, full), BF16), pl.BlockSpec((tp, full), lambda i: (i, 0))),
-        (sds((ni, full, lanes), BF16), per(full, lanes)),
-        (sds((ni, full, lanes), BF16), per(full, lanes)),
-        (sds((ni, full, ds), BF16), per(full, ds)),
-        (sds((ni, full, ds), BF16), per(full, ds)),
-        (sds((ni, full, lanes), F32), per(full, lanes)),
-        (sds((ni, full, lanes), BF16), per(full, lanes)),
-        (sds((ni, 8, lanes), F32), per(8, lanes)),
-        (sds((full, 128), F32), once(full, 128)),
-        (sds((full, 128), F32), once(full, 128)),
-        (sds((ds, lanes), BF16), once(ds, lanes)),
-        (sds((ds, lanes), BF16), once(ds, lanes)),
+        (sds((ni * tp, full), BF16), tokens),
+        (sds((ni * tp, full), BF16), tokens),
+        (sds((ni, tp, full), BF16), per(tp, full)),
+        (sds((ni, kp, full), BF16), per(kp, full)),
+        (sds((ni, ds, full), BF16), per(ds, full)),
+        (sds((ni, ds, full), BF16), per(ds, full)),
+        (sds((ni, tp, full), BF16), per(tp, full)),
+        (sds((ni, tp, full), BF16), per(tp, full)),
+        (sds((ni, 3, tp, 128), F32), per(3, tp, 128)),
+        (sds((16, full), F32), once(16, full)),
+        (sds((n_pack, full), F32), once(n_pack, full)),
+        (sds((2, ds, kp), BF16), once(2, ds, kp)),
+        (sds((2, tp, ds), BF16), once(2, tp, ds)),
         (sds(w1.shape, BF16), ANY),
         (sds(w2.shape, BF16), ANY),
-        (sds(b1.shape, F32), ANY),
     ]
+    small = (b1, cb2, gain, shift, tw1, tb1, tw2, tb2, keep)
     return pl.pallas_call(
         functools.partial(front_kernel, (n_dp, ni, ch, pat, tp, unit_d)),
         grid=(ni,),
         out_shape=[o[0] for o in outs],
-        in_specs=[ANY, ANY, once(*col.shape), ANY, ANY, ANY]
-        + [once(*msg.shape), once(*keep.shape), once(*tb2.shape)],
+        in_specs=[ANY, ANY, once(*gp.shape), ANY, ANY] + [once(*a.shape) for a in small],
         out_specs=[o[1] for o in outs],
         scratch_shapes=[
-            pltpu.VMEM((ni, full, pat), BF16),
-            pltpu.VMEM((ni, full, pat), BF16),
-            pltpu.VMEM((n_dp,) + msg.shape, BF16),
-            pltpu.VMEM((4, full, 128), F32),
-            pltpu.VMEM((full, 128), F32),
-            pltpu.VMEM((2, ds, lanes), F32),
-            pltpu.VMEM((full, lanes), BF16),
+            pltpu.VMEM((ni, pat, full), BF16),
+            pltpu.VMEM((ni, pat, full), BF16),
+            pltpu.VMEM((2 * unit_d, kp), BF16),
+            pltpu.VMEM((128, 128), F32),
+            pltpu.VMEM((n_pack, ch), F32),
+            pltpu.VMEM((n_pack, full), F32),
+            pltpu.VMEM((n_dp, 2 * unit_d, kp), BF16),
+            pltpu.VMEM((2, ds, kp), F32),
+            pltpu.VMEM((full, 128), BF16),
+            pltpu.VMEM((kp, kp), F32),
+            pltpu.VMEM((tp, 128), F32),
+            pltpu.VMEM((tp, full), F32),
             pltpu.SemaphoreType.DMA((n_dp,)),
             pltpu.SemaphoreType.DMA((n_dp,)),
-            pltpu.SemaphoreType.DMA((6,)),
-            pltpu.SemaphoreType.DMA((6,)),
+            pltpu.SemaphoreType.DMA((5,)),
+            pltpu.SemaphoreType.DMA((5,)),
             pltpu.SemaphoreType.DMA((2,)),
         ],
         compiler_params=pltpu.CompilerParams(
             collective_id=0, has_side_effects=True, vmem_limit_bytes=VMEM_BYTES
         ),
         name="front",
-    )(x, go, col, w1, w2, b1, msg, keep, tb2)
+    )(x, go, gp, w1, w2, *small)
 
 
 def back_kernel(
@@ -372,19 +392,17 @@
     w1p_hbm,
     w2_hbm,
     w2p_hbm,
-    b1_ref,
-    b1p_ref,
-    xp_hbm,
+    u0_hbm,
     f_hbm,
     hid_hbm,
     slope_hbm,
     mix_hbm,
-    yp_hbm,
-    stat_ref,
-    prm_ref,
-    colf_ref,
-    tw1_ref,
-    tw2_ref,
+    u1_hbm,
+    col_hbm,
+    norm_ref,
+    pack_ref,
+    tw_ref,
+    twt_ref,
     bo_hbm,
     gi_hbm,
     pool_o,
@@ -397,6 +415,7 @@
     yc,
     w1s,
     w2s,
+    bias,
     gh,
     ph,
     gs,
@@ -407,20 +426,22 @@
     r2,
     b3,
     r3,
-    xs,
+    us,
     fs,
     hs,
     ls,
     ms,
-    ys,
+    vs,
+    cs,
     bos,
     gis,
     ob,
     sb,
+    mg,
     ol,
     tg,
-    wide_prm,
-    acc_col,
+    fg,
+    acc_norm,
     acc_tok,
     row_h,
     row_c,
@@ -465,9 +486,10 @@
     n_blk = half // BLK
     toks = ni * tp
     toks_pad = gh.shape[0]
-    lanes = xs.shape[2]
+    kp = fs.shape[1]
     my_first = core * ni
-    ds = tw1_ref.shape[0]
+    ds = tw_ref.shape[1]
+    images = 2 * ni
 
     loads = [
         pltpu.make_async_copy(st_hbm, st.at[pl.ds(0, toks)], w_sem.at[0]),
@@ -481,7 +503,15 @@
         c.start()
 
     def image_loads(i, slot):
-        pairs = ((xp_hbm, xs), (f_hbm, fs), (hid_hbm, hs), (slope_hbm, ls), (mix_hbm, ms), (yp_hbm, ys))
+        pairs = (
+            (u0_hbm, us),
+            (f_hbm, fs),
+            (hid_hbm, hs),
+            (slope_hbm, ls),
+            (mix_hbm, ms),
+            (u1_hbm, vs),
+            (col_hbm, cs),
+        )
         return [
             pltpu.make_async_copy(a.at[i], b.at[slot], in_sem.at[slot, n])
             for n, (a, b) in enumerate(pairs)
@@ -499,17 +529,17 @@
     row_h[...] = jnp.zeros_like(row_h)
     row_c[...] = jnp.zeros_like(row_c)
     row_p[...] = jnp.zeros_like(row_p)
-    acc_col[...] = jnp.zeros_like(acc_col)
+    acc_norm[...] = jnp.zeros_like(acc_norm)
     acc_tok[...] = jnp.zeros_like(acc_tok)
     pool_a[...] = jnp.zeros_like(pool_a)
     sq_a[...] = jnp.zeros_like(sq_a)
-    for n in range(4):
-        at = PRM_LANE - 128 + n
-        wide_prm[n] = jnp.broadcast_to(prm_ref[:, at : at + 1], (full, 128))
-    at = 2 * ni
-    wide_prm[4] = jnp.broadcast_to(colf_ref[:, at : at + 1], (full, 128))
-    ob[...] = jnp.zeros_like(ob)
-    sb[...] = jnp.zeros_like(sb)
+    for n in range(half // ch):
+        row = pack_ref[images + 1 + n : images + 2 + n, :]
+        swapped = jnp.concatenate([row[:, ch:], row[:, :ch]], axis=1)
+        row = jnp.where(core == 0, row, swapped)
+        bias[0:1, n * ch : (n + 1) * ch] = row[:, :ch]
+        bias[0:1, half + n * ch : half + (n + 1) * ch] = row[:, ch:]
+    ol[...] = jnp.zeros_like(ol)
     ident = eye(256, 256)
     loads[0].wait()
     loads[1].wait()
@@ -586,12 +616,12 @@
         for c in second_copies(slot):
             c.start()
 
-    def hidden_block(side, j, bias_ref):
+    def hidden_block(side, j):
         at = pl.ds(pl.multiple_of(j * BLK, BLK), BLK)
         col = pl.ds(pl.multiple_of(side * half + j * BLK, BLK), BLK)
         w1 = w1s[side, :, at]
         w2 = w2s[side, at, :]
-        bias = bias_ref[0:1, at]
+        b_row = bias[0:1, col]
         for i in range(ni):
             r0 = i * tp
             r = slice(r0, r0 + tp)
@@ -599,7 +629,7 @@
             up_grad = nt(yt[r, :], w2)
             acc = jnp.zeros((8, BLK), F32)
             for a in range(0, tp, 16):
-                v = pre[a : a + 16] + bias
+                v = pre[a : a + 16] + b_row
                 cdf, pdf = gelu_parts(v)
                 gh[r0 + a : r0 + a + 16, col] = (v * cdf).astype(BF16)
                 p = up_grad[a : a + 16] * (cdf + v * pdf)
@@ -616,11 +646,11 @@
 
     def block_step(j, carry):
         slot = lax.rem(j, 2)
-        for m, v in enumerate(hidden_block(1, j, b1p_ref)):
+        for m, v in enumerate(hidden_block(1, j)):
             for k in range(nz):
                 pb[slot, m, k] = split(v, k).astype(BF16)
         pair_copy(slot).start()
-        grads = hidden_block(0, j, b1_ref)
+        grads = hidden_block(0, j)
         pair_copy(slot).wait()
         for m, v in enumerate(grads):
             for k in range(nz):
@@ -660,8 +690,8 @@
         sq_a[0:1, :] += jnp.where(lane == my_first + i, sq, 0.0)
         out = nn(gh[r, :half], w2s[0]) + nn(gh[r, half:], w2s[1])
         grad = nt(ph[r, :half], w1s[0]) + nt(ph[r, half:], w1s[1])
-        ob[:tp, :] = out.astype(BF16)
-        sb[:tp, :] = grad.astype(BF16)
+        ob[...] = out
+        sb[...] = grad
 
     def drain(i):
         @pl.when(i == 0)
@@ -679,8 +709,7 @@
         def _():
             finish_third(n_blk - 1)
 
-    chunk = 64
-    chunks = [slice(r, r + chunk) for r in range(0, full, chunk)]
+    pieces = [slice(r, r + ROWS) for r in range(0, tp, ROWS)]
 
     def out_copies(i, slot):
         there = pl.ds(pl.multiple_of((1 - core) * ch, 128), ch)
@@ -689,7 +718,7 @@
         for n, (src, dst) in enumerate(((bos, bo_hbm), (gis, gi_hbm))):
             res.append(
                 remote(
-                    src.at[slot, there],
+                    src.at[slot, :, there],
                     dst.at[my_first + i],
                     out_s.at[slot, n],
                     out_r.at[i, n],
@@ -698,7 +727,7 @@
             )
             res.append(
                 pltpu.make_async_copy(
-                    src.at[slot, here], dst.at[my_first + i], out_l.at[slot, n]
+                    src.at[slot, :, here], dst.at[my_first + i], out_l.at[slot, n]
                 )
             )
         return res
@@ -707,7 +736,7 @@
         there = pl.ds(pl.multiple_of((1 - core) * ch, 128), ch)
         return [
             remote(
-                src.at[0, there],
+                src.at[0, :, there],
                 dst.at[(1 - core) * ni + i],
                 out_s.at[0, n],
                 out_r.at[i, n],
@@ -716,6 +745,10 @@
             for n, (src, dst) in enumerate(((bos, bo_hbm), (gis, gi_hbm)))
         ]
 
+    def store_rows(ref, slot, r, v):
+        stop = min(r.stop, pat)
+        ref[slot, r.start : stop, :] = v[: stop - r.start].astype(BF16)
+
     def image_step(i, carry):
         slot = lax.rem(i, 2)
         second_half(i)
@@ -737,104 +770,77 @@
                 else:
                     c.wait()
 
-        stats = stat_ref[i]
-        mean0, rstd0, mean1, rstd1 = (stats[n : n + 1, :] for n in range(4))
-        kept = stats[4:5, :]
-        inv_count = stats[5:6, 0:128]
-        lane = lax.broadcasted_iota(jnp.int32, (chunk, 128), 1)
-        pick = lane == my_first + i
-        zero8 = jnp.zeros((8, lanes), F32)
-        e_sum, eu_sum = zero8, zero8
-        outs, backs = [], []
-        for c0 in range(0, full, 256):
-            outs.append(nt(ident, ob[:, c0 : c0 + 256]))
-            backs.append(nt(ident, sb[:, c0 : c0 + 256]))
-
-        def piece(parts, r):
-            c0 = r.start // 256
-            return parts[c0][r.start - 256 * c0 : r.stop - 256 * c0]
-
-        for r in chunks:
-            mix = ms[slot, r, :]
-            bo = kept * (mix + (piece(outs, r) + wide(wide_prm[4, r, :])))
-            bos[slot, r, :] = bo[:, :pat].astype(BF16)
-            pooled = jnp.sum(bo, 1, keepdims=True) * inv_count
-            pool_a[r, :] += jnp.where(pick, pooled, 0.0)
-        for r in chunks:
-            sg = piece(backs, r)
-            unit = (ms[slot, r, :] - mean1) * rstd1
-            su = sg * unit
-            acc_col[1, r, :] += su[:, :128] + su[:, 128:]
-            acc_col[3, r, :] += sg[:, :128] + sg[:, 128:]
-            e = sg * wide(wide_prm[1, r, :])
-            e_sum += fold(e)
-            eu_sum += fold(e * unit)
-        em = jnp.sum(e_sum, 0, keepdims=True) / full
-        eum = jnp.sum(eu_sum, 0, keepdims=True) / full
-        b2_sum = zero8
-        for r in chunks:
-            sg = piece(backs, r)
-            unit = (ms[slot, r, :] - mean1) * rstd1
-            e = sg * wide(wide_prm[1, r, :])
-            mg = ys[slot, r, :].astype(F32) + rstd1 * (e - em - unit * eum)
-            ms[slot, r, :] = mg
-            ol[r, :] = mg.astype(BF16)
-            b2_sum += fold(mg)
-        row_p[0:8, :] += b2_sum
-        big = 128
-        for r0 in range(0, full, big):
-            hg = nt(ol[r0 : r0 + big, :], tw2_ref[...])
-            for a in range(0, big, 32):
-                r = slice(r0 + a, r0 + a + 32)
-                tg[r, :] = (hg[a : a + 32] * ls[slot, r, :].astype(F32)).astype(BF16)
-        acc_tok[0] += tn(tg[...], fs[slot])
-        acc_tok[1] += tn(hs[slot], ol[...])
-        e_sum, eu_sum = zero8, zero8
-        valid = lax.broadcasted_iota(jnp.int32, (chunk, lanes), 1) < pat
-        firsts = []
-        for r0 in range(0, full, big):
-            firsts.append(nn(tg[r0 : r0 + big, :], tw1_ref[...]))
-
-        def first_piece(r):
-            v = firsts[r.start // big][r.start % big : r.start % big + chunk]
-            return jnp.where(valid, v, 0.0)
-
-        for r in chunks:
-            fg = first_piece(r)
-            unit = (xs[slot, r, :].astype(F32) - mean0) * rstd0
-            su = fg * unit
-            acc_col[0, r, :] += su[:, :128] + su[:, 128:]
-            acc_col[2, r, :] += fg[:, :128] + fg[:, 128:]
-            e = fg * wide(wide_prm[0, r, :])
-            e_sum += fold(e)
-            eu_sum += fold(e * unit)
-        em = jnp.sum(e_sum, 0, keepdims=True) / full
-        eum = jnp.sum(eu_sum, 0, keepdims=True) / full
-        for r in chunks:
-            fg = first_piece(r)
-            unit = (xs[slot, r, :].astype(F32) - mean0) * rstd0
-            e = fg * wide(wide_prm[0, r, :])
-            gi = ms[slot, r, :] + rstd0 * (e - em - unit * eum)
-            gis[slot, r, :] = gi[:, :pat].astype(BF16)
+        chan_bias = pack_ref[images : images + 1, :]
+        zero8 = jnp.zeros((8, full), F32)
+        pool, gain, shift = zero8, zero8, zero8
+        kept_sum = jnp.zeros((8, 128), F32)
+        for r in pieces:
+            kept = cs[slot, 2, r, :]
+            kept_sum += fold(kept)
+            bo = across(kept, full) * (ms[slot, r, :].astype(F32) + (ob[r, :] + chan_bias))
+            pool += fold(bo)
+            store_rows(bos, slot, r, bo)
+            sg = sb[r, :]
+            unit = vs[slot, r, :].astype(F32)
+            gain += fold(sg * unit)
+            shift += fold(sg)
+            e = sg * norm_ref[1:2, :]
+            m = jnp.sum(e, 1, keepdims=True) * (1.0 / full)
+            n = jnp.sum(e * unit, 1, keepdims=True) * (1.0 / full)
+            y_rows = pl.ds(pl.multiple_of(i * tp + r.start, 16), ROWS)
+            v = yt[y_rows, :].astype(F32) + across(cs[slot, 1, r, :], full) * (e - m - unit * n)
+            mg[r, :] = v
+            ol[r, :] = v.astype(BF16)
+        acc_norm[1] += gain
+        acc_norm[3] += shift
+        count = jnp.sum(kept_sum, 0, keepdims=True)
+        pool_a[pl.ds(my_first + i, 1), :] = jnp.sum(pool, 0, keepdims=True) / across(count, full)
+        for c in lane_pieces(full):
+            hg = nn(tw_ref[1], ol[:, c])
+            for a in range(0, ds, 32):
+                r = slice(a, a + 32)
+                tg[r, c] = (hg[r] * ls[slot, r, c].astype(F32)).astype(BF16)
+            fg[:, c] = nn(twt_ref[0], tg[:, c])
+        acc_tok[0] += nt(tg[...], fs[slot])
+        acc_tok[1] += nt(hs[slot], ol[...])
+        row_p[...] += nt(jnp.ones((16, full), BF16), ol[...])
+        gain, shift = zero8, zero8
+        for r in pieces:
+            g = fg[r, :]
+            unit = us[slot, r, :].astype(F32)
+            gain += fold(g * unit)
+            shift += fold(g)
+            e = g * norm_ref[0:1, :]
+            m = jnp.sum(e, 1, keepdims=True) * (1.0 / full)
+            n = jnp.sum(e * unit, 1, keepdims=True) * (1.0 / full)
+            v = mg[r, :] + across(cs[slot, 0, r, :], full) * (e - m - unit * n)
+            store_rows(gis, slot, r, v)
+        acc_norm[0] += gain
+        acc_norm[2] += shift
         for c in out_copies(i, slot):
             c.start()
         return carry
 
     lax.fori_loop(0, ni, image_step, 0)
 
-    lane = lax.broadcasted_iota(jnp.int32, (2 * unit_d, 128), 1)
     h_0 = jnp.where(core == 0, row_h[0:1, :half], row_h[0:1, half:])
     h_1 = jnp.where(core == 0, row_h[0:1, half:], row_h[0:1, :half])
+    norms = jnp.concatenate([jnp.sum(acc_norm[n], 0, keepdims=True) for n in range(4)], 0)
+    norms = jnp.concatenate([norms, jnp.zeros((4, full), F32)], 0)
     per_h = half // n_dp
     per_c = ch // n_dp
     tail = msgs.shape[1] - 2 * unit_d
-    b2_row = jnp.sum(row_p[...], 0, keepdims=True)
 
     def cut(v, start, size):
         n = v.shape[1]
-        v = jnp.broadcast_to(v, (8, n))
-        v = pltpu.roll(v, (n - start) % n, 1)[0:1, :lanes]
-        return jnp.where(lax.broadcasted_iota(jnp.int32, (1, lanes), 1) < size, v, 0.0)
+        a = min(start // 128 * 128, n - 256)
+        v = v[:, a : a + 256]
+        if v.shape[0] == 1:
+            v = jnp.broadcast_to(v, (8, 256))
+        if start > a:
+            v = pltpu.roll(v, 256 - (start - a), 1)
+        lane = lax.broadcasted_iota(jnp.int32, v.shape, 1)
+        return jnp.where(lane < size, v, 0.0)
 
     for d in range(n_dp):
         top = jnp.concatenate(
@@ -844,21 +850,16 @@
             ],
             axis=0,
         )
-        rows = slice(rows_own * d, rows_own * (d + 1))
-        right = top[:, 128:]
-        for n in range(4):
-            s = jnp.sum(acc_col[n, rows, :], 1, keepdims=True)
-            right = jnp.where(lane == PRM_LANE - 128 + n, s, right)
-        msgs[d, : 2 * unit_d, :128] = top[:, :128].astype(BF16)
-        msgs[d, : 2 * unit_d, 128:] = right.astype(BF16)
+        msgs[d, : 2 * unit_d, :] = top.astype(BF16)
         extra = jnp.concatenate(
             [
-                b2_row,
-                cut(h_0, per_h * d, per_h),
-                cut(h_1, per_h * d, per_h),
-                cut(row_c[0:1, :], per_c * d, per_c),
-                cut(row_c[0:1, :], ch + per_c * d, per_c),
-                jnp.zeros((tail - 5, lanes), F32),
+                row_p[0:1, :],
+                cut(h_0, per_h * d, per_h)[0:1],
+                cut(h_1, per_h * d, per_h)[0:1],
+                cut(row_c[0:1, :], per_c * d, per_c)[0:1],
+                cut(row_c[0:1, :], ch + per_c * d, per_c)[0:1],
+                jnp.zeros((3, kp), F32),
+                cut(norms, rows_own * d, rows_own),
             ],
             axis=0,
         )
@@ -880,7 +881,7 @@
 
     lax.fori_loop(1, n_dp, send, 0)
     pool_copy = remote(
-        pool_a.at[pl.ds(pl.multiple_of((1 - core) * ch, 128), ch)], pool_r, fin_s.at[0], fin_r.at[0], other
+        pool_a.at[:, pl.ds(pl.multiple_of((1 - core) * ch, 128), ch)], pool_r, fin_s.at[0], fin_r.at[0], other
     )
     pool_copy.start()
     sq_copy = remote(sq_a, sq_r, fin_s.at[1], fin_r.at[1], other)
@@ -915,24 +916,23 @@
             c.wait_recv()
     pool_copy.wait()
     sq_copy.wait()
-    pool_o[...] = pool_a[pl.ds(pl.multiple_of(core * ch, 128), ch), :] + pool_r[...]
+    pool_o[...] = pool_a[:, pl.ds(pl.multiple_of(core * ch, 128), ch)] + pool_r[...]
     sq_o[...] = sq_a[...] + sq_r[...]
     red_copy.wait()
     red_o[...] = red_a[...] + red_r[...]
 
 
-def back(n_dp, grid3, st, yt, w1, w1p, w2, w2p, b1, b1p, xp, f, hid, slope, mix, yp, stat, prm, colf, tw1, tw2, pat):
-    ni, full, lanes = xp.shape
+def back(n_dp, grid3, st, yt, w1, w1p, w2, w2p, u0, f, hid, slope, mix, u1, col, norm, pack, tw, twt, pat):
+    ni, tp, full = u0.shape
     ch = full // 2
     half = w1.shape[1]
     toks = st.shape[0]
-    tp = toks // ni
-    ds = tw1.shape[0]
+    ds, kp = tw.shape[1:]
     unit_d = ds // n_dp
     toks_pad = up(toks, 256)
     nz, ny, nx = grid3
     rows_own = full // n_dp
-    n_msg = up(2 * unit_d + 5, 16)
+    n_msg = 2 * unit_d + 16
     sds = jax.ShapeDtypeStruct
     vm = pltpu.VMEM
     dma = pltpu.SemaphoreType.DMA
@@ -940,14 +940,14 @@
     return pl.pallas_call(
         functools.partial(back_kernel, (n_dp, ni, ch, pat, tp, unit_d, nz, ny, nx)),
         out_shape=[
-            sds((2 * ni, ch, pat), BF16),
-            sds((2 * ni, ch, pat), BF16),
-            sds((ch, 128), F32),
+            sds((2 * ni, pat, ch), BF16),
+            sds((2 * ni, pat, ch), BF16),
+            sds((up(2 * ni, 8), ch), F32),
             sds((8, 128), F32),
-            sds((n_msg, lanes), F32),
+            sds((n_msg, kp), F32),
             sds((2, rows_own, half), F32),
         ],
-        in_specs=[ANY] * 6 + [VM, VM] + [ANY] * 6 + [VM] * 5,
+        in_specs=[ANY] * 13 + [VM] * 4,
         out_specs=[ANY, ANY, VM, VM, VM, VM],
         scratch_shapes=[
             vm((toks_pad, full), BF16),
@@ -956,6 +956,7 @@
             vm((full, toks_pad), BF16),
             vm((2, full, half), BF16),
             vm((2, half, full), BF16),
+            vm((8, 2 * half), F32),
             vm((toks_pad, 2 * half), BF16),
             vm((toks_pad, 2 * half), BF16),
             vm((2, 2) + part, BF16),
@@ -966,34 +967,36 @@
             vm((2, 2, nz, rows_own, BLK), BF16),
             vm((2, nz, 2, rows_own, BLK), BF16),
             vm((2, nz - 1, 2, rows_own, BLK), BF16),
-            vm((2, full, lanes), BF16),
-            vm((2, full, lanes), BF16),
-            vm((2, full, ds), BF16),
-            vm((2, full, ds), BF16),
-            vm((2, full, lanes), F32),
-            vm((2, full, lanes), BF16),
-            vm((2, full, pat), BF16),
-            vm((2, full, pat), BF16),
-            vm((256, full), BF16),
-            vm((256, full), BF16),
-            vm((full, lanes), BF16),
-            vm((full, ds), BF16),
-            vm((5, full, 128), F32),
-            vm((4, full, 128), F32),
-            vm((2, ds, lanes), F32),
+            vm((2, tp, full), BF16),
+            vm((2, kp, full), BF16),
+            vm((2, ds, full), BF16),
+            vm((2, ds, full), BF16),
+            vm((2, tp, full), BF16),
+            vm((2, tp, full), BF16),
+            vm((2, 3, tp, 128), F32),
+            vm((2, pat, full), BF16),
+            vm((2, pat, full), BF16),
+            vm((tp, full), F32),
+            vm((tp, full), F32),
+            vm((tp, full), F32),
+            vm((kp, full), BF16),
+            vm((ds, full), BF16),
+            vm((tp, full), F32),
+            vm((4, 8, full), F32),
+            vm((2, ds, kp), F32),
             vm((8, 2 * half), F32),
             vm((8, full), F32),
-            vm((8, lanes), F32),
-            vm((full, 128), F32),
-            vm((ch, 128), F32),
+            vm((16, kp), F32),
+            vm((up(2 * ni, 8), full), F32),
+            vm((up(2 * ni, 8), ch), F32),
             vm((8, 128), F32),
             vm((8, 128), F32),
-            vm((n_dp, n_msg, lanes), BF16),
-            vm((n_dp, n_msg, lanes), BF16),
-            vm((n_msg, lanes), F32),
-            vm((n_msg, lanes), F32),
+            vm((n_dp, n_msg, kp), BF16),
+            vm((n_dp, n_msg, kp), BF16),
+            vm((n_msg, kp), F32),
+            vm((n_msg, kp), F32),
             dma((6,)),
-            dma((2, 6)),
+            dma((2, 7)),
             dma((2,)),
             dma((2,)),
             dma((2, 2)),
@@ -1014,7 +1017,7 @@
             collective_id=1, has_side_effects=True, vmem_limit_bytes=VMEM_BYTES
         ),
         name="back",
-    )(st, yt, w1, w1p, w2, w2p, b1, b1p, xp, f, hid, slope, mix, yp, stat, prm, colf, tw1, tw2)
+    )(st, yt, w1, w1p, w2, w2p, u0, f, hid, slope, mix, u1, col, norm, pack, tw, twt)
 
 
 def finish_kernel(
@@ -1048,58 +1051,61 @@
     @pl.when(pl.program_id(0) == 0)
     def _():
         images = pool_o.shape[0]
-        pool_o[...] = jnp.transpose(pool_ref[...])[:images]
+        pool_o[...] = pool_ref[:images, :]
         sq_o[...] = sq_ref[0:1, :images]
         red = red_ref[...]
-        flat = jnp.transpose(red[: 2 * unit_d, 128:])
-        at = PRM_LANE - 128
-        gain_o[...] = flat[at : at + 2]
-        shift_o[...] = flat[at + 2 : at + 4]
-        first = jnp.transpose(red[:unit_d, :])
-        tw1_o[...] = first[:pat]
-        tb1_o[...] = first[pat : pat + 1]
-        tw2_o[...] = red[unit_d : 2 * unit_d, :pat]
         n = 2 * unit_d
+        tw1_o[...] = red[:unit_d, :pat]
+        tw2_o[...] = red[unit_d:n, :pat]
+        gain_o[...] = red[n + 8 : n + 10, :n]
+        shift_o[...] = red[n + 10 : n + 12, :n]
+        tb1_o[...] = jnp.transpose(red[: up(unit_d, 8), 128:])[pat - 128 : pat - 127, :unit_d]
         tb2_o[...] = red[n : n + 1, :pat]
         w1_o[...] = gw_ref[0]
-        w2_o[...] = jnp.transpose(gw_ref[1])
+        w2_o[...] = gw_ref[1]
         b1_o[...] = jnp.where(core == 0, red[n + 1 : n + 2, :per_h], red[n + 2 : n + 3, :per_h])
         b2_o[...] = jnp.where(core == 0, red[n + 3 : n + 4, :per_c], red[n + 4 : n + 5, :per_c])
 
 
 def finish(bo, gi, pool, sq, red, gw, unit_d, per_h, per_c):
-    images, ch, pat = bo.shape
+    images, pat, ch = bo.shape
     ds = unit_d
     sds = jax.ShapeDtypeStruct
     once = lambda s: pl.BlockSpec(s, lambda i: (0,) * len(s))
-    per = pl.BlockSpec((1, ch, pat), lambda i: (i, 0, 0))
+    steps = 4 if images % 4 == 0 else images
+    per = pl.BlockSpec((images // steps, pat, ch), lambda i: (i, 0, 0))
     rows_own, half = gw.shape[1:]
     outs = [
-        (images, ch, pat),
+        (images, pat, ch),
         (images, ch),
-        (images, ch, pat),
+        (images, pat, ch),
         (2, rows_own),
         (2, rows_own),
-        (pat, ds),
+        (ds, pat),
         (1, ds),
         (ds, pat),
         (1, pat),
         (rows_own, half),
         (1, per_h),
-        (half, rows_own),
+        (rows_own, half),
         (1, per_c),
         (1, images),
     ]
     res = pl.pallas_call(
         functools.partial(finish_kernel, (pat, unit_d, per_h, per_c)),
-        grid=(images,),
+        grid=(steps,),
         out_shape=[sds(s, F32) for s in outs],
         in_specs=[per, per] + [once(a.shape) for a in (pool, sq, red, gw)],
         out_specs=[per if len(s) == 3 else once(s) for s in outs],
         compiler_params=pltpu.CompilerParams(vmem_limit_bytes=VMEM_BYTES),
         name="finish",
     )(bo, gi, pool, sq, red, gw)
-    return tuple(r.reshape(-1) if r.shape[0] == 1 else r for r in res)
+    res = [r.reshape(-1) if r.shape[0] == 1 else r for r in res]
+    for n in (0, 2):
+        res[n] = jnp.swapaxes(res[n], 1, 2)
+    for n in (5, 11):
+        res[n] = res[n].T
+    return tuple(res)
 
 
 def fused_body(
@@ -1123,23 +1129,26 @@
     images, ch, pat = mixer_input.shape
     unit_d = token_b1.shape[0]
     half = chan_b1.shape[0]
-    lanes = pad_lanes(pat)
-    left = jnp.concatenate([token_w1.T, token_w2], 0)
-    bias = jnp.pad(token_b1[:, None], ((0, unit_d), (0, PRM_LANE - pat - 1)))
-    norms = jnp.concatenate([ln_gain.T, ln_shift.T], 1)
-    msg = jnp.concatenate(
-        [left, bias, jnp.pad(norms, ((0, 0), (0, lanes - PRM_LANE - 4)))], 1
-    )
-    col = jnp.concatenate([grad_pooled.T, chan_b2.astype(F32)[:, None]], 1)
-    col = jnp.pad(col, ((0, 0), (0, 128 - col.shape[1])))
-    b1 = jnp.broadcast_to(chan_b1.astype(F32)[None, :], (8, half))
-    tb2 = jnp.broadcast_to(jnp.pad(token_b2.astype(F32), (0, lanes - pat))[None, :], (8, lanes))
-    st, yt, xp, f, hid, slope, mix, yp, stat, prm, colf, tw1, tw2, w1p, w2p, b1p = front(
-        n_dp, mixer_input, grad_out, col, chan_w1, chan_w2, b1, msg, keep_mask, tb2
+    st, yt, u0, f, hid, slope, mix, u1, col, norm, pack, tw, twt, w1p, w2p = front(
+        n_dp,
+        jnp.swapaxes(mixer_input, 1, 2),
+        jnp.swapaxes(grad_out, 1, 2),
+        grad_pooled,
+        chan_w1,
+        chan_w2,
+        chan_b1.reshape(1, -1),
+        chan_b2.reshape(1, -1),
+        ln_gain,
+        ln_shift,
+        token_w1.T,
+        token_b1.reshape(1, -1),
+        token_w2,
+        token_b2.reshape(1, -1),
+        keep_mask,
     )
     bo, gi, pool, sq, red, gw = back(
-        n_dp, grid3, st, yt, chan_w1, w1p, chan_w2, w2p, b1, b1p, xp, f, hid, slope, mix, yp,
-        stat, prm, colf, tw1, tw2, pat,
+        n_dp, grid3, st, yt, chan_w1, w1p, chan_w2, w2p, u0, f, hid, slope, mix, u1, col,
+        norm, pack, tw, twt, pat,
     )
     return finish(bo, gi, pool, sq, red, gw, unit_d, half // n_dp, ch // n_dp)
 

time: 167 us -> 132 us (0.79)
  the two profiles are of different devices: /device:TPU:0 before, /device:TPU:31 now
where the time goes in v2:
time: 132 us
  Pallas kernels  127 us (96%)
  local copies, waits for them, and re-layouts  3.75 us (3%)
    pallas_call x1, Pallas kernels, back(): pl.pallas_call(functools.partial(back_kernel, (n_dp, ni, ch, pat, tp, uni...  95.4 us
    pallas_call x1, Pallas kernels, front(): pl.pallas_call(functools.partial(front_kernel, (n_dp, ni, ch, pat, tp, un...  25.9 us
    pallas_call x1, Pallas kernels, finish(): pl.pallas_call(functools.partial(finish_kernel, (pat, unit_d, per_h, per_...  6.07 us

profile of v2, /device:TPU:31, one launch (start us, length us, event | category | flops | bytes accessed | tf_op | source)
XLA Modules:
  0.0 131.8 jit_solution(13916748582004795512)
XLA Ops:
  0.6 1.2 reshape.58.tb2_ref
  1.9 1.2 reshape.56.cb2_ref
  3.1 1.3 reshape.55.b1_ref
  4.4 25.9 %front.1 = (bf16[1248,768]{1,0:T(8,128)(2,1)}, bf16[1248,768]{1,0:T(8,128)(2,1)}, bf16[6,208,768]{2,1,0:T(8,128)(2,1)}, bf16[6,256,768]{2,1,0:T(8,128)(2,1)}, bf...) custom-call(bf16[12,196,384]{2,1,0:T(8,128)(2,1)} %bitcast.13, ...), custom_call_target="tpu_custom_call" | custom-call | tf_op jit(solution)/shard_map/front/pallas_call | solution.py:355
  30.3 95.4 %back.1 = (bf16[12,196,384]{2,1,0:T(8,128)(2,1)}, bf16[12,196,384]{2,1,0:T(8,128)(2,1)}, f32[16,384]{1,0:T(8,128)}, f32[8,128]{1,0:T(8,128)}, f32[64,256]{1,0:T(8,128)}, /*index=5*/f32[2,48,1536]{2,1,0:T(8,128)}) custom-call(bf16[1248,768]{1,0:T(8,128)(2,1)} %get-tuple-element.49.st_hbm, bf16[1248,768]{1,0:T(8,128)(2,1)} %get-tuple-element.50.yt_hbm, ...), custom_call_target="tpu_custom_call" | custom-call | tf_op jit(solution)/shard_map/back/pallas_call | solution.py:940
  125.7 6.1 %finish.1 = (f32[12,196,384]{2,1,0:T(8,128)}, f32[12,384]{1,0:T(8,128)}, f32[12,196,384]{2,1,0:T(8,128)}, f32[2,48]{1,0:T(2,128)}, f32[2,48]{1,0:T(2,128)}, /*in...) custom-call(bf16[12,196,384]{2,1,0:T(8,128)(2,1)} %get-tuple-element, ...), custom_call_target="tpu_custom_call" | custom-call | tf_op jit(solution)/shard_map/finish/pallas_call | solution.py:1094

commit v3 on v2

v3 whole, which is shorter than its diff:
```python
import functools
import math

import jax
import jax.numpy as jnp
from jax import lax
from jax.experimental import pallas as pl
from jax.experimental.pallas import tpu as pltpu
from jax.sharding import PartitionSpec as P

MESH = pl.DeviceIdType.MESH
EPS = 1e-05
F32 = jnp.float32
BF16 = jnp.bfloat16
VM = pl.BlockSpec(memory_space=pltpu.VMEM)
ANY = pl.BlockSpec(memory_space=pl.ANY)
BLK = 256
VMEM_BYTES = 63 * 2**20


def up(n, m):
    return -(-n // m) * m


def nn(a, b):
    return lax.dot_general(a, b, (((1,), (0,)), ((), ())), preferred_element_type=F32)


def nt(a, b):
    return lax.dot_general(a, b, (((1,), (1,)), ((), ())), preferred_element_type=F32)


def tn(a, b):
    return lax.dot_general(a, b, (((0,), (0,)), ((), ())), preferred_element_type=F32)


def eye(rows, cols):
    r = lax.broadcasted_iota(jnp.int32, (rows, cols), 0)
    c = lax.broadcasted_iota(jnp.int32, (rows, cols), 1)
    return (r == c).astype(F32).astype(BF16)


def gelu_parts(v):
    cdf = 0.5 + 0.5 * lax.erf(v * math.sqrt(0.5))
    return cdf, jnp.exp(-0.5 * (v * v)) * (1.0 / math.sqrt(2.0 * math.pi))


def fold(v):
    return jnp.sum(v.reshape(v.shape[0] // 8, 8, v.shape[1]), 0)


def where_am_i():
    return lax.axis_index("dp"), lax.axis_index("tensor")


def greet_all(dp_size, dp, core):
    barrier = pltpu.get_barrier_semaphore()

    def one(n, c):
        pl.semaphore_signal(
            barrier, inc=1, device_id=(lax.rem(dp + n, dp_size), core), device_id_type=MESH
        )
        return c

    lax.fori_loop(1, dp_size, one, 0)
    pl.semaphore_signal(barrier, inc=1, device_id=(dp, 1 - core), device_id_type=MESH)
    pl.semaphore_wait(barrier, dp_size)


def remote(src, dst, send, recv, device):
    return pltpu.make_async_remote_copy(
        src_ref=src,
        dst_ref=dst,
        send_sem=send,
        recv_sem=recv,
        device_id=device,
        device_id_type=MESH,
    )


ROWS = 16


def row_pieces(pat):
    return [slice(r, min(r + ROWS, pat)) for r in range(0, pat, ROWS)]


def lane_pieces(full):
    return [slice(c, c + 256) for c in range(0, full, 256)]


def across(v, full):
    return jnp.concatenate([v] * (full // 128), axis=1)


def centre(v):
    n = v.shape[1]
    d = v - jnp.sum(v, 1, keepdims=True) * (1.0 / n)
    r = lax.rsqrt(jnp.sum(d * d, 1, keepdims=True) * (1.0 / n) + EPS)
    return d * r, r


def mixer_kernel(
    dims,
    x_hbm,
    go_hbm,
    gp_ref,
    w1_hbm,
    w2_hbm,
    b1_ref,
    cb2_ref,
    gain_ref,
    shift_ref,
    tw1_ref,
    tb1_ref,
    tw2_ref,
    tb2_ref,
    keep_ref,
    bo_hbm,
    gi_hbm,
    u0_hbm,
    f_hbm,
    hid_hbm,
    slope_hbm,
    mix_hbm,
    u1_hbm,
    pool_o,
    sq_o,
    red_o,
    gw_o,
    xf,
    gof,
    msg,
    square,
    pack,
    packf,
    tok,
    tmp_w,
    prm,
    keep_t,
    tb2_w,
    norm,
    tw,
    twt,
    st,
    yt,
    w1s,
    w2s,
    bias,
    gh,
    ph,
    gs,
    pb,
    ra,
    r1,
    b2,
    r2,
    b3,
    r3,
    us,
    fs,
    hs,
    ls,
    ms,
    vs,
    cs,
    bos,
    gis,
    ob,
    mg,
    ol,
    tg,
    fg,
    acc_norm,
    acc_tok,
    row_h,
    row_c,
    row_p,
    pool_a,
    pool_r,
    sq_a,
    sq_r,
    msgs,
    msgr,
    red_a,
    red_r,
    tg_s,
    tg_r,
    pair_send,
    pair_recv,
    loc_sem,
    spill,
    in_sem,
    sa,
    rsa,
    s1,
    rs1,
    s2,
    rs2,
    s3,
    rs3,
    out_s,
    out_r,
    out_l,
    tok_s,
    tok_r,
    fin_s,
    fin_r,
):
    n_dp, ni, ch, pat, tp, unit_d, nz, ny, nx = dims
    dp, core = where_am_i()
    x = lax.rem(dp, nx)
    y = lax.rem(dp // nx, ny)
    z = dp // (nx * ny)
    other = (dp, 1 - core)
    x_dev = ((z * ny + y) * nx + (1 - x), core)
    y_dev = ((z * ny + (1 - y)) * nx + x, core)
    full = 2 * ch
    rows_own = full // n_dp
    half = w1s.shape[2]
    n_blk = half // BLK
    toks = ni * tp
    toks_pad = gh.shape[0]
    kp = fs.shape[1]
    my_first = core * ni
    ds = tw.shape[1]
    images = 2 * ni
    here = pl.ds(pl.multiple_of(core * ch, 128), ch)
    there = pl.ds(pl.multiple_of((1 - core) * ch, 128), ch)
    bias_rows = half // ch
    pieces = [slice(r, r + ROWS) for r in range(0, tp, ROWS)]

    ours = pl.ds(my_first, ni)
    theirs = pl.ds((1 - core) * ni, ni)
    pair_copies = [
        remote(a, b, pair_send.at[n], pair_recv.at[n], other)
        for n, (a, b) in enumerate(
            (
                (pack, packf.at[:, here]),
                (x_hbm.at[theirs], xf.at[:, :, here]),
                (go_hbm.at[theirs], gof.at[:, :, here]),
                (w1_hbm, w1s.at[1]),
                (w2_hbm, w2s.at[1]),
            )
        )
    ]
    local_copies = [
        pltpu.make_async_copy(a, b, loc_sem.at[n])
        for n, (a, b) in enumerate(
            (
                (x_hbm.at[ours], xf.at[:, :, here]),
                (go_hbm.at[ours], gof.at[:, :, here]),
                (w1_hbm, w1s.at[0]),
                (w2_hbm, w2s.at[0]),
            )
        )
    ]

    def weights_copy(n):
        to = lax.rem(dp + n, n_dp)
        return remote(msg, tok.at[dp], tg_s.at[n], tg_r.at[dp], (to, core))

    def weights_arrival(n):
        source = lax.rem(dp + n_dp - n, n_dp)
        return remote(msg, tok.at[source], tg_s.at[n], tg_r.at[source], (source, core))

    for c in local_copies:
        c.start()
    square[...] = jnp.zeros_like(square)
    at = pat - 128
    square[at : at + 1, :unit_d] = tb1_ref[...].astype(F32)
    square[at + 4 : at + 6, :rows_own] = gain_ref[...].astype(F32)
    square[at + 6 : at + 8, :rows_own] = shift_ref[...].astype(F32)
    columns = jnp.transpose(square[...])[:rows_own]
    tmp_w[0, :rows_own, :] = jnp.zeros((rows_own, kp), F32)
    tmp_w[0, :unit_d, :pat] = tw1_ref[...].astype(F32)
    tmp_w[0, unit_d:rows_own, :pat] = tw2_ref[...].astype(F32)
    msg[:, :128] = tmp_w[0, :rows_own, :128].astype(BF16)
    msg[:, 128:] = (tmp_w[0, :rows_own, 128:] + columns).astype(BF16)
    pack[...] = jnp.zeros_like(pack)
    pack[:images, :] = gp_ref[...]
    pack[images : images + 1, :] = cb2_ref[...].astype(F32)
    for n in range(bias_rows):
        pack[images + 1 + n : images + 2 + n, :] = b1_ref[:, n * ch : (n + 1) * ch].astype(F32)
    greet_all(n_dp, dp, core)

    def send(n, c):
        weights_copy(n).start()
        return c

    lax.fori_loop(1, n_dp, send, 0)
    for c in pair_copies:
        c.start()

    tok[dp] = msg[...]
    packf[:, here] = pack[...]
    keep_t[...] = jnp.zeros_like(keep_t)
    keep_t[:images, :pat] = keep_ref[...].astype(F32)
    keep_t[images : images + 1, :pat] = tb2_ref[...].astype(F32)
    turned = jnp.transpose(keep_t[...])
    keep_t[...] = turned
    tb2_w[...] = jnp.broadcast_to(turned[:tp, images : images + 1], (tp, 128))
    zero_rows = jnp.zeros((toks_pad - toks, gh.shape[1]), BF16)
    gh[toks:, :] = zero_rows
    ph[toks:, :] = zero_rows
    st[toks:, :] = zero_rows[:, :full]
    yt[toks:, :] = zero_rows[:, :full]
    for ref in (row_h, row_c, row_p, acc_norm, acc_tok, pool_a, sq_a, ol):
        ref[...] = jnp.zeros_like(ref)
    partial = row_pieces(pat)
    last = slice(pat // ROWS * ROWS, tp)
    blank = jnp.zeros((last.stop - last.start, full), BF16)
    for n in range(2):
        us[n, last, :] = blank
        vs[n, last, :] = blank
        ms[n, last, :] = blank
        fs[n, last.start :, :] = jnp.zeros((kp - last.start, full), BF16)
        fs[n, pat : pat + 1, :] = jnp.ones((1, full), BF16)
    for c in local_copies[:2]:
        c.wait()
    for c in pair_copies[:3]:
        c.wait_recv()

    def token_rows(i, r):
        return pl.ds(pl.multiple_of(i * tp + r.start, 16), r.stop - r.start)

    def early_step(i, carry):
        number = my_first + i
        count = jnp.sum(keep_ref[pl.ds(number, 1), :].astype(F32), 1, keepdims=True)
        g = packf[pl.ds(number, 1), :] / count
        rows = token_rows(i, last)
        st[rows, :] = blank
        yt[rows, :] = blank
        cs[i, :, last, :] = jnp.zeros((3, tp - last.start, 128), F32)
        for r in partial:
            size = r.stop - r.start
            rows = token_rows(i, r)
            unit, rstd = centre(xf[i, r, :].astype(F32))
            st[rows, :] = unit.astype(BF16)
            cs[i, 0, r, :] = jnp.broadcast_to(rstd, (size, 128))
            lane = lax.broadcasted_iota(jnp.int32, (size, 128), 1)
            k = jnp.sum(jnp.where(lane == number, keep_t[r, :128], 0.0), 1, keepdims=True)
            yt[rows, :] = (k * (gof[i, r, :].astype(F32) + g)).astype(BF16)
            cs[i, 2, r, :] = jnp.broadcast_to(k, (size, 128))
        return carry

    lax.fori_loop(0, ni, early_step, 0)
    for n in range(bias_rows):
        row = packf[images + 1 + n : images + 2 + n, :]
        swapped = jnp.concatenate([row[:, ch:], row[:, :ch]], axis=1)
        row = jnp.where(core == 0, row, swapped)
        bias[0:1, n * ch : (n + 1) * ch] = row[:, :ch]
        bias[0:1, half + n * ch : half + (n + 1) * ch] = row[:, ch:]

    def arrive_w(n, c):
        weights_arrival(n).wait_recv()
        return c

    lax.fori_loop(1, n_dp, arrive_w, 0)
    lane = lax.broadcasted_iota(jnp.int32, (unit_d, kp), 1)
    for d in range(n_dp):
        block = tok[d].astype(F32)
        tmp_w[0, unit_d * d : unit_d * (d + 1), :] = jnp.where(lane <= pat, block[:unit_d], 0.0)
        tmp_w[1, unit_d * d : unit_d * (d + 1), :] = jnp.where(lane < pat, block[unit_d:], 0.0)
        prm[rows_own * d : rows_own * (d + 1), :] = tok[d, :, 128:]
    r = lax.broadcasted_iota(jnp.int32, (16, 128), 0)
    c = lax.broadcasted_iota(jnp.int32, (16, 128), 1)
    norm[...] = nt(((c - (at + 4) == r) & (r < 4)).astype(F32).astype(BF16), prm[...])
    ident = eye(kp, kp)
    for n in range(2):
        w = tmp_w[n].astype(BF16)
        tw[n] = w
        t = nt(ident, w)
        r = lax.broadcasted_iota(jnp.int32, t.shape, 0)
        twt[n] = jnp.where(r < pat, t, 0.0)[:tp].astype(BF16)

    def saved(i):
        slot = lax.rem(i, 2)
        pairs = (
            (us, u0_hbm),
            (fs, f_hbm),
            (hs, hid_hbm),
            (ls, slope_hbm),
            (vs, u1_hbm),
            (ms, mix_hbm),
        )
        return [
            pltpu.make_async_copy(a.at[slot], b.at[i], spill.at[slot, n])
            for n, (a, b) in enumerate(pairs)
        ]

    def token_step(i, carry):
        slot = lax.rem(i, 2)

        @pl.when(i >= 2)
        def _():
            for c in saved(i - 2):
                c.wait()

        for r in partial:
            unit = st[token_rows(i, r), :]
            us[slot, r, :] = unit
            f = unit.astype(F32) * norm[0:1, :] + norm[2:3, :]
            fs[slot, r, :] = f.astype(BF16)
        for c in lane_pieces(full):
            pre = nn(tw[0], fs[slot, :, c])
            for a in range(0, ds, 32):
                v = pre[a : a + 32]
                cdf, pdf = gelu_parts(v)
                hs[slot, a : a + 32, c] = (v * cdf).astype(BF16)
                ls[slot, a : a + 32, c] = (cdf + v * pdf).astype(BF16)
            ob[:, c] = nn(twt[1], hs[slot, :, c])
        for r in partial:
            v = xf[i, r, :].astype(F32) + (ob[r, :] + across(tb2_w[r, :], full))
            ms[slot, r, :] = v.astype(BF16)
            unit, rstd = centre(v)
            vs[slot, r, :] = unit.astype(BF16)
            st[token_rows(i, r), :] = (unit * norm[1:2, :] + norm[3:4, :]).astype(BF16)
            cs[i, 1, r, :] = jnp.broadcast_to(rstd, (r.stop - r.start, 128))
        for c in saved(i):
            c.start()
        return carry

    lax.fori_loop(0, ni, token_step, 0)
    for i in (ni - 2, ni - 1):
        for c in saved(i):
            c.wait()
    for c in local_copies[2:]:
        c.wait()
    for c in pair_copies[3:]:
        c.wait_recv()

    def image_loads(i, slot):
        pairs = ((u0_hbm, us), (f_hbm, fs), (hid_hbm, hs), (slope_hbm, ls), (u1_hbm, vs))
        return [
            pltpu.make_async_copy(a.at[i], b.at[slot], in_sem.at[slot, n])
            for n, (a, b) in enumerate(pairs)
        ]

    def late_loads(i, slot):
        return [pltpu.make_async_copy(mix_hbm.at[i], ms.at[slot], in_sem.at[slot, 5])]

    for c in image_loads(0, 0):
        c.start()
    for c in late_loads(0, 0):
        c.start()

    def pair_copy(slot):
        return remote(pb, ra.at[slot], sa.at[0], rsa.at[slot], other)

    def first_copies(j):
        slot = lax.rem(j, 3)
        return (
            remote(
                gs.at[slot, 0, :, :, 1 - x], r1.at[j, 0], s1.at[slot, 0], rs1.at[j, 0], x_dev
            ),
            remote(gs.at[slot, 1, :, 1 - y], r1.at[j, 1], s1.at[slot, 1], rs1.at[j, 1], y_dev),
        )

    def second_copies(j):
        slot = lax.rem(j, 3)
        return (
            remote(b2.at[slot, 0, :, 1 - y], r2.at[j, 0], s2.at[slot, 0], rs2.at[j, 0], y_dev),
            remote(b2.at[slot, 1, :, 1 - x], r2.at[j, 1], s2.at[slot, 1], rs2.at[j, 1], x_dev),
        )

    def third_copies(j):
        slot = lax.rem(j, 2)
        out = []
        for n in range(1, nz):
            to = lax.rem(z + n, nz)
            out.append(
                remote(
                    b3.at[slot, to],
                    r3.at[j, n - 1],
                    s3.at[slot, n - 1],
                    rs3.at[j, n - 1],
                    ((to * ny + y) * nx + x, core),
                )
            )
        return out

    def finish_third(j):
        slot = lax.rem(j, 2)
        for c in third_copies(j):
            c.wait()
        at = pl.ds(pl.multiple_of(j * BLK, BLK), BLK)
        for m in range(2):
            v = b3[slot, z, m].astype(F32)
            for n in range(nz - 1):
                v = v + r3[j, n, m].astype(F32)
            gw_o[m, :, at] = v

    def finish_second(j):
        slot, into = lax.rem(j, 3), lax.rem(j, 2)
        for c in second_copies(j):
            c.wait()
        for m, mine in ((0, y), (1, x)):
            for k in range(nz):
                v = b2[slot, m, k, mine].astype(F32) + r2[j, m, k].astype(F32)
                b3[into, k, m] = v.astype(BF16)
        for c in third_copies(j):
            c.start()

    def finish_first(j):
        slot = lax.rem(j, 3)
        for c in first_copies(j):
            c.wait()
        for k in range(nz):
            for n in range(2):
                v = gs[slot, 0, k, n, x].astype(F32) + r1[j, 0, k, n].astype(F32)
                b2[slot, 0, k, n] = v.astype(BF16)
                v = gs[slot, 1, k, y, n].astype(F32) + r1[j, 1, k, n].astype(F32)
                b2[slot, 1, k, n] = v.astype(BF16)
        for c in second_copies(j):
            c.start()

    def hidden_block(side, j):
        at = pl.ds(pl.multiple_of(j * BLK, BLK), BLK)
        col = pl.ds(pl.multiple_of(side * half + j * BLK, BLK), BLK)
        w1 = w1s[side, :, at]
        w2 = w2s[side, at, :]
        b_row = bias[0:1, col]
        for i in range(ni):
            r0 = i * tp
            r = slice(r0, r0 + tp)
            pre = nn(st[r, :], w1)
            up_grad = nt(yt[r, :], w2)
            acc = jnp.zeros((8, BLK), F32)
            for a in range(0, tp, 16):
                v = pre[a : a + 16] + b_row
                cdf, pdf = gelu_parts(v)
                gh[r0 + a : r0 + a + 16, col] = (v * cdf).astype(BF16)
                p = up_grad[a : a + 16] * (cdf + v * pdf)
                ph[r0 + a : r0 + a + 16, col] = p.astype(BF16)
                acc += fold(p)
            row = jnp.sum(acc, 0, keepdims=True)
            row_h[0:1, col] += row
            row_h[1 + i : 2 + i, col] = row
        return tn(st[...], ph[:, col]), tn(yt[...], gh[:, col])

    def rounds(s):
        for lag, work in ((8, finish_third), (6, finish_second), (3, finish_first)):

            @pl.when((s >= lag) & (s < n_blk + lag))
            def _():
                work(s - lag)

    def split(v, k):
        per = full // nz
        return v[k * per : (k + 1) * per].reshape(ny, nx, rows_own, BLK)

    def block_step(j, carry):
        slot = lax.rem(j, 2)
        for m, v in enumerate(hidden_block(1, j)):
            for k in range(nz):
                pb[m, k] = split(v, k).astype(BF16)
        pair_copy(slot).start()
        grads = hidden_block(0, j)
        pair_copy(slot).wait()
        rounds(j)
        for m, v in enumerate(grads):
            for k in range(nz):
                gs[lax.rem(j, 3), m, k] = (split(v, k) + ra[slot, m, k].astype(F32)).astype(BF16)
        for c in first_copies(j):
            c.start()
        return carry

    lax.fori_loop(0, n_blk, block_step, 0)

    def out_copies(n, i):
        src, dst = ((bos, bo_hbm), (gis, gi_hbm))[n]
        slot = lax.rem(i, 2)
        to = dst.at[my_first + i]
        return (
            remote(src.at[slot, :, there], to, out_s.at[slot, n], out_r.at[i, n], other),
            pltpu.make_async_copy(src.at[slot, :, here], to, out_l.at[slot, n]),
        )

    def out_start(n, i):
        for c in out_copies(n, i):
            c.start()

    def out_sent(n, i):
        away, local = out_copies(n, i)
        away.wait_send()
        local.wait()

    def out_arrived(n, i):
        src, dst = ((bos, bo_hbm), (gis, gi_hbm))[n]
        remote(
            src.at[0, :, there],
            dst.at[(1 - core) * ni + i],
            out_s.at[0, n],
            out_r.at[i, n],
            other,
        ).wait_recv()

    def store_rows(ref, slot, r, v):
        stop = min(r.stop, pat)
        ref[slot, r.start : stop, :] = v[: stop - r.start].astype(BF16)

    def backward_step(i, carry):
        slot = lax.rem(i, 2)
        rounds(n_blk + i)
        rows = pl.ds(pl.multiple_of(i * tp, 16), tp)
        ob[...] = nt(ph[rows, :half], w1s[0]) + nt(ph[rows, half:], w1s[1])

        @pl.when(i + 1 < ni)
        def _():
            for c in image_loads(i + 1, 1 - slot):
                c.start()

        for c in image_loads(i, slot):
            c.wait()

        @pl.when(i >= 2)
        def _():
            out_sent(1, i - 2)

        zero8 = jnp.zeros((8, full), F32)
        dy, gain, shift = zero8, zero8, zero8
        for r in pieces:
            sg = ob[r, :]
            unit = vs[slot, r, :].astype(F32)
            gain += fold(sg * unit)
            shift += fold(sg)
            e = sg * norm[1:2, :]
            m = jnp.sum(e, 1, keepdims=True) * (1.0 / full)
            n = jnp.sum(e * unit, 1, keepdims=True) * (1.0 / full)
            y_rows = pl.ds(pl.multiple_of(i * tp + r.start, 16), ROWS)
            v = yt[y_rows, :].astype(F32)
            dy += fold(v)
            v = v + across(cs[i, 1, r, :], full) * (e - m - unit * n)
            mg[r, :] = v
            ol[r, :] = v.astype(BF16)
        dy = jnp.sum(dy, 0, keepdims=True)
        row_c[0:1, :] += dy
        row_c[pl.ds(1 + i, 1), :] = dy
        acc_norm[1] += gain
        acc_norm[3] += shift
        for c in lane_pieces(full):
            hg = nn(tw[1], ol[:, c])
            for a in range(0, ds, 32):
                r = slice(a, a + 32)
                tg[r, c] = (hg[r] * ls[slot, r, c].astype(F32)).astype(BF16)
            fg[:, c] = nn(twt[0], tg[:, c])
        acc_tok[0] += nt(tg[...], fs[slot])
        acc_tok[1] += nt(hs[slot], ol[...])
        row_p[...] += nt(jnp.ones((16, full), BF16), ol[...])
        gain, shift = zero8, zero8
        for r in pieces:
            g = fg[r, :]
            unit = us[slot, r, :].astype(F32)
            gain += fold(g * unit)
            shift += fold(g)
            e = g * norm[0:1, :]
            m = jnp.sum(e, 1, keepdims=True) * (1.0 / full)
            n = jnp.sum(e * unit, 1, keepdims=True) * (1.0 / full)
            v = mg[r, :] + across(cs[i, 0, r, :], full) * (e - m - unit * n)
            store_rows(gis, slot, r, v)
        acc_norm[0] += gain
        acc_norm[2] += shift
        out_start(1, i)
        return carry

    lax.fori_loop(0, ni, backward_step, 0)
    h_0 = jnp.where(core == 0, row_h[0:1, :half], row_h[0:1, half:])
    h_1 = jnp.where(core == 0, row_h[0:1, half:], row_h[0:1, :half])
    norms = jnp.concatenate([jnp.sum(acc_norm[n], 0, keepdims=True) for n in range(4)], 0)
    norms = jnp.concatenate([norms, jnp.zeros((4, full), F32)], 0)
    per_h = half // n_dp
    per_c = ch // n_dp
    tail = msgs.shape[1] - 2 * unit_d

    def cut(v, start, size):
        n = v.shape[1]
        a = min(start // 128 * 128, n - 256)
        v = v[:, a : a + 256]
        if v.shape[0] == 1:
            v = jnp.broadcast_to(v, (8, 256))
        if start > a:
            v = pltpu.roll(v, 256 - (start - a), 1)
        lane = lax.broadcasted_iota(jnp.int32, v.shape, 1)
        return jnp.where(lane < size, v, 0.0)

    for d in range(n_dp):
        top = jnp.concatenate(
            [
                acc_tok[0, unit_d * d : unit_d * (d + 1), :],
                acc_tok[1, unit_d * d : unit_d * (d + 1), :],
            ],
            axis=0,
        )
        msgs[d, : 2 * unit_d, :] = top.astype(BF16)
        extra = jnp.concatenate(
            [
                row_p[0:1, :],
                cut(h_0, per_h * d, per_h)[0:1],
                cut(h_1, per_h * d, per_h)[0:1],
                cut(row_c[0:1, :], per_c * d, per_c)[0:1],
                cut(row_c[0:1, :], ch + per_c * d, per_c)[0:1],
                jnp.zeros((3, kp), F32),
                cut(norms, rows_own * d, rows_own),
            ],
            axis=0,
        )
        msgs[d, 2 * unit_d :, :] = extra.astype(BF16)

    def token_send(n):
        to = lax.rem(dp + n, n_dp)
        return remote(msgs.at[to], msgr.at[dp], tok_s.at[n], tok_r.at[dp], (to, core))

    def token_arrival(n):
        source = lax.rem(dp + n_dp - n, n_dp)
        return remote(
            msgs.at[source], msgr.at[source], tok_s.at[n], tok_r.at[source], (source, core)
        )

    def send(n, c):
        token_send(n).start()
        return c

    lax.fori_loop(1, n_dp, send, 0)
    msgr[dp] = msgs[dp]

    def forward_step(i, carry):
        slot = lax.rem(i, 2)
        rounds(n_blk + ni + i)
        r = pl.ds(pl.multiple_of(i * tp, 16), tp)

        @pl.when(i + 1 < ni)
        def _():
            for c in late_loads(i + 1, 1 - slot):
                c.start()

        ob[...] = nn(gh[r, :half], w2s[0]) + nn(gh[r, half:], w2s[1])
        g = gh[r, :]
        p = ph[r, :]
        s = st[r, :]
        y_all = yt[r, :]
        both = nt(s, s) * nt(p, p) + nt(g, g) * nt(y_all, y_all)
        sq = jnp.sum(jnp.sum(both, 0, keepdims=True), 1, keepdims=True)
        rh = row_h[pl.ds(1 + i, 1), :]
        rc = row_c[pl.ds(1 + i, 1), :]
        sq = sq + jnp.sum(rh * rh, 1, keepdims=True) + jnp.sum(rc * rc, 1, keepdims=True)
        lane = lax.broadcasted_iota(jnp.int32, (1, 128), 1)
        sq_a[0:1, :] += jnp.where(lane == my_first + i, sq, 0.0)
        for c in late_loads(i, slot):
            c.wait()

        @pl.when(i >= 2)
        def _():
            out_sent(0, i - 2)

        chan_bias = packf[images : images + 1, :]
        pool = jnp.zeros((8, full), F32)
        kept_sum = jnp.zeros((8, 128), F32)
        for r in pieces:
            kept = cs[i, 2, r, :]
            kept_sum += fold(kept)
            bo = across(kept, full) * (ms[slot, r, :].astype(F32) + (ob[r, :] + chan_bias))
            pool += fold(bo)
            store_rows(bos, slot, r, bo)
        count = jnp.sum(kept_sum, 0, keepdims=True)
        pool_a[pl.ds(my_first + i, 1), :] = jnp.sum(pool, 0, keepdims=True) / across(count, full)
        out_start(0, i)
        return carry

    lax.fori_loop(0, ni, forward_step, 0)
    pool_copy = remote(pool_a.at[:, there], pool_r, fin_s.at[0], fin_r.at[0], other)
    pool_copy.start()
    sq_copy = remote(sq_a, sq_r, fin_s.at[1], fin_r.at[1], other)
    sq_copy.start()

    def arrive(n, c):
        token_arrival(n).wait_recv()
        return c

    lax.fori_loop(1, n_dp, arrive, 0)
    total = msgr[0].astype(F32)
    for d in range(1, n_dp):
        total = total + msgr[d].astype(F32)
    red_a[...] = total
    red_copy = remote(red_a, red_r, fin_s.at[2], fin_r.at[2], other)
    red_copy.start()

    def sent(n, c):
        token_send(n).wait_send()
        return c

    lax.fori_loop(1, n_dp, sent, 0)

    def sent_w(n, c):
        weights_copy(n).wait_send()
        return c

    lax.fori_loop(1, n_dp, sent_w, 0)
    for c in pair_copies:
        c.wait_send()
    for n in range(2):
        for i in (ni - 2, ni - 1):
            out_sent(n, i)
        for i in range(ni):
            out_arrived(n, i)
    pool_copy.wait()
    sq_copy.wait()
    pool_o[...] = pool_a[:, here] + pool_r[...]
    sq_o[...] = sq_a[...] + sq_r[...]
    red_copy.wait()
    red_o[...] = red_a[...] + red_r[...]


def mixer(n_dp, grid3, x, go, gp, w1, w2, b1, cb2, gain, shift, tw1, tb1, tw2, tb2, keep):
    images, pat, ch = x.shape
    ni = images // 2
    full = 2 * ch
    half = w1.shape[1]
    unit_d = tw1.shape[0]
    ds = unit_d * n_dp
    tp = up(pat, 16)
    kp = up(pat, 256)
    toks_pad = up(ni * tp, 256)
    n_pack = up(images + 1 + half // ch, 8)
    n_img = up(images, 8)
    nz, ny, nx = grid3
    rows_own = full // n_dp
    n_msg = 2 * unit_d + 16
    n_blk = half // BLK
    sds = jax.ShapeDtypeStruct
    vm = pltpu.VMEM
    dma = pltpu.SemaphoreType.DMA
    part = (nz, ny, nx, rows_own, BLK)
    outs = [
        (sds((images, pat, ch), BF16), ANY),
        (sds((images, pat, ch), BF16), ANY),
        (sds((ni, tp, full), BF16), ANY),
        (sds((ni, kp, full), BF16), ANY),
        (sds((ni, ds, full), BF16), ANY),
        (sds((ni, ds, full), BF16), ANY),
        (sds((ni, tp, full), BF16), ANY),
        (sds((ni, tp, full), BF16), ANY),
        (sds((n_img, ch), F32), VM),
        (sds((8, 128), F32), VM),
        (sds((n_msg, kp), F32), VM),
        (sds((2, rows_own, half), F32), VM),
    ]
    res = pl.pallas_call(
        functools.partial(mixer_kernel, (n_dp, ni, ch, pat, tp, unit_d, nz, ny, nx)),
        out_shape=[o[0] for o in outs],
        in_specs=[ANY, ANY, VM, ANY, ANY] + [VM] * 9,
        out_specs=[o[1] for o in outs],
        scratch_shapes=[
            vm((ni, pat, full), BF16),
            vm((ni, pat, full), BF16),
            vm((2 * unit_d, kp), BF16),
            vm((128, 128), F32),
            vm((n_pack, ch), F32),
            vm((n_pack, full), F32),
            vm((n_dp, 2 * unit_d, kp), BF16),
            vm((2, ds, kp), F32),
            vm((full, 128), BF16),
            vm((kp, kp), F32),
            vm((tp, 128), F32),
            vm((16, full), F32),
            vm((2, ds, kp), BF16),
            vm((2, tp, ds), BF16),
            vm((toks_pad, full), BF16),
            vm((toks_pad, full), BF16),
            vm((2, full, half), BF16),
            vm((2, half, full), BF16),
            vm((8, 2 * half), F32),
            vm((toks_pad, 2 * half), BF16),
            vm((toks_pad, 2 * half), BF16),
            vm((3, 2) + part, BF16),
            vm((2,) + part, BF16),
            vm((2, 2) + part, BF16),
            vm((n_blk, 2, nz, 2, rows_own, BLK), BF16),
            vm((3, 2, nz, 2, rows_own, BLK), BF16),
            vm((n_blk, 2, nz, rows_own, BLK), BF16),
            vm((2, nz, 2, rows_own, BLK), BF16),
            vm((n_blk, nz - 1, 2, rows_own, BLK), BF16),
            vm((2, tp, full), BF16),
            vm((2, kp, full), BF16),
            vm((2, ds, full), BF16),
            vm((2, ds, full), BF16),
            vm((2, tp, full), BF16),
            vm((2, tp, full), BF16),
            vm((ni, 3, tp, 128), F32),
            vm((2, pat, full), BF16),
            vm((2, pat, full), BF16),
            vm((tp, full), F32),
            vm((tp, full), F32),
            vm((kp, full), BF16),
            vm((ds, full), BF16),
            vm((tp, full), F32),
            vm((4, 8, full), F32),
            vm((2, ds, kp), F32),
            vm((8, 2 * half), F32),
            vm((8, full), F32),
            vm((16, kp), F32),
            vm((n_img, full), F32),
            vm((n_img, ch), F32),
            vm((8, 128), F32),
            vm((8, 128), F32),
            vm((n_dp, n_msg, kp), BF16),
            vm((n_dp, n_msg, kp), BF16),
            vm((n_msg, kp), F32),
            vm((n_msg, kp), F32),
            dma((n_dp,)),
            dma((n_dp,)),
            dma((5,)),
            dma((5,)),
            dma((4,)),
            dma((2, 6)),
            dma((2, 6)),
            dma((1,)),
            dma((2,)),
            dma((3, 2)),
            dma((n_blk, 2)),
            dma((3, 2)),
            dma((n_blk, 2)),
            dma((2, nz - 1)),
            dma((n_blk, nz - 1)),
            dma((2, 2)),
            dma((ni, 2)),
            dma((2, 2)),
            dma((n_dp,)),
            dma((n_dp,)),
            dma((3,)),
            dma((3,)),
        ],
        compiler_params=pltpu.CompilerParams(
            collective_id=0, has_side_effects=True, vmem_limit_bytes=VMEM_BYTES
        ),
        name="mixer",
    )(x, go, gp, w1, w2, b1, cb2, gain, shift, tw1, tb1, tw2, tb2, keep)
    return res[:2] + res[8:]


def finish_kernel(
    dims,
    bo_ref,
    gi_ref,
    pool_ref,
    sq_ref,
    red_ref,
    gw_ref,
    bo_o,
    pool_o,
    gi_o,
    gain_o,
    shift_o,
    tw1_o,
    tb1_o,
    tw2_o,
    tb2_o,
    w1_o,
    b1_o,
    w2_o,
    b2_o,
    sq_o,
):
    pat, unit_d, per_h, per_c = dims
    _, core = where_am_i()
    bo_o[...] = bo_ref[...].astype(F32)
    gi_o[...] = gi_ref[...].astype(F32)

    @pl.when(pl.program_id(0) == 0)
    def _():
        images = pool_o.shape[0]
        pool_o[...] = pool_ref[:images, :]
        sq_o[...] = sq_ref[0:1, :images]
        red = red_ref[...]
        n = 2 * unit_d
        tw1_o[...] = red[:unit_d, :pat]
        tw2_o[...] = red[unit_d:n, :pat]
        gain_o[...] = red[n + 8 : n + 10, :n]
        shift_o[...] = red[n + 10 : n + 12, :n]
        tb1_o[...] = jnp.transpose(red[: up(unit_d, 8), 128:])[pat - 128 : pat - 127, :unit_d]
        tb2_o[...] = red[n : n + 1, :pat]
        w1_o[...] = gw_ref[0]
        w2_o[...] = gw_ref[1]
        b1_o[...] = jnp.where(core == 0, red[n + 1 : n + 2, :per_h], red[n + 2 : n + 3, :per_h])
        b2_o[...] = jnp.where(core == 0, red[n + 3 : n + 4, :per_c], red[n + 4 : n + 5, :per_c])


def finish(bo, gi, pool, sq, red, gw, unit_d, per_h, per_c):
    images, pat, ch = bo.shape
    ds = unit_d
    sds = jax.ShapeDtypeStruct
    once = lambda s: pl.BlockSpec(s, lambda i: (0,) * len(s))
    steps = 4 if images % 4 == 0 else images
    per = pl.BlockSpec((images // steps, pat, ch), lambda i: (i, 0, 0))
    rows_own, half = gw.shape[1:]
    outs = [
        (images, pat, ch),
        (images, ch),
        (images, pat, ch),
        (2, rows_own),
        (2, rows_own),
        (ds, pat),
        (1, ds),
        (ds, pat),
        (1, pat),
        (rows_own, half),
        (1, per_h),
        (rows_own, half),
        (1, per_c),
        (1, images),
    ]
    res = pl.pallas_call(
        functools.partial(finish_kernel, (pat, unit_d, per_h, per_c)),
        grid=(steps,),
        out_shape=[sds(s, F32) for s in outs],
        in_specs=[per, per] + [once(a.shape) for a in (pool, sq, red, gw)],
        out_specs=[per if len(s) == 3 else once(s) for s in outs],
        compiler_params=pltpu.CompilerParams(vmem_limit_bytes=VMEM_BYTES),
        name="finish",
    )(bo, gi, pool, sq, red, gw)
    res = [r.reshape(-1) if r.shape[0] == 1 else r for r in res]
    for n in (0, 2):
        res[n] = jnp.swapaxes(res[n], 1, 2)
    for n in (5, 11):
        res[n] = res[n].T
    return tuple(res)


def fused_body(
    n_dp,
    grid3,
    mixer_input,
    keep_mask,
    ln_gain,
    ln_shift,
    token_w1,
    token_b1,
    token_w2,
    token_b2,
    chan_w1,
    chan_b1,
    chan_w2,
    chan_b2,
    grad_out,
    grad_pooled,
):
    images, ch, pat = mixer_input.shape
    unit_d = token_b1.shape[0]
    half = chan_b1.shape[0]
    bo, gi, pool, sq, red, gw = mixer(
        n_dp,
        grid3,
        jnp.swapaxes(mixer_input, 1, 2),
        jnp.swapaxes(grad_out, 1, 2),
        grad_pooled,
        chan_w1,
        chan_w2,
        chan_b1.reshape(1, -1),
        chan_b2.reshape(1, -1),
        ln_gain,
        ln_shift,
        token_w1.T,
        token_b1.reshape(1, -1),
        token_w2,
        token_b2.reshape(1, -1),
        keep_mask,
    )
    return finish(bo, gi, pool, sq, red, gw, unit_d, half // n_dp, ch // n_dp)


D = 768


epsilon = 1e-05


def gelu_exact(values_in):
    return jax.nn.gelu(values_in, approximate=False)


def gelu_slope(pre_sum, upstream):
    unused, backward = jax.vjp(gelu_exact, pre_sum)
    return backward(upstream)[0]


def channel_sums(first_term, second_term):
    return lax.psum((first_term, second_term), "tensor")


def normalize(values_in, gains, shifts):
    totals, square = channel_sums(jnp.sum(values_in, 1), jnp.sum(values_in * values_in, 1))
    average = totals / D
    spread = square / D - average * average
    scaling = lax.rsqrt(spread + epsilon)[:, None, :]
    unit_part = (values_in - average[:, None, :]) * scaling
    return (unit_part * gains[None, :, None] + shifts[None, :, None], unit_part, scaling)


def normalize_back(upstream, unit_part, scaling, gains):
    scaled = upstream * gains[None, :, None]
    totals, along_unit = channel_sums(jnp.sum(scaled, 1), jnp.sum(scaled * unit_part, 1))
    inner_part = scaled - totals[:, None, :] / D - unit_part * along_unit[:, None, :] / D
    return (scaling * inner_part, jnp.sum(upstream * unit_part, (0, 2)), jnp.sum(upstream, (0, 2)))


def body(
    mixer_input,
    keep_mask,
    ln_gain,
    ln_shift,
    token_w1,
    token_b1,
    token_w2,
    token_b2,
    chan_w1,
    chan_b1,
    chan_w2,
    chan_b2,
    grad_out,
    grad_pooled,
):
    images, channels, patches = mixer_input.shape
    full_width = channels * lax.axis_size("tensor")
    offset = lax.axis_index("tensor") * channels
    gains, shifts, weight_in, bias_in, weight_back = (
        lax.all_gather(ln_gain, "dp", axis=1, tiled=True),
        lax.all_gather(ln_shift, "dp", axis=1, tiled=True),
        lax.all_gather(token_w1, "dp", axis=1, tiled=True),
        lax.all_gather(token_b1, "dp", axis=0, tiled=True),
        lax.all_gather(token_w2, "dp", axis=0, tiled=True),
    )
    gain_own = lax.dynamic_slice_in_dim(gains, offset, channels, 1).astype(jnp.float32)
    shift_own = lax.dynamic_slice_in_dim(shifts, offset, channels, 1).astype(jnp.float32)
    kept = keep_mask.astype(jnp.float32)
    counts = jnp.sum(kept, 1)
    source = mixer_input.astype(jnp.float32)
    normed, unit_first, scale_first = normalize(source, gain_own[0], shift_own[0])
    first_low = normed.astype(jnp.bfloat16)
    token_pre = jnp.einsum(
        "bcp,ph->bch", first_low, weight_in, preferred_element_type=jnp.float32
    ) + bias_in.astype(jnp.float32)
    token_hid = gelu_exact(token_pre).astype(jnp.bfloat16)
    token_out = jnp.einsum(
        "bch,hp->bcp", token_hid, weight_back, preferred_element_type=jnp.float32
    ) + token_b2.astype(jnp.float32)
    mixture = source + token_out
    normed, unit_second, scale_second = normalize(mixture, gain_own[1], shift_own[1])
    second = normed.astype(jnp.bfloat16)
    section = lax.all_gather(second, "tensor", axis=1, tiled=True)
    pre_sum = jnp.einsum("bcp,ch->bhp", section, chan_w1, preferred_element_type=jnp.float32)
    gathered = section
    grams = jnp.einsum("bcp,bcq->bpq", section, section, preferred_element_type=jnp.float32)
    chan_pre = pre_sum
    gram_second = grams
    chan_pre = chan_pre + chan_b1.astype(jnp.float32)[None, :, None]
    chan_hid = gelu_exact(chan_pre).astype(jnp.bfloat16)
    partial_value = jnp.einsum("bhp,hc->bcp", chan_hid, chan_w2, preferred_element_type=jnp.float32)
    chan_out = (
        lax.psum_scatter(
            partial_value.astype(jnp.bfloat16), "tensor", scatter_dimension=1, tiled=True
        ).astype(jnp.float32)
        + chan_b2.astype(jnp.float32)[None, :, None]
    )
    masked = kept[:, None, :] * (mixture + chan_out)
    pooled = jnp.sum(masked, 2) / counts[:, None]
    grad_result = kept[:, None, :] * (
        grad_out.astype(jnp.float32) + grad_pooled[:, :, None] / counts[:, None, None]
    )
    grad_low = grad_result.astype(jnp.bfloat16)
    grad_chan_b2 = jnp.sum(grad_low, (0, 2), dtype=jnp.float32)
    section = lax.all_gather(grad_low, "tensor", axis=1, tiled=True)
    hid_sum = jnp.einsum("bcp,hc->bhp", section, chan_w2, preferred_element_type=jnp.float32)
    column_block = jnp.einsum("bhp,bcp->hc", chan_hid, section, preferred_element_type=jnp.float32)
    grams = jnp.einsum("bcp,bcq->bpq", section, section, preferred_element_type=jnp.float32)
    pre_grad = gelu_slope(chan_pre, hid_sum).astype(jnp.bfloat16)
    grad_chan_b1 = jnp.sum(pre_grad, (0, 2), dtype=jnp.float32)
    grad_chan_w1 = jnp.einsum("bcp,bhp->ch", gathered, pre_grad, preferred_element_type=jnp.float32)
    share_w1, share_b1, share_w2, share_b2 = (
        lax.psum_scatter(
            grad_chan_w1.astype(jnp.bfloat16), "dp", scatter_dimension=0, tiled=True
        ).astype(jnp.float32),
        lax.psum_scatter(
            grad_chan_b1.astype(jnp.bfloat16), "dp", scatter_dimension=0, tiled=True
        ).astype(jnp.float32),
        lax.psum_scatter(
            column_block.astype(jnp.bfloat16), "dp", scatter_dimension=1, tiled=True
        ).astype(jnp.float32),
        lax.psum_scatter(
            grad_chan_b2.astype(jnp.bfloat16), "dp", scatter_dimension=0, tiled=True
        ).astype(jnp.float32),
    )
    second_part = jnp.einsum("bhp,ch->bcp", pre_grad, chan_w1, preferred_element_type=jnp.float32)
    second_grad = lax.psum_scatter(
        second_part.astype(jnp.bfloat16), "tensor", scatter_dimension=1, tiled=True
    ).astype(jnp.float32)
    gram_pre = jnp.einsum("bhp,bhq->bpq", pre_grad, pre_grad, preferred_element_type=jnp.float32)
    gram_hid = jnp.einsum("bhp,bhq->bpq", chan_hid, chan_hid, preferred_element_type=jnp.float32)
    own_terms = jnp.sum(gram_second * gram_pre + gram_hid * grams, (1, 2))
    own_terms = own_terms + jnp.sum(jnp.square(jnp.sum(pre_grad, 2, dtype=jnp.float32)), 1)
    own_terms = own_terms + jnp.sum(jnp.square(jnp.sum(grad_low, 2, dtype=jnp.float32)), 1)
    example_sq = lax.psum(own_terms, "tensor")
    back_second, gain_second, shift_second = normalize_back(
        second_grad, unit_second, scale_second, gain_own[1]
    )
    mixture_grad = grad_result + back_second
    out_low = mixture_grad.astype(jnp.bfloat16)
    grad_token_b2 = jnp.sum(out_low, (0, 1), dtype=jnp.float32)
    token_hid_grad = jnp.einsum(
        "bcp,hp->bch", out_low, weight_back, preferred_element_type=jnp.float32
    )
    grad_token_w2 = jnp.einsum(
        "bch,bcp->hp", token_hid, out_low, preferred_element_type=jnp.float32
    )
    token_pre_grad = gelu_slope(token_pre, token_hid_grad).astype(jnp.bfloat16)
    grad_token_b1 = jnp.sum(token_pre_grad, (0, 1), dtype=jnp.float32)
    grad_token_w1 = jnp.einsum(
        "bcp,bch->ph", first_low, token_pre_grad, preferred_element_type=jnp.float32
    )
    first_grad = jnp.einsum(
        "bch,ph->bcp", token_pre_grad, weight_in, preferred_element_type=jnp.float32
    )
    back_first, gain_first, shift_first = normalize_back(
        first_grad, unit_first, scale_first, gain_own[0]
    )
    grad_input = mixture_grad + back_first
    gain_parts = lax.dynamic_update_slice_in_dim(
        jnp.zeros((2, full_width), jnp.float32), jnp.stack([gain_first, gain_second]), offset, 1
    )
    shift_parts = lax.dynamic_update_slice_in_dim(
        jnp.zeros((2, full_width), jnp.float32), jnp.stack([shift_first, shift_second]), offset, 1
    )
    total_gain, total_shift, total_w1, total_b1, total_w2 = (
        lax.psum(gain_parts.astype(jnp.bfloat16), "tensor").astype(jnp.float32),
        lax.psum(shift_parts.astype(jnp.bfloat16), "tensor").astype(jnp.float32),
        lax.psum(grad_token_w1.astype(jnp.bfloat16), "tensor").astype(jnp.float32),
        lax.psum(grad_token_b1.astype(jnp.bfloat16), "tensor").astype(jnp.float32),
        lax.psum(grad_token_w2.astype(jnp.bfloat16), "tensor").astype(jnp.float32),
    )
    share_gain, share_shift, share_tw1, share_tb1, share_tw2 = (
        lax.psum_scatter(
            total_gain.astype(jnp.bfloat16), "dp", scatter_dimension=1, tiled=True
        ).astype(jnp.float32),
        lax.psum_scatter(
            total_shift.astype(jnp.bfloat16), "dp", scatter_dimension=1, tiled=True
        ).astype(jnp.float32),
        lax.psum_scatter(
            total_w1.astype(jnp.bfloat16), "dp", scatter_dimension=1, tiled=True
        ).astype(jnp.float32),
        lax.psum_scatter(
            total_b1.astype(jnp.bfloat16), "dp", scatter_dimension=0, tiled=True
        ).astype(jnp.float32),
        lax.psum_scatter(
            total_w2.astype(jnp.bfloat16), "dp", scatter_dimension=0, tiled=True
        ).astype(jnp.float32),
    )
    share_tb2 = lax.psum(grad_token_b2, ("dp", "tensor"))
    return (
        masked,
        pooled,
        grad_input,
        share_gain,
        share_shift,
        share_tw1,
        share_tb1,
        share_tw2,
        share_tb2,
        share_w1,
        share_b1,
        share_w2,
        share_b2,
        example_sq,
    )


def solution(mesh):
    n_dp, n_tensor = mesh.shape["dp"], mesh.shape["tensor"]
    chosen = body
    if (n_dp, n_tensor) == (16, 2):
        chosen = functools.partial(fused_body, n_dp, (4, 2, 2))
    return jax.shard_map(
        chosen,
        mesh=mesh,
        in_specs=(
            P("dp", "tensor", None),
            P("dp", None),
            P(None, "dp"),
            P(None, "dp"),
            P(None, "dp"),
            P("dp"),
            P("dp", None),
            P(),
            P(None, "tensor"),
            P("tensor"),
            P("tensor", None),
            P("tensor"),
            P("dp", "tensor", None),
            P("dp", "tensor"),
        ),
        out_specs=(
            P("dp", "tensor", None),
            P("dp", "tensor"),
            P("dp", "tensor", None),
            P(None, "dp"),
            P(None, "dp"),
            P(None, "dp"),
            P("dp"),
            P("dp", None),
            P(),
            P("dp", "tensor"),
            P(("tensor", "dp")),
            P("tensor", "dp"),
            P(("tensor", "dp")),
            P("dp"),
        ),
        check_vma=False,
    )
```

time: 132 us -> 113 us (0.86)
  the two profiles are of different devices: /device:TPU:31 before, /device:TPU:0 now
where the time goes in v3:
time: 113 us; the launch traced here: 112 us
  Pallas kernels  108 us (96%)
  local copies, waits for them, and re-layouts  3.75 us (3%)
    pallas_call x1, Pallas kernels, mixer(): pl.pallas_call(functools.partial(mixer_kernel, (n_dp, ni, ch, pat, tp, un...  101 us
    pallas_call x1, Pallas kernels, finish(): pl.pallas_call(functools.partial(finish_kernel, (pat, unit_d, per_h, per_...  6.07 us

profile of v3, /device:TPU:0, one launch (start us, length us, event | category | flops | bytes accessed | tf_op | source)
XLA Modules:
  0.0 112.0 jit_solution(5928001753346607464)
XLA Ops:
  0.6 1.2 %reshape.58.tb2_ref = bf16[1,196]{1,0:T(2,128)(2,1)} reshape(bf16[196]{0:T(256)(128)(2,1)} %param.21) | data formatting | bytes 784 | tf_op jit(solution)/shard_map/reshape | solution.py:1065
  1.9 1.2 %reshape.56.cb2_ref = bf16[1,384]{1,0:T(2,128)(2,1)} reshape(bf16[384]{0:T(512)(128)(2,1)} %param.25) | data formatting | bytes 1536 | tf_op jit(solution)/shard_map/reshape | solution.py:1059
  3.1 1.3 %reshape.55.b1_ref = bf16[1,1536]{1,0:T(2,128)(2,1)} reshape(bf16[1536]{0:T(1024)(128)(2,1)} %param.23) | data formatting | bytes 6144 | tf_op jit(solution)/shard_map/reshape | solution.py:1058
  4.4 101.5 %mixer.1 = (bf16[12,196,384]{2,1,0:T(8,128)(2,1)}, bf16[12,196,384]{2,1,0:T(8,128)(2,1)}, bf16[6,208,768]{2,1,0:T(8,128)(2,1)}, bf16[6,256,768]{2,1,0:T(8,128)(2...) custom-call(bf16[12,196,384]{2,1,0:T(8,128)(2,1)} %bitcast.13, ...), custom_call_target="tpu_custom_call" | custom-call | tf_op jit(solution)/shard_map/mixer/pallas_call | solution.py:848
  105.9 6.1 %finish.1 = (f32[12,196,384]{2,1,0:T(8,128)}, f32[12,384]{1,0:T(8,128)}, f32[12,196,384]{2,1,0:T(8,128)}, f32[2,48]{1,0:T(2,128)}, f32[2,48]{1,0:T(2,128)}, /*in...) custom-call(bf16[12,196,384]{2,1,0:T(8,128)(2,1)} %get-tuple-element, ...), custom_call_target="tpu_custom_call" | custom-call | tf_op jit(solution)/shard_map/finish/pallas_call | solution.py:1012

commit v4 on v3

--- a/solution.py
+++ b/solution.py
@@ -107,14 +107,12 @@
     gp_ref,
     w1_hbm,
     w2_hbm,
-    b1_ref,
-    cb2_ref,
+    row_ref,
     gain_ref,
     shift_ref,
     tw1_ref,
     tb1_ref,
     tw2_ref,
-    tb2_ref,
     keep_ref,
     bo_hbm,
     gi_hbm,
@@ -166,8 +164,8 @@
     cs,
     bos,
     gis,
+    sg,
     ob,
-    mg,
     ol,
     tg,
     fg,
@@ -175,13 +173,14 @@
     acc_tok,
     row_h,
     row_c,
-    row_p,
     pool_a,
     pool_r,
     sq_a,
     sq_r,
     msgs,
     msgr,
+    msgz,
+    msgl,
     red_a,
     red_r,
     tg_s,
@@ -217,7 +216,7 @@
     y_dev = ((z * ny + (1 - y)) * nx + x, core)
     full = 2 * ch
     rows_own = full // n_dp
-    half = w1s.shape[2]
+    half = w1s.shape[1] // 2
     n_blk = half // BLK
     toks = ni * tp
     toks_pad = gh.shape[0]
@@ -239,8 +238,8 @@
                 (pack, packf.at[:, here]),
                 (x_hbm.at[theirs], xf.at[:, :, here]),
                 (go_hbm.at[theirs], gof.at[:, :, here]),
-                (w1_hbm, w1s.at[1]),
-                (w2_hbm, w2s.at[1]),
+                (w2_hbm, w2s.at[pl.ds(half, half)]),
+                (w1_hbm, w1s.at[:, pl.ds(half, half)]),
             )
         )
     ]
@@ -250,8 +249,8 @@
             (
                 (x_hbm.at[ours], xf.at[:, :, here]),
                 (go_hbm.at[ours], gof.at[:, :, here]),
-                (w1_hbm, w1s.at[0]),
-                (w2_hbm, w2s.at[0]),
+                (w1_hbm, w1s.at[:, pl.ds(0, half)]),
+                (w2_hbm, w2s.at[pl.ds(0, half)]),
             )
         )
     ]
@@ -279,9 +278,9 @@
     msg[:, 128:] = (tmp_w[0, :rows_own, 128:] + columns).astype(BF16)
     pack[...] = jnp.zeros_like(pack)
     pack[:images, :] = gp_ref[...]
-    pack[images : images + 1, :] = cb2_ref[...].astype(F32)
+    pack[images : images + 1, :] = row_ref[:, half : half + ch].astype(F32)
     for n in range(bias_rows):
-        pack[images + 1 + n : images + 2 + n, :] = b1_ref[:, n * ch : (n + 1) * ch].astype(F32)
+        pack[images + 1 + n : images + 2 + n, :] = row_ref[:, n * ch : (n + 1) * ch].astype(F32)
     greet_all(n_dp, dp, core)
 
     def send(n, c):
@@ -296,7 +295,7 @@
     packf[:, here] = pack[...]
     keep_t[...] = jnp.zeros_like(keep_t)
     keep_t[:images, :pat] = keep_ref[...].astype(F32)
-    keep_t[images : images + 1, :pat] = tb2_ref[...].astype(F32)
+    keep_t[images : images + 1, :pat] = row_ref[:, half + ch : half + ch + pat].astype(F32)
     turned = jnp.transpose(keep_t[...])
     keep_t[...] = turned
     tb2_w[...] = jnp.broadcast_to(turned[:tp, images : images + 1], (tp, 128))
@@ -305,7 +304,7 @@
     ph[toks:, :] = zero_rows
     st[toks:, :] = zero_rows[:, :full]
     yt[toks:, :] = zero_rows[:, :full]
-    for ref in (row_h, row_c, row_p, acc_norm, acc_tok, pool_a, sq_a, ol):
+    for ref in (row_h, row_c, acc_norm, acc_tok, pool_a, sq_a, ol):
         ref[...] = jnp.zeros_like(ref)
     partial = row_pieces(pat)
     last = slice(pat // ROWS * ROWS, tp)
@@ -316,6 +315,7 @@
         ms[n, last, :] = blank
         fs[n, last.start :, :] = jnp.zeros((kp - last.start, full), BF16)
         fs[n, pat : pat + 1, :] = jnp.ones((1, full), BF16)
+        hs[n, ds:, :] = jnp.ones((16, full), BF16)
     for c in local_copies[:2]:
         c.wait()
     for c in pair_copies[:3]:
@@ -345,6 +345,9 @@
         return carry
 
     lax.fori_loop(0, ni, early_step, 0)
+    local_copies[3].wait()
+    for a in range(0, half, BLK):
+        ph[:toks, a : a + BLK] = nt(yt[:toks, :], w2s[a : a + BLK, :]).astype(BF16)
     for n in range(bias_rows):
         row = packf[images + 1 + n : images + 2 + n, :]
         swapped = jnp.concatenate([row[:, ch:], row[:, :ch]], axis=1)
@@ -385,7 +388,7 @@
             (ms, mix_hbm),
         )
         return [
-            pltpu.make_async_copy(a.at[slot], b.at[i], spill.at[slot, n])
+            pltpu.make_async_copy(a.at[slot, pl.ds(0, b.shape[1])], b.at[i], spill.at[slot, n])
             for n, (a, b) in enumerate(pairs)
         ]
 
@@ -409,7 +412,7 @@
                 cdf, pdf = gelu_parts(v)
                 hs[slot, a : a + 32, c] = (v * cdf).astype(BF16)
                 ls[slot, a : a + 32, c] = (cdf + v * pdf).astype(BF16)
-            ob[:, c] = nn(twt[1], hs[slot, :, c])
+            ob[:, c] = nn(twt[1], hs[slot, :ds, c])
         for r in partial:
             v = xf[i, r, :].astype(F32) + (ob[r, :] + across(tb2_w[r, :], full))
             ms[slot, r, :] = v.astype(BF16)
@@ -425,15 +428,14 @@
     for i in (ni - 2, ni - 1):
         for c in saved(i):
             c.wait()
-    for c in local_copies[2:]:
-        c.wait()
+    local_copies[2].wait()
     for c in pair_copies[3:]:
         c.wait_recv()
 
     def image_loads(i, slot):
         pairs = ((u0_hbm, us), (f_hbm, fs), (hid_hbm, hs), (slope_hbm, ls), (u1_hbm, vs))
         return [
-            pltpu.make_async_copy(a.at[i], b.at[slot], in_sem.at[slot, n])
+            pltpu.make_async_copy(a.at[i], b.at[slot, pl.ds(0, a.shape[1])], in_sem.at[slot, n])
             for n, (a, b) in enumerate(pairs)
         ]
 
@@ -449,7 +451,7 @@
         return remote(pb, ra.at[slot], sa.at[0], rsa.at[slot], other)
 
     def first_copies(j):
-        slot = lax.rem(j, 3)
+        slot = lax.rem(j, 2)
         return (
             remote(
                 gs.at[slot, 0, :, :, 1 - x], r1.at[j, 0], s1.at[slot, 0], rs1.at[j, 0], x_dev
@@ -458,7 +460,7 @@
         )
 
     def second_copies(j):
-        slot = lax.rem(j, 3)
+        slot = lax.rem(j, 2)
         return (
             remote(b2.at[slot, 0, :, 1 - y], r2.at[j, 0], s2.at[slot, 0], rs2.at[j, 0], y_dev),
             remote(b2.at[slot, 1, :, 1 - x], r2.at[j, 1], s2.at[slot, 1], rs2.at[j, 1], x_dev),
@@ -492,7 +494,7 @@
             gw_o[m, :, at] = v
 
     def finish_second(j):
-        slot, into = lax.rem(j, 3), lax.rem(j, 2)
+        slot, into = lax.rem(j, 2), lax.rem(j, 2)
         for c in second_copies(j):
             c.wait()
         for m, mine in ((0, y), (1, x)):
@@ -503,48 +505,51 @@
             c.start()
 
     def finish_first(j):
-        slot = lax.rem(j, 3)
+        slot, into = lax.rem(j, 2), lax.rem(j, 2)
         for c in first_copies(j):
             c.wait()
         for k in range(nz):
             for n in range(2):
                 v = gs[slot, 0, k, n, x].astype(F32) + r1[j, 0, k, n].astype(F32)
-                b2[slot, 0, k, n] = v.astype(BF16)
+                b2[into, 0, k, n] = v.astype(BF16)
                 v = gs[slot, 1, k, y, n].astype(F32) + r1[j, 1, k, n].astype(F32)
-                b2[slot, 1, k, n] = v.astype(BF16)
+                b2[into, 1, k, n] = v.astype(BF16)
         for c in second_copies(j):
             c.start()
 
     def hidden_block(side, j):
-        at = pl.ds(pl.multiple_of(j * BLK, BLK), BLK)
         col = pl.ds(pl.multiple_of(side * half + j * BLK, BLK), BLK)
-        w1 = w1s[side, :, at]
-        w2 = w2s[side, at, :]
+        w1 = w1s[:, col]
+        w2 = w2s[col, :]
         b_row = bias[0:1, col]
-        for i in range(ni):
-            r0 = i * tp
-            r = slice(r0, r0 + tp)
-            pre = nn(st[r, :], w1)
-            up_grad = nt(yt[r, :], w2)
-            acc = jnp.zeros((8, BLK), F32)
-            for a in range(0, tp, 16):
-                v = pre[a : a + 16] + b_row
-                cdf, pdf = gelu_parts(v)
-                gh[r0 + a : r0 + a + 16, col] = (v * cdf).astype(BF16)
-                p = up_grad[a : a + 16] * (cdf + v * pdf)
-                ph[r0 + a : r0 + a + 16, col] = p.astype(BF16)
-                acc += fold(p)
-            row = jnp.sum(acc, 0, keepdims=True)
-            row_h[0:1, col] += row
-            row_h[1 + i : 2 + i, col] = row
+        for i0 in range(0, ni, 2):
+            both = slice(i0 * tp, (i0 + 2) * tp)
+            pre = nn(st[both, :], w1)
+            if side == 1:
+                up_grad = nt(yt[both, :], w2)
+            for i in (i0, i0 + 1):
+                acc = jnp.zeros((8, BLK), F32)
+                for a in range(0, tp, 16):
+                    r = slice(i * tp + a, i * tp + a + 16)
+                    q = slice(r.start - both.start, r.stop - both.start)
+                    v = pre[q] + b_row
+                    cdf, pdf = gelu_parts(v)
+                    gh[r, col] = (v * cdf).astype(BF16)
+                    p = up_grad[q] if side == 1 else ph[r, col].astype(F32)
+                    p = p * (cdf + v * pdf)
+                    ph[r, col] = p.astype(BF16)
+                    acc += fold(p)
+                row = jnp.sum(acc, 0, keepdims=True)
+                row_h[0:1, col] += row
+                row_h[1 + i : 2 + i, col] = row
         return tn(st[...], ph[:, col]), tn(yt[...], gh[:, col])
 
-    def rounds(s):
-        for lag, work in ((8, finish_third), (6, finish_second), (3, finish_first)):
-
-            @pl.when((s >= lag) & (s < n_blk + lag))
+    def due(*work):
+        for step, j, exists in work:
+
+            @pl.when(exists)
             def _():
-                work(s - lag)
+                step(j)
 
     def split(v, k):
         per = full // nz
@@ -556,14 +561,18 @@
             for k in range(nz):
                 pb[m, k] = split(v, k).astype(BF16)
         pair_copy(slot).start()
+        due(
+            (finish_third, j - 5, j >= 5),
+            (finish_first, j - 2, j >= 2),
+        )
         grads = hidden_block(0, j)
         pair_copy(slot).wait()
-        rounds(j)
         for m, v in enumerate(grads):
             for k in range(nz):
-                gs[lax.rem(j, 3), m, k] = (split(v, k) + ra[slot, m, k].astype(F32)).astype(BF16)
+                gs[slot, m, k] = (split(v, k) + ra[slot, m, k].astype(F32)).astype(BF16)
         for c in first_copies(j):
             c.start()
+        due((finish_second, j - 3, j >= 3))
         return carry
 
     lax.fori_loop(0, n_blk, block_step, 0)
@@ -602,9 +611,11 @@
 
     def backward_step(i, carry):
         slot = lax.rem(i, 2)
-        rounds(n_blk + i)
-        rows = pl.ds(pl.multiple_of(i * tp, 16), tp)
-        ob[...] = nt(ph[rows, :half], w1s[0]) + nt(ph[rows, half:], w1s[1])
+        due(
+            (finish_third, n_blk - 3, i == 4),
+            (finish_second, n_blk - 2, i == 4),
+            (finish_first, n_blk - 1, i == 2),
+        )
 
         @pl.when(i + 1 < ni)
         def _():
@@ -621,18 +632,18 @@
         zero8 = jnp.zeros((8, full), F32)
         dy, gain, shift = zero8, zero8, zero8
         for r in pieces:
-            sg = ob[r, :]
+            e_rows = token_rows(i, r)
+            grad = sg[e_rows, :].astype(F32)
             unit = vs[slot, r, :].astype(F32)
-            gain += fold(sg * unit)
-            shift += fold(sg)
-            e = sg * norm[1:2, :]
+            gain += fold(grad * unit)
+            shift += fold(grad)
+            e = grad * norm[1:2, :]
             m = jnp.sum(e, 1, keepdims=True) * (1.0 / full)
             n = jnp.sum(e * unit, 1, keepdims=True) * (1.0 / full)
-            y_rows = pl.ds(pl.multiple_of(i * tp + r.start, 16), ROWS)
-            v = yt[y_rows, :].astype(F32)
+            v = yt[e_rows, :].astype(F32)
             dy += fold(v)
             v = v + across(cs[i, 1, r, :], full) * (e - m - unit * n)
-            mg[r, :] = v
+            ob[r, :] = v
             ol[r, :] = v.astype(BF16)
         dy = jnp.sum(dy, 0, keepdims=True)
         row_c[0:1, :] += dy
@@ -645,9 +656,8 @@
                 r = slice(a, a + 32)
                 tg[r, c] = (hg[r] * ls[slot, r, c].astype(F32)).astype(BF16)
             fg[:, c] = nn(twt[0], tg[:, c])
-        acc_tok[0] += nt(tg[...], fs[slot])
+        acc_tok[0, :ds] += nt(tg[...], fs[slot])
         acc_tok[1] += nt(hs[slot], ol[...])
-        row_p[...] += nt(jnp.ones((16, full), BF16), ol[...])
         gain, shift = zero8, zero8
         for r in pieces:
             g = fg[r, :]
@@ -657,13 +667,24 @@
             e = g * norm[0:1, :]
             m = jnp.sum(e, 1, keepdims=True) * (1.0 / full)
             n = jnp.sum(e * unit, 1, keepdims=True) * (1.0 / full)
-            v = mg[r, :] + across(cs[i, 0, r, :], full) * (e - m - unit * n)
+            v = ob[r, :] + across(cs[i, 0, r, :], full) * (e - m - unit * n)
             store_rows(gis, slot, r, v)
         acc_norm[0] += gain
         acc_norm[2] += shift
         out_start(1, i)
         return carry
 
+    part = toks // 3
+    for n in range(3):
+        if n == 0:
+            finish_third(n_blk - 5)
+        if n == 1:
+            finish_third(n_blk - 4)
+            finish_first(n_blk - 2)
+        if n == 2:
+            finish_second(n_blk - 3)
+        a = n * part
+        sg[a : a + part, :] = nt(ph[a : a + part, :], w1s[...]).astype(BF16)
     lax.fori_loop(0, ni, backward_step, 0)
     h_0 = jnp.where(core == 0, row_h[0:1, :half], row_h[0:1, half:])
     h_1 = jnp.where(core == 0, row_h[0:1, half:], row_h[0:1, :half])
@@ -671,7 +692,7 @@
     norms = jnp.concatenate([norms, jnp.zeros((4, full), F32)], 0)
     per_h = half // n_dp
     per_c = ch // n_dp
-    tail = msgs.shape[1] - 2 * unit_d
+    tail = msgs.shape[3] - 2 * unit_d
 
     def cut(v, start, size):
         n = v.shape[1]
@@ -685,6 +706,7 @@
         return jnp.where(lane < size, v, 0.0)
 
     for d in range(n_dp):
+        place = (d // (ny * nx), d // nx % ny, d % nx)
         top = jnp.concatenate(
             [
                 acc_tok[0, unit_d * d : unit_d * (d + 1), :],
@@ -692,10 +714,10 @@
             ],
             axis=0,
         )
-        msgs[d, : 2 * unit_d, :] = top.astype(BF16)
+        msgs[place + (slice(0, 2 * unit_d),)] = top.astype(BF16)
         extra = jnp.concatenate(
             [
-                row_p[0:1, :],
+                acc_tok[1, ds : ds + 1, :],
                 cut(h_0, per_h * d, per_h)[0:1],
                 cut(h_1, per_h * d, per_h)[0:1],
                 cut(row_c[0:1, :], per_c * d, per_c)[0:1],
@@ -705,47 +727,83 @@
             ],
             axis=0,
         )
-        msgs[d, 2 * unit_d :, :] = extra.astype(BF16)
-
-    def token_send(n):
-        to = lax.rem(dp + n, n_dp)
-        return remote(msgs.at[to], msgr.at[dp], tok_s.at[n], tok_r.at[dp], (to, core))
-
-    def token_arrival(n):
-        source = lax.rem(dp + n_dp - n, n_dp)
-        return remote(
-            msgs.at[source], msgr.at[source], tok_s.at[n], tok_r.at[source], (source, core)
+        msgs[place + (slice(2 * unit_d, None),)] = extra.astype(BF16)
+
+    plane_copies = []
+    for n, (ay, ax) in enumerate(((0, 1), (1, 0), (1, 1))):
+        to_y = 1 - y if ay else y
+        to_x = 1 - x if ax else x
+        plane_copies.append(
+            remote(
+                msgs.at[:, to_y, to_x],
+                msgr.at[n],
+                tok_s.at[n],
+                tok_r.at[n],
+                ((z * ny + to_y) * nx + to_x, core),
+            )
         )
-
-    def send(n, c):
-        token_send(n).start()
-        return c
-
-    lax.fori_loop(1, n_dp, send, 0)
-    msgr[dp] = msgs[dp]
-
-    def forward_step(i, carry):
-        slot = lax.rem(i, 2)
-        rounds(n_blk + ni + i)
-        r = pl.ds(pl.multiple_of(i * tp, 16), tp)
-
-        @pl.when(i + 1 < ni)
-        def _():
-            for c in late_loads(i + 1, 1 - slot):
-                c.start()
-
-        ob[...] = nn(gh[r, :half], w2s[0]) + nn(gh[r, half:], w2s[1])
-        g = gh[r, :]
-        p = ph[r, :]
-        s = st[r, :]
-        y_all = yt[r, :]
-        both = nt(s, s) * nt(p, p) + nt(g, g) * nt(y_all, y_all)
+    line_copies = []
+    for n in range(1, nz):
+        to_z = lax.rem(z + n, nz)
+        line_copies.append(
+            remote(
+                msgz.at[to_z],
+                msgl.at[n - 1],
+                tok_s.at[n + 2],
+                tok_r.at[n + 2],
+                ((to_z * ny + y) * nx + x, core),
+            )
+        )
+    red_copy = remote(red_a, red_r, fin_s.at[2], fin_r.at[2], other)
+
+    def plane_sum():
+        for c in plane_copies:
+            c.wait()
+        for n in range(nz):
+            v = msgs[n, y, x].astype(F32)
+            for m in range(3):
+                v = v + msgr[m, n].astype(F32)
+            msgz[n] = v.astype(BF16)
+        for c in line_copies:
+            c.start()
+
+    def line_sum():
+        for c in line_copies:
+            c.wait()
+        v = msgz[z].astype(F32)
+        for n in range(nz - 1):
+            v = v + msgl[n].astype(F32)
+        red_a[...] = v
+        red_copy.start()
+
+    for c in plane_copies:
+        c.start()
+
+    def gram_step(i, carry):
+        due(
+            (finish_third, n_blk - 2, i == 0),
+            (finish_third, n_blk - 1, i == 3),
+            (lambda j: line_sum(), 0, i == 4),
+        )
+        r = token_rows(i, slice(0, tp))
+        g, p, s, dy = gh[r, :], ph[r, :], st[r, :], yt[r, :]
+        both = nt(s, s) * nt(p, p) + nt(g, g) * nt(dy, dy)
         sq = jnp.sum(jnp.sum(both, 0, keepdims=True), 1, keepdims=True)
         rh = row_h[pl.ds(1 + i, 1), :]
         rc = row_c[pl.ds(1 + i, 1), :]
         sq = sq + jnp.sum(rh * rh, 1, keepdims=True) + jnp.sum(rc * rc, 1, keepdims=True)
         lane = lax.broadcasted_iota(jnp.int32, (1, 128), 1)
         sq_a[0:1, :] += jnp.where(lane == my_first + i, sq, 0.0)
+        return carry
+
+    def forward_step(i, carry):
+        slot = lax.rem(i, 2)
+
+        @pl.when(i + 1 < ni)
+        def _():
+            for c in late_loads(i + 1, 1 - slot):
+                c.start()
+
         for c in late_loads(i, slot):
             c.wait()
 
@@ -759,7 +817,8 @@
         for r in pieces:
             kept = cs[i, 2, r, :]
             kept_sum += fold(kept)
-            bo = across(kept, full) * (ms[slot, r, :].astype(F32) + (ob[r, :] + chan_bias))
+            out = sg[token_rows(i, r), :].astype(F32)
+            bo = across(kept, full) * (ms[slot, r, :].astype(F32) + (out + chan_bias))
             pool += fold(bo)
             store_rows(bos, slot, r, bo)
         count = jnp.sum(kept_sum, 0, keepdims=True)
@@ -767,29 +826,16 @@
         out_start(0, i)
         return carry
 
+    finish_second(n_blk - 1)
+    for a in range(0, toks, part):
+        sg[a : a + part, :] = nn(gh[a : a + part, :], w2s[...]).astype(BF16)
     lax.fori_loop(0, ni, forward_step, 0)
     pool_copy = remote(pool_a.at[:, there], pool_r, fin_s.at[0], fin_r.at[0], other)
     pool_copy.start()
+    plane_sum()
+    lax.fori_loop(0, ni, gram_step, 0)
     sq_copy = remote(sq_a, sq_r, fin_s.at[1], fin_r.at[1], other)
     sq_copy.start()
-
-    def arrive(n, c):
-        token_arrival(n).wait_recv()
-        return c
-
-    lax.fori_loop(1, n_dp, arrive, 0)
-    total = msgr[0].astype(F32)
-    for d in range(1, n_dp):
-        total = total + msgr[d].astype(F32)
-    red_a[...] = total
-    red_copy = remote(red_a, red_r, fin_s.at[2], fin_r.at[2], other)
-    red_copy.start()
-
-    def sent(n, c):
-        token_send(n).wait_send()
-        return c
-
-    lax.fori_loop(1, n_dp, sent, 0)
 
     def sent_w(n, c):
         weights_copy(n).wait_send()
@@ -811,7 +857,7 @@
     red_o[...] = red_a[...] + red_r[...]
 
 
-def mixer(n_dp, grid3, x, go, gp, w1, w2, b1, cb2, gain, shift, tw1, tb1, tw2, tb2, keep):
+def mixer(n_dp, grid3, x, go, gp, w1, w2, row, gain, shift, tw1, tb1, tw2, keep):
     images, pat, ch = x.shape
     ni = images // 2
     full = 2 * ch
@@ -848,7 +894,7 @@
     res = pl.pallas_call(
         functools.partial(mixer_kernel, (n_dp, ni, ch, pat, tp, unit_d, nz, ny, nx)),
         out_shape=[o[0] for o in outs],
-        in_specs=[ANY, ANY, VM, ANY, ANY] + [VM] * 9,
+        in_specs=[ANY, ANY, VM, ANY, ANY] + [VM] * 7,
         out_specs=[o[1] for o in outs],
         scratch_shapes=[
             vm((ni, pat, full), BF16),
@@ -867,44 +913,45 @@
             vm((2, tp, ds), BF16),
             vm((toks_pad, full), BF16),
             vm((toks_pad, full), BF16),
-            vm((2, full, half), BF16),
-            vm((2, half, full), BF16),
+            vm((full, 2 * half), BF16),
+            vm((2 * half, full), BF16),
             vm((8, 2 * half), F32),
             vm((toks_pad, 2 * half), BF16),
             vm((toks_pad, 2 * half), BF16),
-            vm((3, 2) + part, BF16),
+            vm((2, 2) + part, BF16),
             vm((2,) + part, BF16),
             vm((2, 2) + part, BF16),
             vm((n_blk, 2, nz, 2, rows_own, BLK), BF16),
-            vm((3, 2, nz, 2, rows_own, BLK), BF16),
+            vm((2, 2, nz, 2, rows_own, BLK), BF16),
             vm((n_blk, 2, nz, rows_own, BLK), BF16),
             vm((2, nz, 2, rows_own, BLK), BF16),
             vm((n_blk, nz - 1, 2, rows_own, BLK), BF16),
             vm((2, tp, full), BF16),
             vm((2, kp, full), BF16),
-            vm((2, ds, full), BF16),
+            vm((2, ds + 16, full), BF16),
             vm((2, ds, full), BF16),
             vm((2, tp, full), BF16),
             vm((2, tp, full), BF16),
             vm((ni, 3, tp, 128), F32),
             vm((2, pat, full), BF16),
             vm((2, pat, full), BF16),
-            vm((tp, full), F32),
+            vm((ni * tp, full), BF16),
             vm((tp, full), F32),
             vm((kp, full), BF16),
             vm((ds, full), BF16),
             vm((tp, full), F32),
             vm((4, 8, full), F32),
-            vm((2, ds, kp), F32),
+            vm((2, ds + 16, kp), F32),
             vm((8, 2 * half), F32),
             vm((8, full), F32),
-            vm((16, kp), F32),
             vm((n_img, full), F32),
             vm((n_img, ch), F32),
             vm((8, 128), F32),
             vm((8, 128), F32),
-            vm((n_dp, n_msg, kp), BF16),
-            vm((n_dp, n_msg, kp), BF16),
+            vm((nz, ny, nx, n_msg, kp), BF16),
+            vm((3, nz, n_msg, kp), BF16),
+            vm((nz, n_msg, kp), BF16),
+            vm((nz - 1, n_msg, kp), BF16),
             vm((n_msg, kp), F32),
             vm((n_msg, kp), F32),
             dma((n_dp,)),
@@ -916,17 +963,17 @@
             dma((2, 6)),
             dma((1,)),
             dma((2,)),
-            dma((3, 2)),
+            dma((2, 2)),
             dma((n_blk, 2)),
-            dma((3, 2)),
+            dma((2, 2)),
             dma((n_blk, 2)),
             dma((2, nz - 1)),
             dma((n_blk, nz - 1)),
             dma((2, 2)),
             dma((ni, 2)),
             dma((2, 2)),
-            dma((n_dp,)),
-            dma((n_dp,)),
+            dma((nz + 2,)),
+            dma((nz + 2,)),
             dma((3,)),
             dma((3,)),
         ],
@@ -934,21 +981,21 @@
             collective_id=0, has_side_effects=True, vmem_limit_bytes=VMEM_BYTES
         ),
         name="mixer",
-    )(x, go, gp, w1, w2, b1, cb2, gain, shift, tw1, tb1, tw2, tb2, keep)
+    )(x, go, gp, w1, w2, row, gain, shift, tw1, tb1, tw2, keep)
     return res[:2] + res[8:]
 
 
 def finish_kernel(
     dims,
-    bo_ref,
-    gi_ref,
+    bo_hbm,
+    gi_hbm,
     pool_ref,
     sq_ref,
     red_ref,
     gw_ref,
-    bo_o,
+    bo_out,
     pool_o,
-    gi_o,
+    gi_out,
     gain_o,
     shift_o,
     tw1_o,
@@ -960,39 +1007,57 @@
     w2_o,
     b2_o,
     sq_o,
+    narrow,
+    broad,
+    in_sem,
+    out_sem,
 ):
     pat, unit_d, per_h, per_c = dims
     _, core = where_am_i()
-    bo_o[...] = bo_ref[...].astype(F32)
-    gi_o[...] = gi_ref[...].astype(F32)
-
-    @pl.when(pl.program_id(0) == 0)
-    def _():
-        images = pool_o.shape[0]
-        pool_o[...] = pool_ref[:images, :]
-        sq_o[...] = sq_ref[0:1, :images]
-        red = red_ref[...]
-        n = 2 * unit_d
-        tw1_o[...] = red[:unit_d, :pat]
-        tw2_o[...] = red[unit_d:n, :pat]
-        gain_o[...] = red[n + 8 : n + 10, :n]
-        shift_o[...] = red[n + 10 : n + 12, :n]
-        tb1_o[...] = jnp.transpose(red[: up(unit_d, 8), 128:])[pat - 128 : pat - 127, :unit_d]
-        tb2_o[...] = red[n : n + 1, :pat]
-        w1_o[...] = gw_ref[0]
-        w2_o[...] = gw_ref[1]
-        b1_o[...] = jnp.where(core == 0, red[n + 1 : n + 2, :per_h], red[n + 2 : n + 3, :per_h])
-        b2_o[...] = jnp.where(core == 0, red[n + 3 : n + 4, :per_c], red[n + 4 : n + 5, :per_c])
+    parts = narrow.shape[1]
+    jobs = []
+    for n, (src, dst) in enumerate(((bo_hbm, bo_out), (gi_hbm, gi_out))):
+        for m in range(parts):
+            size = narrow.shape[2]
+            rows = pl.ds(m * size, size)
+            jobs.append(
+                (
+                    (n, m),
+                    pltpu.make_async_copy(src.at[rows], narrow.at[n, m], in_sem.at[n, m]),
+                    pltpu.make_async_copy(broad.at[n, m], dst.at[rows], out_sem.at[n, m]),
+                )
+            )
+    for _, load, _ in jobs:
+        load.start()
+    for at, load, store in jobs:
+        load.wait()
+        broad[at] = narrow[at].astype(F32)
+        store.start()
+    images = pool_o.shape[0]
+    pool_o[...] = pool_ref[:images, :]
+    sq_o[...] = sq_ref[0:1, :images]
+    red = red_ref[...]
+    n = 2 * unit_d
+    tw1_o[...] = red[:unit_d, :pat]
+    tw2_o[...] = red[unit_d:n, :pat]
+    gain_o[...] = red[n + 8 : n + 10, :n]
+    shift_o[...] = red[n + 10 : n + 12, :n]
+    tb1_o[...] = jnp.transpose(red[: up(unit_d, 8), 128:])[pat - 128 : pat - 127, :unit_d]
+    tb2_o[...] = red[n : n + 1, :pat]
+    w1_o[...] = gw_ref[0]
+    w2_o[...] = gw_ref[1]
+    b1_o[...] = jnp.where(core == 0, red[n + 1 : n + 2, :per_h], red[n + 2 : n + 3, :per_h])
+    b2_o[...] = jnp.where(core == 0, red[n + 3 : n + 4, :per_c], red[n + 4 : n + 5, :per_c])
+    for _, _, store in jobs:
+        store.wait()
 
 
 def finish(bo, gi, pool, sq, red, gw, unit_d, per_h, per_c):
     images, pat, ch = bo.shape
     ds = unit_d
     sds = jax.ShapeDtypeStruct
-    once = lambda s: pl.BlockSpec(s, lambda i: (0,) * len(s))
-    steps = 4 if images % 4 == 0 else images
-    per = pl.BlockSpec((images // steps, pat, ch), lambda i: (i, 0, 0))
     rows_own, half = gw.shape[1:]
+    parts = 6 if images % 6 == 0 else 1
     outs = [
         (images, pat, ch),
         (images, ch),
@@ -1011,10 +1076,15 @@
     ]
     res = pl.pallas_call(
         functools.partial(finish_kernel, (pat, unit_d, per_h, per_c)),
-        grid=(steps,),
         out_shape=[sds(s, F32) for s in outs],
-        in_specs=[per, per] + [once(a.shape) for a in (pool, sq, red, gw)],
-        out_specs=[per if len(s) == 3 else once(s) for s in outs],
+        in_specs=[ANY, ANY, VM, VM, VM, VM],
+        out_specs=[ANY if len(s) == 3 else VM for s in outs],
+        scratch_shapes=[
+            pltpu.VMEM((2, parts, images // parts, pat, ch), BF16),
+            pltpu.VMEM((2, parts, images // parts, pat, ch), F32),
+            pltpu.SemaphoreType.DMA((2, parts)),
+            pltpu.SemaphoreType.DMA((2, parts)),
+        ],
         compiler_params=pltpu.CompilerParams(vmem_limit_bytes=VMEM_BYTES),
         name="finish",
     )(bo, gi, pool, sq, red, gw)
@@ -1047,6 +1117,9 @@
     images, ch, pat = mixer_input.shape
     unit_d = token_b1.shape[0]
     half = chan_b1.shape[0]
+    biases = [chan_b1, chan_b2, token_b2]
+    biases = [jnp.pad(b, (0, up(b.shape[0], 128) - b.shape[0])) for b in biases]
+    biases = jnp.concatenate(biases).reshape(1, -1)
     bo, gi, pool, sq, red, gw = mixer(
         n_dp,
         grid3,
@@ -1055,14 +1128,12 @@
         grad_pooled,
         chan_w1,
         chan_w2,
-        chan_b1.reshape(1, -1),
-        chan_b2.reshape(1, -1),
+        biases,
         ln_gain,
         ln_shift,
         token_w1.T,
         token_b1.reshape(1, -1),
         token_w2,
-        token_b2.reshape(1, -1),
         keep_mask,
     )
     return finish(bo, gi, pool, sq, red, gw, unit_d, half // n_dp, ch // n_dp)

time: 113 us -> 107 us (0.947)
  local copies, waits for them, and re-layouts: 3.75 us -> 0.61 us
  Pallas kernels: 108 us -> 105 us
    reshape x3 -> x1, local copies, waits for them, and re-layouts: 3.75 us -> 0.61 us  [fused_body(): biases = jnp.concatenate(biases).reshape(1, -1)]
    pallas_call x1, Pallas kernels: 101 us -> 98.6 us  [mixer(): pl.pallas_call(functools.partial(mixer_kernel, (n_dp, ni, ch, pat, tp, un...]
where the time goes in v4:
time: 107 us
  Pallas kernels  105 us (98%)
    pallas_call x1, Pallas kernels, mixer(): pl.pallas_call(functools.partial(mixer_kernel, (n_dp, ni, ch, pat, tp, un...  98.6 us
    pallas_call x1, Pallas kernels, finish(): pl.pallas_call(functools.partial(finish_kernel, (pat, unit_d, per_h, per_...  6.17 us

profile of v4, /device:TPU:0, one launch (start us, length us, event | category | flops | bytes accessed | tf_op | source)
XLA Modules:
  0.0 106.9 jit_solution(4090353394496162314)
XLA Ops:
  0.6 0.7 fusion.1
  1.4 0.6 reshape.49.row_ref
  2.0 98.6 %mixer.1 = (bf16[12,196,384]{2,1,0:T(8,128)(2,1)}, bf16[12,196,384]{2,1,0:T(8,128)(2,1)}, bf16[6,208,768]{2,1,0:T(8,128)(2,1)}, bf16[6,256,768]{2,1,0:T(8,128)(2...) custom-call(bf16[12,196,384]{2,1,0:T(8,128)(2,1)} %bitcast.13, ...), custom_call_target="tpu_custom_call" | custom-call | tf_op jit(solution)/shard_map/mixer/pallas_call | solution.py:894
  100.5 6.2 %finish.1 = (f32[12,196,384]{2,1,0:T(8,128)}, f32[12,384]{1,0:T(8,128)}, f32[12,196,384]{2,1,0:T(8,128)}, f32[2,48]{1,0:T(2,128)}, f32[2,48]{1,0:T(2,128)}, /*in...) custom-call(bf16[12,196,384]{2,1,0:T(8,128)(2,1)} %get-tuple-element, ...), custom_call_target="tpu_custom_call" | custom-call | tf_op jit(solution)/shard_map/finish/pallas_call | solution.py:1077

commit v5 on v4

--- a/solution.py
+++ b/solution.py
@@ -107,12 +107,14 @@
     gp_ref,
     w1_hbm,
     w2_hbm,
-    row_ref,
+    b1_ref,
+    cb2_ref,
     gain_ref,
     shift_ref,
     tw1_ref,
     tb1_ref,
     tw2_ref,
+    tb2_ref,
     keep_ref,
     bo_hbm,
     gi_hbm,
@@ -278,9 +280,10 @@
     msg[:, 128:] = (tmp_w[0, :rows_own, 128:] + columns).astype(BF16)
     pack[...] = jnp.zeros_like(pack)
     pack[:images, :] = gp_ref[...]
-    pack[images : images + 1, :] = row_ref[:, half : half + ch].astype(F32)
+    pack[images : images + 1, :] = cb2_ref[...].astype(F32).reshape(1, ch)
+    b1_row = b1_ref[...].astype(F32).reshape(1, half)
     for n in range(bias_rows):
-        pack[images + 1 + n : images + 2 + n, :] = row_ref[:, n * ch : (n + 1) * ch].astype(F32)
+        pack[images + 1 + n : images + 2 + n, :] = b1_row[:, n * ch : (n + 1) * ch]
     greet_all(n_dp, dp, core)
 
     def send(n, c):
@@ -295,7 +298,7 @@
     packf[:, here] = pack[...]
     keep_t[...] = jnp.zeros_like(keep_t)
     keep_t[:images, :pat] = keep_ref[...].astype(F32)
-    keep_t[images : images + 1, :pat] = row_ref[:, half + ch : half + ch + pat].astype(F32)
+    keep_t[images : images + 1, :pat] = tb2_ref[...].astype(F32).reshape(1, pat)
     turned = jnp.transpose(keep_t[...])
     keep_t[...] = turned
     tb2_w[...] = jnp.broadcast_to(turned[:tp, images : images + 1], (tp, 128))
@@ -612,9 +615,10 @@
     def backward_step(i, carry):
         slot = lax.rem(i, 2)
         due(
-            (finish_third, n_blk - 3, i == 4),
-            (finish_second, n_blk - 2, i == 4),
-            (finish_first, n_blk - 1, i == 2),
+            (finish_third, n_blk - 3, i == 5),
+            (finish_second, n_blk - 3, i == 0),
+            (finish_second, n_blk - 2, i == 5),
+            (finish_first, n_blk - 1, i == 3),
         )
 
         @pl.when(i + 1 < ni)
@@ -650,14 +654,13 @@
         row_c[pl.ds(1 + i, 1), :] = dy
         acc_norm[1] += gain
         acc_norm[3] += shift
-        for c in lane_pieces(full):
-            hg = nn(tw[1], ol[:, c])
-            for a in range(0, ds, 32):
-                r = slice(a, a + 32)
-                tg[r, c] = (hg[r] * ls[slot, r, c].astype(F32)).astype(BF16)
-            fg[:, c] = nn(twt[0], tg[:, c])
+        hg = nn(tw[1], ol[...])
+        acc_tok[1] += nt(hs[slot], ol[...])
+        for a in range(0, ds, 16):
+            r = slice(a, a + 16)
+            tg[r, :] = (hg[r] * ls[slot, r, :].astype(F32)).astype(BF16)
         acc_tok[0, :ds] += nt(tg[...], fs[slot])
-        acc_tok[1] += nt(hs[slot], ol[...])
+        fg[...] = nn(twt[0], tg[...])
         gain, shift = zero8, zero8
         for r in pieces:
             g = fg[r, :]
@@ -676,13 +679,11 @@
 
     part = toks // 3
     for n in range(3):
-        if n == 0:
+        if n == 1:
             finish_third(n_blk - 5)
-        if n == 1:
+        if n == 2:
             finish_third(n_blk - 4)
             finish_first(n_blk - 2)
-        if n == 2:
-            finish_second(n_blk - 3)
         a = n * part
         sg[a : a + part, :] = nt(ph[a : a + part, :], w1s[...]).astype(BF16)
     lax.fori_loop(0, ni, backward_step, 0)
@@ -857,7 +858,7 @@
     red_o[...] = red_a[...] + red_r[...]
 
 
-def mixer(n_dp, grid3, x, go, gp, w1, w2, row, gain, shift, tw1, tb1, tw2, keep):
+def mixer(n_dp, grid3, x, go, gp, w1, w2, b1, cb2, gain, shift, tw1, tb1, tw2, tb2, keep):
     images, pat, ch = x.shape
     ni = images // 2
     full = 2 * ch
@@ -894,7 +895,7 @@
     res = pl.pallas_call(
         functools.partial(mixer_kernel, (n_dp, ni, ch, pat, tp, unit_d, nz, ny, nx)),
         out_shape=[o[0] for o in outs],
-        in_specs=[ANY, ANY, VM, ANY, ANY] + [VM] * 7,
+        in_specs=[ANY, ANY, VM, ANY, ANY] + [VM] * 9,
         out_specs=[o[1] for o in outs],
         scratch_shapes=[
             vm((ni, pat, full), BF16),
@@ -981,7 +982,7 @@
             collective_id=0, has_side_effects=True, vmem_limit_bytes=VMEM_BYTES
         ),
         name="mixer",
-    )(x, go, gp, w1, w2, row, gain, shift, tw1, tb1, tw2, keep)
+    )(x, go, gp, w1, w2, b1, cb2, gain, shift, tw1, tb1, tw2, tb2, keep)
     return res[:2] + res[8:]
 
 
@@ -992,7 +993,7 @@
     pool_ref,
     sq_ref,
     red_ref,
-    gw_ref,
+    gw_hbm,
     bo_out,
     pool_o,
     gi_out,
@@ -1002,15 +1003,17 @@
     tb1_o,
     tw2_o,
     tb2_o,
-    w1_o,
+    w1_out,
     b1_o,
-    w2_o,
+    w2_out,
     b2_o,
     sq_o,
     narrow,
     broad,
+    gw,
     in_sem,
     out_sem,
+    gw_sem,
 ):
     pat, unit_d, per_h, per_c = dims
     _, core = where_am_i()
@@ -1027,11 +1030,20 @@
                     pltpu.make_async_copy(broad.at[n, m], dst.at[rows], out_sem.at[n, m]),
                 )
             )
+    load_w = pltpu.make_async_copy(gw_hbm, gw, gw_sem.at[0])
+    store_w = [
+        pltpu.make_async_copy(gw.at[n], dst, gw_sem.at[1 + n])
+        for n, dst in enumerate((w1_out, w2_out))
+    ]
     for _, load, _ in jobs:
         load.start()
+    load_w.start()
     for at, load, store in jobs:
         load.wait()
         broad[at] = narrow[at].astype(F32)
+        store.start()
+    load_w.wait()
+    for store in store_w:
         store.start()
     images = pool_o.shape[0]
     pool_o[...] = pool_ref[:images, :]
@@ -1044,11 +1056,11 @@
     shift_o[...] = red[n + 10 : n + 12, :n]
     tb1_o[...] = jnp.transpose(red[: up(unit_d, 8), 128:])[pat - 128 : pat - 127, :unit_d]
     tb2_o[...] = red[n : n + 1, :pat]
-    w1_o[...] = gw_ref[0]
-    w2_o[...] = gw_ref[1]
     b1_o[...] = jnp.where(core == 0, red[n + 1 : n + 2, :per_h], red[n + 2 : n + 3, :per_h])
     b2_o[...] = jnp.where(core == 0, red[n + 3 : n + 4, :per_c], red[n + 4 : n + 5, :per_c])
     for _, _, store in jobs:
+        store.wait()
+    for store in store_w:
         store.wait()
 
 
@@ -1077,13 +1089,15 @@
     res = pl.pallas_call(
         functools.partial(finish_kernel, (pat, unit_d, per_h, per_c)),
         out_shape=[sds(s, F32) for s in outs],
-        in_specs=[ANY, ANY, VM, VM, VM, VM],
-        out_specs=[ANY if len(s) == 3 else VM for s in outs],
+        in_specs=[ANY, ANY, VM, VM, VM, ANY],
+        out_specs=[ANY if n in (0, 2, 9, 11) else VM for n in range(len(outs))],
         scratch_shapes=[
             pltpu.VMEM((2, parts, images // parts, pat, ch), BF16),
             pltpu.VMEM((2, parts, images // parts, pat, ch), F32),
+            pltpu.VMEM(gw.shape, F32),
             pltpu.SemaphoreType.DMA((2, parts)),
             pltpu.SemaphoreType.DMA((2, parts)),
+            pltpu.SemaphoreType.DMA((3,)),
         ],
         compiler_params=pltpu.CompilerParams(vmem_limit_bytes=VMEM_BYTES),
         name="finish",
@@ -1117,9 +1131,6 @@
     images, ch, pat = mixer_input.shape
     unit_d = token_b1.shape[0]
     half = chan_b1.shape[0]
-    biases = [chan_b1, chan_b2, token_b2]
-    biases = [jnp.pad(b, (0, up(b.shape[0], 128) - b.shape[0])) for b in biases]
-    biases = jnp.concatenate(biases).reshape(1, -1)
     bo, gi, pool, sq, red, gw = mixer(
         n_dp,
         grid3,
@@ -1128,12 +1139,14 @@
         grad_pooled,
         chan_w1,
         chan_w2,
-        biases,
+        chan_b1,
+        chan_b2,
         ln_gain,
         ln_shift,
         token_w1.T,
         token_b1.reshape(1, -1),
         token_w2,
+        token_b2,
         keep_mask,
     )
     return finish(bo, gi, pool, sq, red, gw, unit_d, half // n_dp, ch // n_dp)

time: 107 us -> 103 us (0.963)
  Pallas kernels: 105 us -> 102 us
    pallas_call x1, Pallas kernels: 98.6 us -> 96.2 us  [mixer(): pl.pallas_call(functools.partial(mixer_kernel, (n_dp, ni, ch, pat, tp, un...]
where the time goes in v5:
time: 103 us
  Pallas kernels  102 us (99%)
    pallas_call x1, Pallas kernels, mixer(): pl.pallas_call(functools.partial(mixer_kernel, (n_dp, ni, ch, pat, tp, un...  96.2 us
    pallas_call x1, Pallas kernels, finish(): pl.pallas_call(functools.partial(finish_kernel, (pat, unit_d, per_h, per_...  5.9 us

profile of v5, /device:TPU:0, one launch (start us, length us, event | category | flops | bytes accessed | tf_op | source)
XLA Modules:
  0.0 102.9 jit_solution(798354242877973077)
XLA Ops:
  0.7 96.2 %mixer.1 = (bf16[12,196,384]{2,1,0:T(8,128)(2,1)}, bf16[12,196,384]{2,1,0:T(8,128)(2,1)}, bf16[6,208,768]{2,1,0:T(8,128)(2,1)}, bf16[6,256,768]{2,1,0:T(8,128)(2...) custom-call(bf16[12,196,384]{2,1,0:T(8,128)(2,1)} %bitcast.13, ...), custom_call_target="tpu_custom_call" | custom-call | tf_op jit(solution)/shard_map/mixer/pallas_call | solution.py:895
  96.9 5.9 %finish.1 = (f32[12,196,384]{2,1,0:T(8,128)}, f32[12,384]{1,0:T(8,128)}, f32[12,196,384]{2,1,0:T(8,128)}, f32[2,48]{1,0:T(2,128)}, f32[2,48]{1,0:T(2,128)}, /*in...) custom-call(bf16[12,196,384]{2,1,0:T(8,128)(2,1)} %get-tuple-element, ...), custom_call_target="tpu_custom_call" | custom-call | tf_op jit(solution)/shard_map/finish/pallas_call | solution.py:1089
